TPU v7x, 256 devices: a whole 4x4x8 slice. The times are simulated.
256 devices in a mesh: dp: 8 (over z_lo, x), fsdp: 16 (over y, z_hi), tensor: 2 (over core).
Axes of the slice: x: 4, y: 4, z: 8 (z_hi: 4, z_lo: 2; z = z_hi * 2 + z_lo), core: 2. Of those that a mesh axis runs over, the one named last changes fastest.
Arguments:
- fresh: bfloat16 [32768, 4608], P(('dp', 'fsdp'), 'tensor'), may hold values from -6 to 6
- replay_buffer: bfloat16 [65536, 4608], P(('dp', 'fsdp'), 'tensor'), may hold values from -6 to 6
- replay_index: int32 [32768], P(('dp', 'fsdp')), may hold values from 0 to 511
- from_replay: int32 [32768], P(('dp', 'fsdp')), may hold values 0 or 1
- cotangent: bfloat16 [32768, 2048], P(('dp', 'fsdp')), may hold values from -48 to 48
- master: float32 [2048, 4608], P(('dp', 'fsdp'), 'tensor'), may hold values from -0.09375 to 0.09375
- moment1: float32 [2048, 4608], P(('dp', 'fsdp'), 'tensor'), may hold values from -6 to 6
- moment2: float32 [2048, 4608], P(('dp', 'fsdp'), 'tensor'), may hold values from 0.25 to 4
- teacher: float32 [2048, 4608], P(('dp', 'fsdp'), 'tensor'), may hold values from -0.09375 to 0.09375
Outputs:
- new_master: float32 [2048, 4608], P(('dp', 'fsdp'), 'tensor')
- new_moment1: float32 [2048, 4608], P(('dp', 'fsdp'), 'tensor')
- new_moment2: float32 [2048, 4608], P(('dp', 'fsdp'), 'tensor')
- new_teacher: float32 [2048, 4608], P(('dp', 'fsdp'), 'tensor')
- teacher_out: float32 [32768, 2048], P(('dp', 'fsdp'), 'tensor')
Inputs may be any that keep to these rules, and one draw needn't show every extreme that they name: `replay_index`: each row names a slot of its own device's block of 512 rows of replay_buffer.
All inputs are finite; a program needn't handle non-finite values. No bound on the sum of `from_replay` on one device may be relied on, other than what follows from the above.
Results may differ from a plain program's by a relative error of at most 0.004.
Values may be sent and summed in bfloat16 or wider, within the bound.
No kernel may reach another device: no remote copies, remote signals or barrier semaphores. Data moves between devices by JAX's collectives and lax.ppermute only.
A program may use at most 128 MiB of HBM per device.

v0:
```python
import math

import jax
import jax.numpy as jnp
from jax import lax
from jax.sharding import PartitionSpec as P

beta_one = 0.9
beta_two = 0.999
learn_rate = 0.001
adam_eps = 1e-08
ema_decay = 0.99
corr_one = 1.0 - math.exp(100.0 * math.log(0.9))
corr_two = 1.0 - math.exp(100.0 * math.log(0.999))


def body(
    fresh, replay_buffer, replay_index, from_replay, cotangent, master, moment1, moment2, teacher
):
    picked = jnp.take(replay_buffer, replay_index, axis=0)
    flag = (from_replay == 1)[:, None]
    student_rows = jnp.where(flag, picked, fresh)
    total_rows = fresh.shape[0] * lax.axis_size(("dp", "fsdp"))
    grad = lax.psum_scatter(
        lax.dot_general(
            cotangent, student_rows, (((0,), (0,)), ((), ())), preferred_element_type=jnp.float32
        ),
        ("dp", "fsdp"),
        scatter_dimension=0,
        tiled=True,
    )
    grad = grad * (1.0 / math.sqrt(total_rows))
    new_moment1 = beta_one * moment1 + (1.0 - beta_one) * grad
    new_moment2 = beta_two * moment2 + (1.0 - beta_two) * grad * grad
    new_master = master - learn_rate * (new_moment1 / corr_one) / (
        jnp.sqrt(new_moment2 / corr_two) + adam_eps
    )
    new_teacher = ema_decay * teacher + (1.0 - ema_decay) * new_master
    gap_low = (new_master - new_teacher).astype(jnp.bfloat16)
    partial_out = lax.dot_general(
        picked,
        lax.all_gather(gap_low, ("dp", "fsdp"), axis=0, tiled=True),
        (((1,), (1,)), ((), ())),
        preferred_element_type=jnp.float32,
    )
    summed = lax.psum_scatter(partial_out, "tensor", scatter_dimension=1, tiled=True)
    teacher_out = summed * from_replay.astype(jnp.float32)[:, None]
    return (new_master, new_moment1, new_moment2, new_teacher, teacher_out)


def solution(mesh):
    return jax.shard_map(
        body,
        mesh=mesh,
        in_specs=(
            P(("dp", "fsdp"), "tensor"),
            P(("dp", "fsdp"), "tensor"),
            P(("dp", "fsdp")),
            P(("dp", "fsdp")),
            P(("dp", "fsdp"), None),
            P(("dp", "fsdp"), "tensor"),
            P(("dp", "fsdp"), "tensor"),
            P(("dp", "fsdp"), "tensor"),
            P(("dp", "fsdp"), "tensor"),
        ),
        out_specs=(
            P(("dp", "fsdp"), "tensor"),
            P(("dp", "fsdp"), "tensor"),
            P(("dp", "fsdp"), "tensor"),
            P(("dp", "fsdp"), "tensor"),
            P(("dp", "fsdp"), "tensor"),
        ),
        check_vma=False,
    )
```

profile of v0, /device:TPU:1, one launch (start us, length us, event | category | flops | bytes accessed | tf_op | source)
XLA Modules:
  0.0 1703.9 jit_solution(16333211543281845974)
XLA Ops:
  7.2 0.0 copy-start
  7.2 0.0 reduce-scatter.7.cloned.1.call-start
  7.2 0.8 compare_select_fusion
  8.1 0.7 compare_and_fusion
  8.8 0.1 copy-done
  8.9 1.4 gather_fusion
  10.3 10.8 convolution_bitcast_fusion
  21.1 18.7 %copy.40 = f32[2048,2304]{1,0:T(8,128)} copy(f32[2048,2304]{0,1:T(8,128)} %convolution_bitcast_fusion) | data formatting | bytes 37748736
  39.8 0.0 reduce-scatter.7.cloned.1.call-update
  39.8 0.0 all-gather.2.cloned.1.call-start
  39.9 686.8 %reduce-scatter.7.cloned.1.call-done = f32[16,2304]{1,0:T(8,128)} async-done(((f32[2048,2304]{1,0:T(8,128)}), f32[16,2304]{1,0:T(8,128)}) %reduce-scatter.7.cloned.1.call-update) | async-done | bytes 147472 | tf_op jit(solution)/shard_map/reduce_scatter | solution.py:24
  726.7 2.1 subtract_convert_fusion
  728.8 0.0 all-gather.2.cloned.1.call-update
  728.8 0.0 reduce-scatter.5.cloned.1.call-start
  728.8 760.9 %all-gather.2.cloned.1.call-done = bf16[2048,2304]{1,0:T(8,128)(2,1)} async-done(((bf16[16,2304]{1,0:T(8,128)(2,1)}), bf16[2048,2304]{1,0:T(8,128)(2,1)}) %all-gather.2.cloned.1.call-update) | async-done | bytes 9437200 | tf_op jit(solution)/shard_map/all_gather | solution.py:42
  1489.8 7.7 fusion.2
  1497.5 0.0 copy-start.1
  1497.5 0.0 reduce-scatter.5.cloned.1.call-update
  1497.5 0.7 copy-done.1
  1498.2 196.9 %reduce-scatter.5.cloned.1.call-done = f32[256,1024]{1,0:T(8,128)} async-done(((f32[256,2048]{1,0:T(8,128)}), f32[256,1024]{1,0:T(8,128)}) %reduce-scatter.5.cloned.1.call-update) | async-done | bytes 1048592 | tf_op jit(solution)/shard_map/reduce_scatter | solution.py:46
  1695.0 2.3 broadcast_multiply_fusion
  (2 shorter events, 0.0 us)
Async XLA Ops:
  7.2 1.7 copy-start
  7.2 719.5 %reduce-scatter.7.cloned.1.call-start = ((), (), s32[]{:S(2)}) async-start(), calls=%async_computation.4 | async-start | bytes 19021824 | tf_op jit(solution)/shard_map/reduce_scatter | solution.py:24
  39.8 1450.0 %all-gather.2.cloned.1.call-start = ((), (), s32[]{:S(2)}) async-start(), calls=%async_computation.2 | async-start | bytes 9510912 | tf_op jit(solution)/shard_map/all_gather | solution.py:42
  728.8 966.3 %reduce-scatter.5.cloned.1.call-start = ((), (), s32[]{:S(2)}) async-start(), calls=%async_computation.3 | async-start | bytes 3145728 | tf_op jit(solution)/shard_map/reduce_scatter | solution.py:46
  1497.5 0.7 copy-start.1
Sparse Core Ops, SparseCore 0:
  39.9 686.6 reduce-scatter.6
  729.0 760.7 all-gather.1
  1497.6 197.3 reduce-scatter.4
where the time goes:
time: 1700 us
  waiting for transfers between devices  1640 us (96%)
  local copies, waits for them, and re-layouts  20.8 us (1%)
  matrix products  18.5 us (1%)
    all_gather x1, waiting for transfers between devices, body(): lax.all_gather(gap_low, ('dp', 'fsdp'), axis=0, tiled=True)  761 us
    reduce_scatter x1, waiting for transfers between devices, body(): lax.psum_scatter(lax.dot_general(cotangent, student_rows, (((0,), (0,)),...  687 us
    reduce_scatter x1, waiting for transfers between devices, body(): lax.psum_scatter(partial_out, 'tensor', scatter_dimension=1, tiled=True)  197 us
  transfers between devices with their start and end apart: 3, of which 3 were waited for; matrix products, arithmetic and copies ran while one was open for 0% of the time, Pallas kernels for 0%

commit v1 on v0

v1 whole, which is shorter than its diff:
```python
import functools
import itertools
import math

import jax
import jax.numpy as jnp
from jax import lax
from jax.experimental import pallas as pl
from jax.experimental.pallas import tpu as pltpu
from jax.sharding import Mesh, PartitionSpec as P

beta_one = 0.9
beta_two = 0.999
learn_rate = 0.001
adam_eps = 1e-08
ema_decay = 0.99
corr_one = 1.0 - math.exp(100.0 * math.log(0.9))
corr_two = 1.0 - math.exp(100.0 * math.log(0.999))

bf16, f32 = jnp.bfloat16, jnp.float32
AXES = ("zl", "x", "y", "zh", "c")
SIZES = (2, 4, 4, 4, 2)
ROWS = tuple(AXES[:4])
VMEM_LIMIT = 48 * 1024 * 1024


def flat(zl, x, y, zh, c):
    return (((zl * 4 + x) * 4 + y) * 4 + zh) * 2 + c


def pairs(move):
    return [
        (flat(*place), flat(*move(*place)))
        for place in itertools.product(*map(range, SIZES))
    ]


def first_ring(s):
    return pairs(
        lambda zl, x, y, zh, c: (zl, (x + s) % 4, y, zh, c)
        if c == 0
        else (zl, x, (y + s) % 4, zh, c)
    )


def second_ring(s):
    return pairs(
        lambda zl, x, y, zh, c: (zl, x, (y + s) % 4, zh, c)
        if c == 0
        else (zl, (x + s) % 4, y, zh, c)
    )


other_core = pairs(lambda zl, x, y, zh, c: (zl, x, y, zh, 1 - c))


def send(array, perm):
    return lax.ppermute(array, AXES, perm)


def dot(lhs, rhs, left, right):
    return lax.dot_general(
        lhs, rhs, (((left,), (right,)), ((), ())), preferred_element_type=f32
    )


def params():
    return pltpu.CompilerParams(vmem_limit_bytes=VMEM_LIMIT)


def rows_kernel(index_ref, flag_ref, buffer_ref, fresh_ref, a_ref, b_ref):
    slots, rows = buffer_ref.shape[0], fresh_ref.shape[0]
    replayed = flag_ref[...] == 1
    slot = lax.broadcasted_iota(jnp.int32, (slots, rows), 0)
    pick = jnp.where((slot == index_ref[...]) & replayed, 1.0, 0.0).astype(bf16)
    same = lax.broadcasted_iota(jnp.int32, (rows, rows), 0) == lax.broadcasted_iota(
        jnp.int32, (rows, rows), 1
    )
    keep = jnp.where(same & jnp.logical_not(replayed), 1.0, 0.0).astype(bf16)
    got = dot(pick, buffer_ref[...], 0, 0) + dot(keep, fresh_ref[...], 0, 0)
    got = got.astype(bf16)
    a_ref[...] = got[: rows // 2]
    b_ref[...] = got[rows // 2 :]


def student_rows(index, flag, buffer, fresh):
    rows, width = fresh.shape
    block = width // 3
    half = jax.ShapeDtypeStruct((rows // 2, width), bf16)
    whole = lambda j: (0, 0)
    return pl.pallas_call(
        rows_kernel,
        grid=(3,),
        in_specs=[
            pl.BlockSpec((1, rows), whole),
            pl.BlockSpec((1, rows), whole),
            pl.BlockSpec((buffer.shape[0], block), lambda j: (0, j)),
            pl.BlockSpec((rows, block), lambda j: (0, j)),
        ],
        out_specs=[pl.BlockSpec((rows // 2, block), lambda j: (0, j))] * 2,
        out_shape=[half, half],
        compiler_params=params(),
        name="student_rows",
    )(index.reshape(1, rows), flag.reshape(1, rows), buffer, fresh)


def turn_kernel(place_ref, cot_ref, *refs):
    outs, turned = refs[:4], refs[4]
    c, p, q = place_ref[0], place_ref[1], place_ref[2]
    turned[...] = cot_ref[...].T
    for k in range(4):
        pk = (p + k) % 4
        for d in range(4):
            qd = (q + d) % 4
            x = jnp.where(c == 0, pk, qd)
            y = jnp.where(c == 0, qd, pk)
            for zl in range(2):
                start = pl.multiple_of(zl * 1024 + x * 256 + y * 64, 64)
                outs[k][pl.ds(d * 128 + zl * 64, 64), :] = turned[pl.ds(start, 64), :]


def turned_parts(place, cot):
    rows, width = cot.shape
    vmem = pl.BlockSpec(memory_space=pltpu.VMEM)
    return pl.pallas_call(
        turn_kernel,
        in_specs=[pl.BlockSpec(memory_space=pltpu.SMEM), vmem],
        out_specs=[vmem] * 4,
        out_shape=[jax.ShapeDtypeStruct((width // 4, rows), bf16)] * 4,
        scratch_shapes=[pltpu.VMEM((width, rows), bf16)],
        compiler_params=params(),
        name="turned_parts",
    )(place, cot)


def grad_kernel(*refs):
    cots, halves, outs = refs[:4], refs[4:12], refs[12:]
    total = None
    for k in range(4):
        rows = jnp.concatenate([halves[2 * k][...], halves[2 * k + 1][...]], axis=0)
        part = dot(cots[k][...], rows, 1, 0)
        total = part if total is None else total + part
    outs[0][...] = total[:128]
    for n in range(6):
        outs[n + 1][...] = total[128 + 64 * n : 192 + 64 * n].astype(bf16)


def grad_parts(cots, halves):
    rows, width = halves[0].shape
    block = width // 3
    out_shape = [jax.ShapeDtypeStruct((128, width), f32)]
    out_shape += [jax.ShapeDtypeStruct((64, width), bf16)] * 6
    return pl.pallas_call(
        grad_kernel,
        grid=(3,),
        in_specs=[pl.BlockSpec(cots[0].shape, lambda j: (0, 0))] * 4
        + [pl.BlockSpec((rows, block), lambda j: (0, j))] * 8,
        out_specs=[pl.BlockSpec((s.shape[0], block), lambda j: (0, j)) for s in out_shape],
        out_shape=out_shape,
        compiler_params=params(),
        name="grad_parts",
    )(*cots, *halves)


def values_kernel(place_ref, *refs):
    halves, gaps = refs[:8], refs[8:16]
    mine_ref, over_ref, outs = refs[16], refs[17], refs[18:21]
    gap, total = refs[21], refs[22]
    step = pl.program_id(0)
    c, q = place_ref[0], place_ref[2]
    for d in range(4):
        for zl in range(2):
            part = jnp.where(c == zl, 0, 256)
            start = pl.multiple_of(part + (q + d) % 4 * 64, 64)
            gap[pl.ds(start, 64), :] = gaps[2 * d + zl][...]
    for k in range(4):
        rows = jnp.concatenate([halves[2 * k][...], halves[2 * k + 1][...]], axis=0)
        part = dot(rows, gap[...], 1, 1)

        @pl.when(step == 0)
        def _():
            total[k] = part

        @pl.when(step > 0)
        def _():
            total[k] = total[k] + part

    @pl.when(step == pl.num_programs(0) - 1)
    def _():
        mine_ref[...] = total[0][:, :256]
        over_ref[...] = total[0][:, 256:].astype(bf16)
        for k in range(3):
            outs[k][...] = total[k + 1].astype(bf16)


def value_parts(place, halves, gaps):
    width = halves[0].shape[1]
    block = width // 3
    whole = lambda j: (0, 0)
    out_shape = [
        jax.ShapeDtypeStruct((256, 256), f32),
        jax.ShapeDtypeStruct((256, 256), bf16),
    ] + [jax.ShapeDtypeStruct((256, 512), bf16)] * 3
    return pl.pallas_call(
        values_kernel,
        grid=(3,),
        in_specs=[pl.BlockSpec(memory_space=pltpu.SMEM)]
        + [pl.BlockSpec((128, block), lambda j: (0, j))] * 8
        + [pl.BlockSpec((64, block), lambda j: (0, j))] * 8,
        out_specs=[pl.BlockSpec(s.shape, whole) for s in out_shape],
        out_shape=out_shape,
        scratch_shapes=[pltpu.VMEM((512, block), bf16), pltpu.VMEM((4, 256, 512), f32)],
        compiler_params=params(),
        name="value_parts",
    )(place, *halves, *gaps)


def join_kernel(place_ref, flag_ref, *refs):
    mine, over, out_ref, held = refs[:4], refs[4], refs[5], refs[6]
    c, p, q = place_ref[0], place_ref[1], place_ref[2]
    for d in range(4):
        held[c, (p + d) % 4] = mine[d][:, :256].astype(f32)
        held[1 - c, (q + d) % 4] = over[d].astype(f32)
    flag = flag_ref[...].astype(f32)
    for x in range(4):
        for j in range(2):
            near = held[0, x, :, j * 128 : (j + 1) * 128]
            far = jnp.concatenate(
                [
                    held[1, 2 * j, :, x * 64 : (x + 1) * 64],
                    held[1, 2 * j + 1, :, x * 64 : (x + 1) * 64],
                ],
                axis=1,
            )
            out_ref[:, x * 256 + j * 128 : x * 256 + (j + 1) * 128] = (near + far) * flag


def joined(place, flag, mine, over):
    vmem = pl.BlockSpec(memory_space=pltpu.VMEM)
    return pl.pallas_call(
        join_kernel,
        in_specs=[pl.BlockSpec(memory_space=pltpu.SMEM)] + [vmem] * 6,
        out_specs=vmem,
        out_shape=jax.ShapeDtypeStruct((256, 1024), f32),
        scratch_shapes=[pltpu.VMEM((2, 4, 256, 256), f32)],
        compiler_params=params(),
        name="joined",
    )(place, flag.reshape(256, 1), *mine, over)


def body(
    fresh, replay_buffer, replay_index, from_replay, cotangent, master, moment1, moment2, teacher
):
    c, x, y = (lax.axis_index(a) for a in ("c", "x", "y"))
    p = jnp.where(c == 0, x, y)
    q = jnp.where(c == 0, y, x)
    place = jnp.stack([c, p, q]).astype(jnp.int32)
    total_rows = fresh.shape[0] * lax.axis_size(ROWS)

    a, b = student_rows(replay_index, from_replay, replay_buffer, fresh)
    up, down = first_ring(1), first_ring(-1)
    left_a = send(a, up)
    right_b = send(b, down)
    left_b = send(b, up)
    right_a = send(a, down)
    cots = turned_parts(place, cotangent)
    far_a = send(left_a, up)
    far_b = send(right_b, down)
    cot_left = send(cots[1], up)
    cot_far = send(cots[2], first_ring(2))
    cot_right = send(cots[3], down)
    halves = (a, b, right_a, right_b, left_a, left_b, far_a, far_b)
    own, a1, b1, a2, b2, am, bm = grad_parts((cots[0], cot_right, cot_left, cot_far), halves)

    up2, down2 = second_ring(1), second_ring(-1)
    pass_a = send(a2, up2)
    pass_b = send(b2, down2)
    got_b = send(b1, up2)
    got_a = send(am, down2)
    sum_a = send((a1.astype(f32) + pass_a.astype(f32)).astype(bf16), up2)
    sum_b = send((bm.astype(f32) + pass_b.astype(f32)).astype(bf16), down2)
    ring_sum = jnp.concatenate(
        [
            own[:64] + sum_a.astype(f32) + got_a.astype(f32),
            own[64:] + sum_b.astype(f32) + got_b.astype(f32),
        ],
        axis=0,
    ).astype(bf16)

    width = own.shape[1]
    slices = lax.all_to_all(ring_sum.reshape(8, 16, width), ("zl", "zh"), 0, 0, tiled=True)
    grad = jnp.sum(slices.astype(f32), axis=0)
    grad = grad * (1.0 / math.sqrt(total_rows))
    new_moment1 = beta_one * moment1 + (1.0 - beta_one) * grad
    new_moment2 = beta_two * moment2 + (1.0 - beta_two) * grad * grad
    new_master = master - learn_rate * (new_moment1 / corr_one) / (
        jnp.sqrt(new_moment2 / corr_two) + adam_eps
    )
    new_teacher = ema_decay * teacher + (1.0 - ema_decay) * new_master
    gap_low = (new_master - new_teacher).astype(bf16)

    copies = jnp.broadcast_to(gap_low[None], (8, 16, width))
    column = lax.all_to_all(copies, ("zl", "zh"), 0, 0, tiled=True)
    ga = column[:4].reshape(64, width)
    gb = column[4:].reshape(64, width)
    left_ga = send(ga, up2)
    right_gb = send(gb, down2)
    left_gb = send(gb, up2)
    right_ga = send(ga, down2)
    far_ga = send(left_ga, up2)
    far_gb = send(right_gb, down2)
    gaps = (ga, gb, right_ga, right_gb, far_ga, far_gb, left_ga, left_gb)
    mine, over, out_right, out_left, out_far = value_parts(place, halves, gaps)

    from_far = send(out_far, first_ring(2))
    from_left = send(out_right, up)
    from_right = send(out_left, down)
    crossing = jnp.stack([over, from_right[:, 256:], from_far[:, 256:], from_left[:, 256:]])
    crossed = send(crossing, other_core)
    teacher_out = joined(
        place, from_replay, (mine, from_right, from_far, from_left), crossed
    )
    return (new_master, new_moment1, new_moment2, new_teacher, teacher_out)


def solution(mesh):
    fine = Mesh(mesh.devices.reshape(SIZES), AXES)
    split = P(ROWS, "c")
    return jax.shard_map(
        body,
        mesh=fine,
        in_specs=(split, split, P(ROWS), P(ROWS), P(ROWS, None), split, split, split, split),
        out_specs=(split, split, split, split, split),
        check_vma=False,
    )
```

time: 1700 us -> 148 us (0.09)
  waiting for transfers between devices: 1640 us -> 41 us
  starting transfers between devices: 0.12 us -> 46.2 us
  blocking collectives: 0 us -> 35.8 us
  matrix products: 18.5 us -> 0 us
  Pallas kernels: 0 us -> 17.1 us
    reduce_scatter x2 -> x0, waiting for transfers between devices: 884 us -> none  [the longest x1 687 us: body(): lax.psum_scatter(lax.dot_general(cotangent, student_rows, (((0,), (0,)),...]
    all_gather x1 -> x0, waiting for transfers between devices: 761 us -> none  [body(): lax.all_gather(gap_low, ('dp', 'fsdp'), axis=0, tiled=True)]
    ppermute x0 -> x25, starting transfers between devices: none -> 46.2 us  [send(): return lax.ppermute(array, AXES, perm)]
    ppermute x0 -> x25, waiting for transfers between devices: none -> 41 us  [send(): return lax.ppermute(array, AXES, perm)]
    all_to_all x0 -> x2, blocking collectives: none -> 35.8 us  [the longest x1 20.6 us: body(): lax.all_to_all(ring_sum.reshape(8, 16, width), ('zl', 'zh'), 0, 0, tiled=...]
    dot_general x2 -> x0, matrix products: 18.5 us -> none  [the longest x1 10.8 us: body(): lax.dot_general(cotangent, student_rows, (((0,), (0,)), ((), ())), prefer...]
    pallas_call x0 -> x5, Pallas kernels: none -> 17.1 us  [the longest x1 7.11 us: value_parts(): pl.pallas_call(values_kernel, grid=(3,), in_specs=[pl.BlockSpec(memory_sp...]
  transfers between devices with their start and end apart: 3 -> 25, of which waited for: 3 -> 14; matrix products, arithmetic and copies ran while one was open for 0% -> 0% of each run, Pallas kernels for 0% -> 1%
where the time goes in v1:
time: 148 us
  starting transfers between devices  46.2 us (31%)
  waiting for transfers between devices  41 us (28%)
  blocking collectives  35.8 us (24%)
  Pallas kernels  17.1 us (12%)
  local copies, waits for them, and re-layouts  5.74 us (4%)
    ppermute x25, starting transfers between devices, send(): return lax.ppermute(array, AXES, perm)  46.2 us
    ppermute x25, waiting for transfers between devices, send(): return lax.ppermute(array, AXES, perm)  41 us
    all_to_all x1, blocking collectives, body(): lax.all_to_all(ring_sum.reshape(8, 16, width), ('zl', 'zh'), 0, 0, tiled=...  20.6 us
    all_to_all x1, blocking collectives, body(): column = lax.all_to_all(copies, ('zl', 'zh'), 0, 0, tiled=True)  15.2 us
    pallas_call x1, Pallas kernels, value_parts(): pl.pallas_call(values_kernel, grid=(3,), in_specs=[pl.BlockSpec(memory_sp...  7.11 us
    unnamed x30, local copies, waits for them, and re-layouts  5.5 us
    pallas_call x1, Pallas kernels, grad_parts(): pl.pallas_call(grad_kernel, grid=(3,), in_specs=[pl.BlockSpec(cots[0].sha...  5.13 us
  transfers between devices with their start and end apart: 25, of which 14 were waited for; matrix products, arithmetic and copies ran while one was open for 0% of the time, Pallas kernels for 1%

profile of v1, /device:TPU:1, one launch (start us, length us, event | category | flops | bytes accessed | tf_op | source)
XLA Modules:
  0.0 148.2 jit_solution(15388607062323216917)
XLA Ops:
  0.6 1.7 %copy-done.1 = bf16[512,2304]{1,0:T(8,128)(2,1)S(1)} copy-done((bf16[512,2304]{1,0:T(8,128)(2,1)S(1)}, bf16[512,2304]{1,0:T(8,128)(2,1)}, u32[]{:S(2)}) %copy-start.1) | copy-done | bytes 2359320
  2.3 1.3 copy-done.2
  3.6 0.7 copy-done.4
  4.3 0.7 copy-done.6
  4.9 1.9 %student_rows.1 = (bf16[128,2304]{1,0:T(8,128)(2,1)S(1)}, bf16[128,2304]{1,0:T(8,128)(2,1)S(1)}) custom-call(s32[1,256]{1,0:T(1,128)S(1)} %bitcast.25, s32[1,256]{1,0:T(1,128)S(1)} %bitcast.23, bf16[512,2304]{1,0:T(8,128)(2,1)S(1)} %copy-done.1, bf16[256,2304]{1,0:T(8,128)(2,1)S(1)} %copy-done.2), custom_call_target="tpu_custom_call" | custom-call | tf_op jit(solution)/shard_map/student_rows/pallas_call | solution.py:91
  6.8 2.2 %collective-permute-start.5 = (bf16[128,2304]{1,0:T(8,128)(2,1)S(1)}, bf16[128,2304]{1,0:T(8,128)(2,1)S(1)}, u32[]{:S(2)}, u32[]{:S(2)}) collective-permute-start(bf16[128,2304]{1,0:T(8,128)(2,1)S(1)} %get-tuple-element.27.refs_4_.refs_0_), channel_id=1, source_target_pairs={{0,32},{1,9},{2,34},{3,11},{4,36},{5,13},{6,38},{7,15},{8,40},{9,1... | collective-permute-start | bytes 1769480 | tf_op jit(solution)/shard_map/ppermute | solution.py:58
  9.0 1.5 %collective-permute-start.4 = (bf16[128,2304]{1,0:T(8,128)(2,1)S(1)}, bf16[128,2304]{1,0:T(8,128)(2,1)S(1)}, u32[]{:S(2)}, u32[]{:S(2)}) collective-permute-start(bf16[128,2304]{1,0:T(8,128)(2,1)S(1)} %get-tuple-element.28.refs_5_.refs_1_), channel_id=1, source_target_pairs={{0,96},{1,25},{2,98},{3,27},{4,100},{5,29},{6,102},{7,31},{8,104},... | collective-permute-start | bytes 1769480 | tf_op jit(solution)/shard_map/ppermute | solution.py:58
  10.5 0.1 pad_add_fusion.place_ref
  10.6 0.9 turned_parts.1
  11.6 1.5 collective-permute-start
  13.0 0.5 collective-permute-start.3
  13.5 1.0 collective-permute-start.6
  14.5 3.5 %collective-permute-done.5.refs_8_.refs_4_ = bf16[128,2304]{1,0:T(8,128)(2,1)S(1)} collective-permute-done((bf16[128,2304]{1,0:T(8,128)(2,1)S(1)}, bf16[128,2304]{1,0:T(8,128)(2,1)S(1)}, u32[]{:S(2)}, u32[]{:S(2)}) %collective-permute-start.5) | collective-permute-done | bytes 589856 | tf_op jit(solution)/shard_map/ppermute | solution.py:58
  18.0 0.0 collective-permute-start.7
  18.0 0.0 collective-permute-done.4.refs_7_.refs_3_
  18.0 2.7 %collective-permute-start.8 = (bf16[128,2304]{1,0:T(8,128)(2,1)S(1)}, bf16[128,2304]{1,0:T(8,128)(2,1)S(1)}, u32[]{:S(2)}, u32[]{:S(2)}) collective-permute-start(bf16[128,2304]{1,0:T(8,128)(2,1)S(1)} %collective-permute-done.4.refs_7_.refs_3_), channel_id=1, source_target_pairs={{0,96},{1,25},{2,98},{3,27},{4,100},{5,29},{6,102},{7,31},{8,104},... | collective-permute-start | bytes 1769480 | tf_op jit(solution)/shard_map/ppermute | solution.py:58
  20.8 0.1 collective-permute-done.refs_1_
  20.9 1.3 collective-permute-start.1
  22.2 11.3 %collective-permute-done.1.refs_2_ = bf16[512,256]{1,0:T(8,128)(2,1)S(1)} collective-permute-done((bf16[512,256]{1,0:T(8,128)(2,1)S(1)}, bf16[512,256]{1,0:T(8,128)(2,1)S(1)}, u32[]{:S(2)}, u32[]{:S(2)}) %collective-permute-start.1) | collective-permute-done | bytes 262176 | tf_op jit(solution)/shard_map/ppermute | solution.py:58
  33.5 1.6 %collective-permute-start.2 = (bf16[512,256]{1,0:T(8,128)(2,1)S(1)}, bf16[512,256]{1,0:T(8,128)(2,1)S(1)}, u32[]{:S(2)}, u32[]{:S(2)}) collective-permute-start(bf16[512,256]{1,0:T(8,128)(2,1)S(1)} %get-tuple-element.26), channel_id=1, source_target_pairs={{0,64},{1,17},{2,66},{3,19},{4,68},{5,21},{6,70},{7,23},{8,72},{9,... | collective-permute-start | bytes 786440 | tf_op jit(solution)/shard_map/ppermute | solution.py:58
  35.1 5.1 %collective-permute-done.2.refs_3_ = bf16[512,256]{1,0:T(8,128)(2,1)S(1)} collective-permute-done((bf16[512,256]{1,0:T(8,128)(2,1)S(1)}, bf16[512,256]{1,0:T(8,128)(2,1)S(1)}, u32[]{:S(2)}, u32[]{:S(2)}) %collective-permute-start.2) | collective-permute-done | bytes 262176 | tf_op jit(solution)/shard_map/ppermute | solution.py:58
  40.3 0.8 copy-done.7
  41.0 0.2 copy-done.8
  41.2 0.2 copy-done.9
  41.4 5.1 %grad_parts.1 = (f32[128,2304]{1,0:T(8,128)}, bf16[64,2304]{1,0:T(8,128)(2,1)S(1)}, bf16[64,2304]{1,0:T(8,128)(2,1)S(1)}, bf16[64,2304]{1,0:T(8,128)(2,1)S(1)}, ...) custom-call(bf16[512,256]{1,0:T(8,128)(2,1)S(1)} %get-tuple-element.23.refs_0_, ...), custom_call_target="tpu_custom_call" | custom-call | tf_op jit(solution)/shard_map/grad_parts/pallas_call | solution.py:153
  46.6 2.8 %collective-permute-start.12 = (bf16[64,2304]{1,0:T(8,128)(2,1)S(1)}, bf16[64,2304]{1,0:T(8,128)(2,1)S(1)}, u32[]{:S(2)}, u32[]{:S(2)}) collective-permute-start(bf16[64,2304]{1,0:T(8,128)(2,1)S(1)} %get-tuple-element.34), channel_id=1, source_target_pairs={{0,24},{1,97},{2,26},{3,99},{4,28},{5,101},{6,30},{7,103},{8,0},{9... | collective-permute-start | bytes 884744 | tf_op jit(solution)/shard_map/ppermute | solution.py:58
  49.3 2.7 %collective-permute-start.11 = (bf16[64,2304]{1,0:T(8,128)(2,1)S(1)}, bf16[64,2304]{1,0:T(8,128)(2,1)S(1)}, u32[]{:S(2)}, u32[]{:S(2)}) collective-permute-start(bf16[64,2304]{1,0:T(8,128)(2,1)S(1)} %get-tuple-element.32), channel_id=1, source_target_pairs={{0,24},{1,97},{2,26},{3,99},{4,28},{5,101},{6,30},{7,103},{8,0},{9... | collective-permute-start | bytes 884744 | tf_op jit(solution)/shard_map/ppermute | solution.py:58
  52.0 1.0 collective-permute-done.12
  53.0 0.1 add_convert_fusion.1
  53.1 3.4 %collective-permute-start.13 = (bf16[64,2304]{1,0:T(8,128)(2,1)S(1)}, bf16[64,2304]{1,0:T(8,128)(2,1)S(1)}, u32[]{:S(2)}, u32[]{:S(2)}) collective-permute-start(bf16[64,2304]{1,0:T(8,128)(2,1)S(1)} %add_convert_fusion.1), channel_id=1, source_target_pairs={{0,24},{1,97},{2,26},{3,99},{4,28},{5,101},{6,30},{7,103},{8,0},{9... | collective-permute-start | bytes 884744 | tf_op jit(solution)/shard_map/ppermute | solution.py:58
  56.5 0.1 add_convert_fusion.3
  56.5 0.1 collective-permute-start.10
  56.6 2.9 %collective-permute-done.14 = bf16[64,2304]{1,0:T(8,128)(2,1)S(1)} collective-permute-done((bf16[64,2304]{1,0:T(8,128)(2,1)S(1)}, bf16[64,2304]{1,0:T(8,128)(2,1)S(1)}, u32[]{:S(2)}, u32[]{:S(2)}) %collective-permute-start.14) | collective-permute-done | bytes 294944 | tf_op jit(solution)/shard_map/ppermute | solution.py:58
  59.6 0.5 collective-permute-done.13
  60.1 3.3 %collective-permute-done.10 = bf16[64,2304]{1,0:T(8,128)(2,1)S(1)} collective-permute-done((bf16[64,2304]{1,0:T(8,128)(2,1)S(1)}, bf16[64,2304]{1,0:T(8,128)(2,1)S(1)}, u32[]{:S(2)}, u32[]{:S(2)}) %collective-permute-start.10) | collective-permute-done | bytes 294944 | tf_op jit(solution)/shard_map/ppermute | solution.py:58
  63.4 0.2 add_convert_fusion.2
  63.6 0.0 copy-start.11
  63.6 0.0 copy-start.12
  63.6 0.0 copy-start.13
  63.7 0.0 copy-start.14
  63.7 20.6 %all_to_all.10 = bf16[8,16,2304]{2,1,0:T(8,128)(2,1)S(1)} all-to-all(bf16[8,16,2304]{2,1,0:T(8,128)(2,1)S(1)} %bitcast.26), channel_id=1, replica_groups=mesh['zl'=2,'x'=4,'y'=4,'zh'=4,'c'=2] {'zl','zh'}, dimensions={0} | all-to-all | bytes 1179648 | tf_op jit(solution)/shard_map/all_to_all | solution.py:291
  84.3 0.1 convert_reduce_fusion
  84.4 0.9 subtract_convert_fusion
  85.3 15.2 %all_to_all.11 = bf16[8,16,2304]{2,1,0:T(8,128)(2,1)S(1)} all-to-all(bf16[8,16,2304]{2,1,0:T(8,128)(2,1)S(1)} %broadcast_in_dim.2), channel_id=1, replica_groups=mesh['zl'=2,'x'=4,'y'=4,'zh'=4,'c'=2] {'zl','zh'}, dimensions={0} | all-to-all | bytes 1179648 | tf_op jit(solution)/shard_map/all_to_all | solution.py:303
  100.6 0.1 collective-permute-start.17
  100.7 2.7 %collective-permute-start.16 = (bf16[64,2304]{1,0:T(8,128)(2,1)S(1)}, bf16[64,2304]{1,0:T(8,128)(2,1)S(1)}, u32[]{:S(2)}, u32[]{:S(2)}) collective-permute-start(bf16[64,2304]{1,0:T(8,128)(2,1)S(1)} %bitcast.16), channel_id=1, source_target_pairs={{0,24},{1,97},{2,26},{3,99},{4,28},{5,101},{6,30},{7,103},{8,0},{9... | collective-permute-start | bytes 884744 | tf_op jit(solution)/shard_map/ppermute | solution.py:58
  103.4 0.0 collective-permute-start.15
  103.4 1.4 collective-permute-start.20
  104.8 2.9 %collective-permute-done.17.refs_14_ = bf16[64,2304]{1,0:T(8,128)(2,1)S(1)} collective-permute-done((bf16[64,2304]{1,0:T(8,128)(2,1)S(1)}, bf16[64,2304]{1,0:T(8,128)(2,1)S(1)}, u32[]{:S(2)}, u32[]{:S(2)}) %collective-permute-start.17) | collective-permute-done | bytes 294944 | tf_op jit(solution)/shard_map/ppermute | solution.py:58
  107.8 2.7 %collective-permute-start.19 = (bf16[64,2304]{1,0:T(8,128)(2,1)S(1)}, bf16[64,2304]{1,0:T(8,128)(2,1)S(1)}, u32[]{:S(2)}, u32[]{:S(2)}) collective-permute-start(bf16[64,2304]{1,0:T(8,128)(2,1)S(1)} %collective-permute-done.16.refs_11_), channel_id=1, source_target_pairs={{0,24},{1,97},{2,26},{3,99},{4,28},{5,101},{6,30},{7,103},{8,0},{9... | collective-permute-start | bytes 884744 | tf_op jit(solution)/shard_map/ppermute | solution.py:58
  110.4 0.2 collective-permute-done.20.refs_15_
  110.6 4.2 %collective-permute-done.18.refs_12_ = bf16[64,2304]{1,0:T(8,128)(2,1)S(1)} collective-permute-done((bf16[64,2304]{1,0:T(8,128)(2,1)S(1)}, bf16[64,2304]{1,0:T(8,128)(2,1)S(1)}, u32[]{:S(2)}, u32[]{:S(2)}) %collective-permute-start.18) | collective-permute-done | bytes 294944 | tf_op jit(solution)/shard_map/ppermute | solution.py:58
  114.8 7.1 %value_parts.1 = (f32[256,256]{1,0:T(8,128)S(1)}, bf16[256,256]{1,0:T(8,128)(2,1)S(1)}, bf16[256,512]{1,0:T(8,128)(2,1)S(1)}, bf16[256,512]{1,0:T(8,128)(2,1)S(1)}, bf16[256,512]{1,0:T(8,128)(2,1)S(1)}) custom-call(s32[3]{0:T(128)S(1)} %pad_add_fusion.place_ref, bf16[128,2304]{1,0:T(8,128)(2,1)S(1)} %get-tuple-element.27.refs_4_.refs_0_, ...), custom_call_target="tpu_custom_call" | custom-call | tf_op jit(solution)/shard_map/value_parts/pallas_call | solution.py:204
  122.0 0.0 copy-start.5
  122.0 1.2 collective-permute-start.23
  123.1 5.9 %collective-permute-start.22 = (bf16[256,512]{1,0:T(8,128)(2,1)S(1)}, bf16[256,512]{1,0:T(8,128)(2,1)S(1)}, u32[]{:S(2)}, u32[]{:S(2)}) collective-permute-start(bf16[256,512]{1,0:T(8,128)(2,1)S(1)} %get-tuple-element.38), channel_id=1, source_target_pairs={{0,64},{1,17},{2,66},{3,19},{4,68},{5,21},{6,70},{7,23},{8,72},{9,... | collective-permute-start | bytes 786440 | tf_op jit(solution)/shard_map/ppermute | solution.py:58
  129.0 2.0 %collective-permute-start.21 = (bf16[256,512]{1,0:T(8,128)(2,1)S(1)}, bf16[256,512]{1,0:T(8,128)(2,1)S(1)}, u32[]{:S(2)}, u32[]{:S(2)}) collective-permute-start(bf16[256,512]{1,0:T(8,128)(2,1)S(1)} %get-tuple-element.37), channel_id=1, source_target_pairs={{0,96},{1,25},{2,98},{3,27},{4,100},{5,29},{6,102},{7,31},{8,104},... | collective-permute-start | bytes 786440 | tf_op jit(solution)/shard_map/ppermute | solution.py:58
  131.0 0.5 collective-permute-done.23.refs_3_
  131.4 4.0 %collective-permute-done.22.refs_2_ = bf16[256,512]{1,0:T(8,128)(2,1)S(1)} collective-permute-done((bf16[256,512]{1,0:T(8,128)(2,1)S(1)}, bf16[256,512]{1,0:T(8,128)(2,1)S(1)}, u32[]{:S(2)}, u32[]{:S(2)}) %collective-permute-start.22) | collective-permute-done | bytes 262176 | tf_op jit(solution)/shard_map/ppermute | solution.py:58
  135.5 0.1 pad_maximum_fusion.1
  135.6 9.0 %collective-permute-start.24 = (bf16[4,256,256]{2,1,0:T(8,128)(2,1)S(1)}, bf16[4,256,256]{2,1,0:T(8,128)(2,1)S(1)}, u32[]{:S(2)}, u32[]{:S(2)}) collective-permute-start(bf16[4,256,256]{2,1,0:T(8,128)(2,1)S(1)} %pad_maximum_fusion.1), channel_id=1, source_target_pairs={{0,1},{1,0},{2,3},{3,2},{4,5},{5,4},{6,7},{7,6},{8,9},{9,8},{10,11... | collective-permute-start | bytes 1572872 | tf_op jit(solution)/shard_map/ppermute | solution.py:58
  144.6 0.1 copy.14.flag_ref
  144.7 1.4 collective-permute-done.24.refs_4_
  146.1 2.0 %joined.1 = f32[256,1024]{1,0:T(8,128)} custom-call(s32[3]{0:T(128)S(1)} %pad_add_fusion.place_ref, s32[256,1]{1,0:T(8,128)S(1)} %copy.14.flag_ref, f32[256,256]{1,0:T(8,128)S(1)} %get-tuple-element.36.refs_0_, bf16[256,512]{1,0:T(8,128)(2,1)S(1)} %collective-permute-done.21.refs_1_, bf16[256,512]{1,0:T(8,128)(2,1)S(1)} %collective-permute-done.22.refs_2_, ...), custom_call_target="tpu_custom_call" | custom-call | tf_op jit(solution)/shard_map/joined/pallas_call | solution.py:240
  (37 shorter events, 0.2 us)
Async XLA Ops:
  0.6 1.7 %copy-start.1 = (bf16[512,2304]{1,0:T(8,128)(2,1)S(1)}, bf16[512,2304]{1,0:T(8,128)(2,1)}, u32[]{:S(2)}) copy-start(bf16[512,2304]{1,0:T(8,128)(2,1)} %buffer_ref.1) | copy-start | bytes 7077892
  2.3 1.3 copy-start.2
  3.6 0.7 copy-start.4
  4.2 0.7 copy-start.6
  4.9 5.7 %copy-start.3 = (bf16[256,2048]{1,0:T(8,128)(2,1)S(1)}, bf16[256,2048]{1,0:T(8,128)(2,1)}, u32[]{:S(2)}) copy-start(bf16[256,2048]{1,0:T(8,128)(2,1)} %cot_ref.1) | copy-start | bytes 3145732
  6.8 11.2 %collective-permute-start.5 = (bf16[128,2304]{1,0:T(8,128)(2,1)S(1)}, bf16[128,2304]{1,0:T(8,128)(2,1)S(1)}, u32[]{:S(2)}, u32[]{:S(2)}) collective-permute-start(bf16[128,2304]{1,0:T(8,128)(2,1)S(1)} %get-tuple-element.27.refs_4_.refs_0_), channel_id=1, source_target_pairs={{0,32},{1,9},{2,34},{3,11},{4,36},{5,13},{6,38},{7,15},{8,40},{9,1... | collective-permute-start | bytes 1769480 | tf_op jit(solution)/shard_map/ppermute | solution.py:58
  9.0 9.0 %collective-permute-start.4 = (bf16[128,2304]{1,0:T(8,128)(2,1)S(1)}, bf16[128,2304]{1,0:T(8,128)(2,1)S(1)}, u32[]{:S(2)}, u32[]{:S(2)}) collective-permute-start(bf16[128,2304]{1,0:T(8,128)(2,1)S(1)} %get-tuple-element.28.refs_5_.refs_1_), channel_id=1, source_target_pairs={{0,96},{1,25},{2,98},{3,27},{4,100},{5,29},{6,102},{7,31},{8,104},... | collective-permute-start | bytes 1769480 | tf_op jit(solution)/shard_map/ppermute | solution.py:58
  11.6 9.3 %collective-permute-start = (bf16[512,256]{1,0:T(8,128)(2,1)S(1)}, bf16[512,256]{1,0:T(8,128)(2,1)S(1)}, u32[]{:S(2)}, u32[]{:S(2)}) collective-permute-start(bf16[512,256]{1,0:T(8,128)(2,1)S(1)} %get-tuple-element.24), channel_id=1, source_target_pairs={{0,96},{1,25},{2,98},{3,27},{4,100},{5,29},{6,102},{7,31},{8,104},... | collective-permute-start | bytes 786440 | tf_op jit(solution)/shard_map/ppermute | solution.py:58
  13.0 27.2 %collective-permute-start.3 = (bf16[128,2304]{1,0:T(8,128)(2,1)S(1)}, bf16[128,2304]{1,0:T(8,128)(2,1)S(1)}, u32[]{:S(2)}, u32[]{:S(2)}) collective-permute-start(bf16[128,2304]{1,0:T(8,128)(2,1)S(1)} %get-tuple-element.27.refs_4_.refs_0_), channel_id=1, source_target_pairs={{0,96},{1,25},{2,98},{3,27},{4,100},{5,29},{6,102},{7,31},{8,104},... | collective-permute-start | bytes 1769480 | tf_op jit(solution)/shard_map/ppermute | solution.py:58
  13.5 26.7 %collective-permute-start.6 = (bf16[128,2304]{1,0:T(8,128)(2,1)S(1)}, bf16[128,2304]{1,0:T(8,128)(2,1)S(1)}, u32[]{:S(2)}, u32[]{:S(2)}) collective-permute-start(bf16[128,2304]{1,0:T(8,128)(2,1)S(1)} %get-tuple-element.28.refs_5_.refs_1_), channel_id=1, source_target_pairs={{0,32},{1,9},{2,34},{3,11},{4,36},{5,13},{6,38},{7,15},{8,40},{9,1... | collective-permute-start | bytes 1769480 | tf_op jit(solution)/shard_map/ppermute | solution.py:58
  18.0 28.5 %copy-start = (bf16[128,2304]{1,0:T(8,128)(2,1)}, bf16[128,2304]{1,0:T(8,128)(2,1)S(1)}, u32[]{:S(2)}) copy-start(bf16[128,2304]{1,0:T(8,128)(2,1)S(1)} %collective-permute-done.5.refs_8_.refs_4_) | copy-start | bytes 1769476
  18.0 22.2 %collective-permute-start.7 = (bf16[128,2304]{1,0:T(8,128)(2,1)S(1)}, bf16[128,2304]{1,0:T(8,128)(2,1)S(1)}, u32[]{:S(2)}, u32[]{:S(2)}) collective-permute-start(bf16[128,2304]{1,0:T(8,128)(2,1)S(1)} %collective-permute-done.5.refs_8_.refs_4_), channel_id=1, source_target_pairs={{0,32},{1,9},{2,34},{3,11},{4,36},{5,13},{6,38},{7,15},{8,40},{9,1... | collective-permute-start | bytes 1769480 | tf_op jit(solution)/shard_map/ppermute | solution.py:58
  18.0 22.2 %collective-permute-start.8 = (bf16[128,2304]{1,0:T(8,128)(2,1)S(1)}, bf16[128,2304]{1,0:T(8,128)(2,1)S(1)}, u32[]{:S(2)}, u32[]{:S(2)}) collective-permute-start(bf16[128,2304]{1,0:T(8,128)(2,1)S(1)} %collective-permute-done.4.refs_7_.refs_3_), channel_id=1, source_target_pairs={{0,96},{1,25},{2,98},{3,27},{4,100},{5,29},{6,102},{7,31},{8,104},... | collective-permute-start | bytes 1769480 | tf_op jit(solution)/shard_map/ppermute | solution.py:58
  20.9 12.6 %collective-permute-start.1 = (bf16[512,256]{1,0:T(8,128)(2,1)S(1)}, bf16[512,256]{1,0:T(8,128)(2,1)S(1)}, u32[]{:S(2)}, u32[]{:S(2)}) collective-permute-start(bf16[512,256]{1,0:T(8,128)(2,1)S(1)} %get-tuple-element.25), channel_id=1, source_target_pairs={{0,32},{1,9},{2,34},{3,11},{4,36},{5,13},{6,38},{7,15},{8,40},{9,1... | collective-permute-start | bytes 786440 | tf_op jit(solution)/shard_map/ppermute | solution.py:58
  33.5 6.7 %collective-permute-start.2 = (bf16[512,256]{1,0:T(8,128)(2,1)S(1)}, bf16[512,256]{1,0:T(8,128)(2,1)S(1)}, u32[]{:S(2)}, u32[]{:S(2)}) collective-permute-start(bf16[512,256]{1,0:T(8,128)(2,1)S(1)} %get-tuple-element.26), channel_id=1, source_target_pairs={{0,64},{1,17},{2,66},{3,19},{4,68},{5,21},{6,70},{7,23},{8,72},{9,... | collective-permute-start | bytes 786440 | tf_op jit(solution)/shard_map/ppermute | solution.py:58
  40.2 0.8 copy-start.7
  40.2 1.0 copy-start.8
  40.2 1.2 copy-start.9
  46.6 16.8 %copy-start.10 = (f32[128,2304]{1,0:T(8,128)S(1)}, f32[128,2304]{1,0:T(8,128)}, u32[]{:S(2)}) copy-start(f32[128,2304]{1,0:T(8,128)} %get-tuple-element.29) | copy-start | bytes 3538948
  46.6 6.5 %collective-permute-start.12 = (bf16[64,2304]{1,0:T(8,128)(2,1)S(1)}, bf16[64,2304]{1,0:T(8,128)(2,1)S(1)}, u32[]{:S(2)}, u32[]{:S(2)}) collective-permute-start(bf16[64,2304]{1,0:T(8,128)(2,1)S(1)} %get-tuple-element.34), channel_id=1, source_target_pairs={{0,24},{1,97},{2,26},{3,99},{4,28},{5,101},{6,30},{7,103},{8,0},{9... | collective-permute-start | bytes 884744 | tf_op jit(solution)/shard_map/ppermute | solution.py:58
  49.3 7.1 %collective-permute-start.9 = (bf16[64,2304]{1,0:T(8,128)(2,1)S(1)}, bf16[64,2304]{1,0:T(8,128)(2,1)S(1)}, u32[]{:S(2)}, u32[]{:S(2)}) collective-permute-start(bf16[64,2304]{1,0:T(8,128)(2,1)S(1)} %get-tuple-element.31), channel_id=1, source_target_pairs={{0,8},{1,33},{2,10},{3,35},{4,12},{5,37},{6,14},{7,39},{8,16},{9,4... | collective-permute-start | bytes 884744 | tf_op jit(solution)/shard_map/ppermute | solution.py:58
  49.3 7.3 %collective-permute-start.11 = (bf16[64,2304]{1,0:T(8,128)(2,1)S(1)}, bf16[64,2304]{1,0:T(8,128)(2,1)S(1)}, u32[]{:S(2)}, u32[]{:S(2)}) collective-permute-start(bf16[64,2304]{1,0:T(8,128)(2,1)S(1)} %get-tuple-element.32), channel_id=1, source_target_pairs={{0,24},{1,97},{2,26},{3,99},{4,28},{5,101},{6,30},{7,103},{8,0},{9... | collective-permute-start | bytes 884744 | tf_op jit(solution)/shard_map/ppermute | solution.py:58
  52.0 7.6 %collective-permute-start.14 = (bf16[64,2304]{1,0:T(8,128)(2,1)S(1)}, bf16[64,2304]{1,0:T(8,128)(2,1)S(1)}, u32[]{:S(2)}, u32[]{:S(2)}) collective-permute-start(bf16[64,2304]{1,0:T(8,128)(2,1)S(1)} %get-tuple-element.35), channel_id=1, source_target_pairs={{0,8},{1,33},{2,10},{3,35},{4,12},{5,37},{6,14},{7,39},{8,16},{9,4... | collective-permute-start | bytes 884744 | tf_op jit(solution)/shard_map/ppermute | solution.py:58
  53.1 7.0 %collective-permute-start.13 = (bf16[64,2304]{1,0:T(8,128)(2,1)S(1)}, bf16[64,2304]{1,0:T(8,128)(2,1)S(1)}, u32[]{:S(2)}, u32[]{:S(2)}) collective-permute-start(bf16[64,2304]{1,0:T(8,128)(2,1)S(1)} %add_convert_fusion.1), channel_id=1, source_target_pairs={{0,24},{1,97},{2,26},{3,99},{4,28},{5,101},{6,30},{7,103},{8,0},{9... | collective-permute-start | bytes 884744 | tf_op jit(solution)/shard_map/ppermute | solution.py:58
  56.5 6.9 %collective-permute-start.10 = (bf16[64,2304]{1,0:T(8,128)(2,1)S(1)}, bf16[64,2304]{1,0:T(8,128)(2,1)S(1)}, u32[]{:S(2)}, u32[]{:S(2)}) collective-permute-start(bf16[64,2304]{1,0:T(8,128)(2,1)S(1)} %add_convert_fusion.3), channel_id=1, source_target_pairs={{0,8},{1,33},{2,10},{3,35},{4,12},{5,37},{6,14},{7,39},{8,16},{9,4... | collective-permute-start | bytes 884744 | tf_op jit(solution)/shard_map/ppermute | solution.py:58
  63.6 20.7 %copy-start.11 = (f32[16,2304]{1,0:T(8,128)S(1)}, f32[16,2304]{1,0:T(8,128)}, u32[]{:S(2)}) copy-start(f32[16,2304]{1,0:T(8,128)} %param.17) | copy-start | bytes 442372
  63.6 20.7 %copy-start.12 = (f32[16,2304]{1,0:T(8,128)S(1)}, f32[16,2304]{1,0:T(8,128)}, u32[]{:S(2)}) copy-start(f32[16,2304]{1,0:T(8,128)} %param.14) | copy-start | bytes 442372
  63.6 20.7 %copy-start.13 = (f32[16,2304]{1,0:T(8,128)S(1)}, f32[16,2304]{1,0:T(8,128)}, u32[]{:S(2)}) copy-start(f32[16,2304]{1,0:T(8,128)} %param.15) | copy-start | bytes 442372
  63.7 20.7 %copy-start.14 = (f32[16,2304]{1,0:T(8,128)S(1)}, f32[16,2304]{1,0:T(8,128)}, u32[]{:S(2)}) copy-start(f32[16,2304]{1,0:T(8,128)} %param.16) | copy-start | bytes 442372
  100.6 7.2 %collective-permute-start.17 = (bf16[64,2304]{1,0:T(8,128)(2,1)S(1)}, bf16[64,2304]{1,0:T(8,128)(2,1)S(1)}, u32[]{:S(2)}, u32[]{:S(2)}) collective-permute-start(bf16[64,2304]{1,0:T(8,128)(2,1)S(1)} %bitcast.19), channel_id=1, source_target_pairs={{0,8},{1,33},{2,10},{3,35},{4,12},{5,37},{6,14},{7,39},{8,16},{9,4... | collective-permute-start | bytes 884744 | tf_op jit(solution)/shard_map/ppermute | solution.py:58
  100.7 7.1 %collective-permute-start.16 = (bf16[64,2304]{1,0:T(8,128)(2,1)S(1)}, bf16[64,2304]{1,0:T(8,128)(2,1)S(1)}, u32[]{:S(2)}, u32[]{:S(2)}) collective-permute-start(bf16[64,2304]{1,0:T(8,128)(2,1)S(1)} %bitcast.16), channel_id=1, source_target_pairs={{0,24},{1,97},{2,26},{3,99},{4,28},{5,101},{6,30},{7,103},{8,0},{9... | collective-permute-start | bytes 884744 | tf_op jit(solution)/shard_map/ppermute | solution.py:58
  103.4 7.1 %collective-permute-start.15 = (bf16[64,2304]{1,0:T(8,128)(2,1)S(1)}, bf16[64,2304]{1,0:T(8,128)(2,1)S(1)}, u32[]{:S(2)}, u32[]{:S(2)}) collective-permute-start(bf16[64,2304]{1,0:T(8,128)(2,1)S(1)} %bitcast.20), channel_id=1, source_target_pairs={{0,24},{1,97},{2,26},{3,99},{4,28},{5,101},{6,30},{7,103},{8,0},{9... | collective-permute-start | bytes 884744 | tf_op jit(solution)/shard_map/ppermute | solution.py:58
  103.4 7.2 %collective-permute-start.20 = (bf16[64,2304]{1,0:T(8,128)(2,1)S(1)}, bf16[64,2304]{1,0:T(8,128)(2,1)S(1)}, u32[]{:S(2)}, u32[]{:S(2)}) collective-permute-start(bf16[64,2304]{1,0:T(8,128)(2,1)S(1)} %bitcast.17), channel_id=1, source_target_pairs={{0,8},{1,33},{2,10},{3,35},{4,12},{5,37},{6,14},{7,39},{8,16},{9,4... | collective-permute-start | bytes 884744 | tf_op jit(solution)/shard_map/ppermute | solution.py:58
  107.8 7.1 %collective-permute-start.18 = (bf16[64,2304]{1,0:T(8,128)(2,1)S(1)}, bf16[64,2304]{1,0:T(8,128)(2,1)S(1)}, u32[]{:S(2)}, u32[]{:S(2)}) collective-permute-start(bf16[64,2304]{1,0:T(8,128)(2,1)S(1)} %collective-permute-done.17.refs_14_), channel_id=1, source_target_pairs={{0,8},{1,33},{2,10},{3,35},{4,12},{5,37},{6,14},{7,39},{8,16},{9,4... | collective-permute-start | bytes 884744 | tf_op jit(solution)/shard_map/ppermute | solution.py:58
  107.8 7.1 %collective-permute-start.19 = (bf16[64,2304]{1,0:T(8,128)(2,1)S(1)}, bf16[64,2304]{1,0:T(8,128)(2,1)S(1)}, u32[]{:S(2)}, u32[]{:S(2)}) collective-permute-start(bf16[64,2304]{1,0:T(8,128)(2,1)S(1)} %collective-permute-done.16.refs_11_), channel_id=1, source_target_pairs={{0,24},{1,97},{2,26},{3,99},{4,28},{5,101},{6,30},{7,103},{8,0},{9... | collective-permute-start | bytes 884744 | tf_op jit(solution)/shard_map/ppermute | solution.py:58
  122.0 22.6 %copy-start.5 = (s32[256]{0:T(256)S(1)}, s32[256]{0:T(256)}, u32[]{:S(2)}) copy-start(s32[256]{0:T(256)} %param.12) | copy-start | bytes 3076
  122.0 9.5 %collective-permute-start.23 = (bf16[256,512]{1,0:T(8,128)(2,1)S(1)}, bf16[256,512]{1,0:T(8,128)(2,1)S(1)}, u32[]{:S(2)}, u32[]{:S(2)}) collective-permute-start(bf16[256,512]{1,0:T(8,128)(2,1)S(1)} %get-tuple-element.39), channel_id=1, source_target_pairs={{0,32},{1,9},{2,34},{3,11},{4,36},{5,13},{6,38},{7,15},{8,40},{9,1... | collective-permute-start | bytes 786440 | tf_op jit(solution)/shard_map/ppermute | solution.py:58
  123.1 12.3 %collective-permute-start.22 = (bf16[256,512]{1,0:T(8,128)(2,1)S(1)}, bf16[256,512]{1,0:T(8,128)(2,1)S(1)}, u32[]{:S(2)}, u32[]{:S(2)}) collective-permute-start(bf16[256,512]{1,0:T(8,128)(2,1)S(1)} %get-tuple-element.38), channel_id=1, source_target_pairs={{0,64},{1,17},{2,66},{3,19},{4,68},{5,21},{6,70},{7,23},{8,72},{9,... | collective-permute-start | bytes 786440 | tf_op jit(solution)/shard_map/ppermute | solution.py:58
  129.0 6.5 %collective-permute-start.21 = (bf16[256,512]{1,0:T(8,128)(2,1)S(1)}, bf16[256,512]{1,0:T(8,128)(2,1)S(1)}, u32[]{:S(2)}, u32[]{:S(2)}) collective-permute-start(bf16[256,512]{1,0:T(8,128)(2,1)S(1)} %get-tuple-element.37), channel_id=1, source_target_pairs={{0,96},{1,25},{2,98},{3,27},{4,100},{5,29},{6,102},{7,31},{8,104},... | collective-permute-start | bytes 786440 | tf_op jit(solution)/shard_map/ppermute | solution.py:58
  135.6 10.5 %collective-permute-start.24 = (bf16[4,256,256]{2,1,0:T(8,128)(2,1)S(1)}, bf16[4,256,256]{2,1,0:T(8,128)(2,1)S(1)}, u32[]{:S(2)}, u32[]{:S(2)}) collective-permute-start(bf16[4,256,256]{2,1,0:T(8,128)(2,1)S(1)} %pad_maximum_fusion.1), channel_id=1, source_target_pairs={{0,1},{1,0},{2,3},{3,2},{4,5},{5,4},{6,7},{7,6},{8,9},{9,8},{10,11... | collective-permute-start | bytes 1572872 | tf_op jit(solution)/shard_map/ppermute | solution.py:58

commit v2 on v1

v2 whole, which is shorter than its diff:
```python
import functools
import itertools
import math

import jax
import jax.numpy as jnp
from jax import lax
from jax.experimental import pallas as pl
from jax.experimental.pallas import tpu as pltpu
from jax.sharding import Mesh, PartitionSpec as P

beta_one = 0.9
beta_two = 0.999
learn_rate = 0.001
adam_eps = 1e-08
ema_decay = 0.99
corr_one = 1.0 - math.exp(100.0 * math.log(0.9))
corr_two = 1.0 - math.exp(100.0 * math.log(0.999))

bf16, f32 = jnp.bfloat16, jnp.float32
AXES = ("zl", "x", "y", "zh", "c")
SIZES = (2, 4, 4, 4, 2)
ROWS = tuple(AXES[:4])
VMEM_LIMIT = 16 * 1024 * 1024
SHARE_LIMIT = 52 * 1024 * 1024


def flat(zl, x, y, zh, c):
    return (((zl * 4 + x) * 4 + y) * 4 + zh) * 2 + c


def pairs(move):
    return [
        (flat(*place), flat(*move(*place)))
        for place in itertools.product(*map(range, SIZES))
    ]


def first_ring(s):
    return pairs(
        lambda zl, x, y, zh, c: (zl, (x + s) % 4, y, zh, c)
        if c == 0
        else (zl, x, (y + s) % 4, zh, c)
    )


def second_ring(s):
    return pairs(
        lambda zl, x, y, zh, c: (zl, x, (y + s) % 4, zh, c)
        if c == 0
        else (zl, (x + s) % 4, y, zh, c)
    )


other_core = pairs(lambda zl, x, y, zh, c: (zl, x, y, zh, 1 - c))


def send(array, perm):
    return lax.ppermute(array, AXES, perm)


def dot(lhs, rhs, left, right):
    return lax.dot_general(
        lhs, rhs, (((left,), (right,)), ((), ())), preferred_element_type=f32
    )


def params():
    return pltpu.CompilerParams(vmem_limit_bytes=VMEM_LIMIT)


def cost(flops, size):
    return pl.CostEstimate(flops=flops, bytes_accessed=size, transcendentals=0)


def in_vmem(count):
    return [pl.BlockSpec(memory_space=pltpu.VMEM)] * count


def scalars():
    return [pl.BlockSpec(memory_space=pltpu.SMEM)]


COLS = 256


def share_kernel(*refs):
    place_ref, slot_ref, buffer_hbm, fresh_hbm, cot_hbm = refs[:5]
    a_ref, b_ref, up_ref, down_ref, own_ref, far_ref = refs[5:11]
    buffer_ref, fresh_ref, cot_ref, turned, sems = refs[11:]
    slots, rows = buffer_ref.shape[0], fresh_ref.shape[0]
    width, half = fresh_ref.shape[1], fresh_ref.shape[0] // 2
    third = width // 3
    cot_copy = pltpu.make_async_copy(cot_hbm, cot_ref, sems.at[0])
    large = []
    for j in range(3):
        cut = (slice(None), pl.ds(j * third, third))
        large.append(
            (
                pltpu.make_async_copy(fresh_hbm.at[cut], fresh_ref.at[cut], sems.at[1 + j]),
                pltpu.make_async_copy(buffer_hbm.at[cut], buffer_ref.at[cut], sems.at[4 + j]),
            )
        )
    for copy in [cot_copy] + [copy for pair in large for copy in pair]:
        copy.start()

    wanted = slot_ref[...]
    slot = lax.broadcasted_iota(jnp.int32, (slots, rows), 0)
    pick = jnp.where(slot == wanted, 1.0, 0.0).astype(bf16).T
    same = lax.broadcasted_iota(jnp.int32, (rows, rows), 0) == lax.broadcasted_iota(
        jnp.int32, (rows, rows), 1
    )
    keep = jnp.where(same & (wanted < 0), 1.0, 0.0).astype(bf16).T

    cot_copy.wait()
    turned[...] = cot_ref[...].T
    c, p, q = place_ref[0], place_ref[1], place_ref[2]
    blocks = width // COLS
    cots = (
        own_ref,
        up_ref.at[pl.ds(blocks * half, 512)],
        far_ref,
        down_ref.at[pl.ds(blocks * half, 512)],
    )
    for k in range(4):
        pk = (p + k) % 4
        for d in range(4):
            qd = (q + d) % 4
            x = jnp.where(c == 0, pk, qd)
            y = jnp.where(c == 0, qd, pk)
            for zl in range(2):
                start = pl.multiple_of(zl * 1024 + x * 256 + y * 64, 64)
                cots[k][pl.ds(d * 128 + zl * 64, 64), :] = turned[pl.ds(start, 64), :]

    for j in range(blocks):
        if j % (blocks // 3) == 0:
            for copy in large[j // (blocks // 3)]:
                copy.wait()
        cut = (slice(None), pl.ds(j * COLS, COLS))
        got = dot(pick, buffer_ref[cut], 1, 0) + dot(keep, fresh_ref[cut], 1, 0)
        got = got.astype(bf16)
        at = pl.ds(j * half, half)
        a_ref[at, :] = got[:half]
        down_ref[at, :] = got[:half]
        b_ref[at, :] = got[half:]
        up_ref[at, :] = got[half:]


def shared(place, slot, buffer, fresh, cot):
    rows, width = fresh.shape
    tall = width // COLS * (rows // 2)
    shapes = [(tall, COLS)] * 2 + [(tall + 512, COLS)] * 2 + [(512, rows)] * 2
    hbm = pl.BlockSpec(memory_space=pl.ANY)
    return pl.pallas_call(
        share_kernel,
        in_specs=scalars() + in_vmem(1) + [hbm] * 3,
        out_specs=in_vmem(6),
        out_shape=[jax.ShapeDtypeStruct(shape, bf16) for shape in shapes],
        scratch_shapes=[
            pltpu.VMEM(buffer.shape, bf16),
            pltpu.VMEM(fresh.shape, bf16),
            pltpu.VMEM(cot.shape, bf16),
            pltpu.VMEM((cot.shape[1], rows), bf16),
            pltpu.SemaphoreType.DMA((7,)),
        ],
        compiler_params=pltpu.CompilerParams(vmem_limit_bytes=SHARE_LIMIT),
        cost_estimate=cost(2 * 768 * rows * width, 8 * rows * width),
        name="shared",
    )(place, slot, buffer, fresh, cot)


def column_block(half, j):
    return half[pl.ds(pl.multiple_of(j * 128, 128), 128), :]


def all_columns(half):
    return jnp.concatenate([half[128 * j : 128 * (j + 1), :] for j in range(9)], axis=1)


def near_kernel(own_ref, *refs):
    halves, out_ref = refs[:6], refs[6]
    carried = halves[0].shape[0]
    cots = (own_ref, halves[2].at[pl.ds(carried, 512)], halves[5].at[pl.ds(carried, 512)])

    @pl.loop(0, out_ref.shape[1] // COLS)
    def _(j):
        total = None
        for k in range(3):
            rows = jnp.concatenate(
                [column_block(halves[2 * k], j), column_block(halves[2 * k + 1], j)], axis=0
            )
            part = dot(cots[k][...], rows, 1, 0)
            total = part if total is None else total + part
        out_ref[:, pl.ds(pl.multiple_of(j * COLS, COLS), COLS)] = total


def near_grad(cot, halves):
    width = halves[0].shape[0] // 128 * COLS
    return pl.pallas_call(
        near_kernel,
        in_specs=in_vmem(7),
        out_specs=in_vmem(1)[0],
        out_shape=jax.ShapeDtypeStruct((512, width), f32),
        compiler_params=params(),
        cost_estimate=cost(2 * 768 * 512 * width, 8 * 512 * width),
        name="near_grad",
    )(cot, *halves)


def far_kernel(starts, near_ref, cot_ref, a_ref, b_ref, *outs):
    @pl.loop(0, near_ref.shape[1] // COLS)
    def _(j):
        cut = (slice(None), pl.ds(pl.multiple_of(j * COLS, COLS), COLS))
        rows = jnp.concatenate([column_block(a_ref, j), column_block(b_ref, j)], axis=0)
        sums = {}
        for start, out in zip(starts, outs):
            chunk, low = start // 128, start % 128
            if chunk not in sums:
                at = slice(128 * chunk, 128 * chunk + 128)
                sums[chunk] = near_ref[at, cut[1]] + dot(cot_ref[at, :], rows, 1, 0)
            out[cut] = sums[chunk][low : low + out.shape[0]].astype(out.dtype)


def grad_parts(starts, near, cot, a, b):
    width = near.shape[1]
    out_shape = [
        jax.ShapeDtypeStruct((64, width), bf16)
        if start
        else jax.ShapeDtypeStruct((128, width), f32)
        for start in starts
    ]
    return pl.pallas_call(
        functools.partial(far_kernel, starts),
        in_specs=in_vmem(4),
        out_specs=in_vmem(len(starts)),
        out_shape=out_shape,
        compiler_params=params(),
        cost_estimate=cost(2 * 256 * 64 * len(starts) * width, 4 * 512 * width),
        name="grad_parts",
    )(near, cot, a, b)


def own_first(c, a, b):
    return [jnp.where(c == 0, a, b), jnp.where(c == 0, b, a)]


def values_kernel(groups, place_ref, *refs):
    halves, gaps, out_ref = refs[:8], refs[8 : 8 + 2 * groups], refs[8 + 2 * groups]
    c = place_ref[0]
    gap = []
    for n in range(groups):
        gap += own_first(c, gaps[2 * n][...], gaps[2 * n + 1][...])
    gap = jnp.concatenate(gap, axis=0)
    for k in range(4):
        rows = jnp.concatenate(
            [all_columns(halves[2 * k]), all_columns(halves[2 * k + 1])], axis=0
        )
        out_ref[pl.ds(256 * k, 256), :] = dot(rows, gap, 1, 1)


def values(place, halves, gaps):
    groups, width = len(gaps) // 2, gaps[0].shape[1]
    return pl.pallas_call(
        functools.partial(values_kernel, groups),
        in_specs=scalars() + in_vmem(len(halves) + len(gaps)),
        out_specs=in_vmem(1)[0],
        out_shape=jax.ShapeDtypeStruct((1024, 128 * groups), f32),
        compiler_params=params(),
        cost_estimate=cost(2 * 1024 * 128 * groups * width, 4 * 1024 * width),
        name="values",
    )(place, *halves, *gaps)


def packed(q, tiles):
    pairs_of = lambda left, right, lo: jnp.concatenate(
        [left[:, lo : lo + 64], right[:, lo : lo + 64]], axis=1
    )
    both = []
    for lo in (0, 64):
        line = jnp.concatenate(
            [pairs_of(tiles[0], tiles[1], lo), pairs_of(tiles[2], tiles[3], lo)], axis=1
        )
        both.append(pltpu.roll(line, q * 64, 1))
    return both


def last_kernel(devices, place_ref, own_ref, side_ref, *refs):
    count = len(devices)
    halves, gaps, outs = refs[: 2 * count], refs[2 * count : 2 * count + 2], refs[2 * count + 2 :]
    c, q = place_ref[0], place_ref[2]
    gap = jnp.concatenate(own_first(c, gaps[0][...], gaps[1][...]), axis=0)
    for n, k in enumerate(devices):
        rows = jnp.concatenate(
            [all_columns(halves[2 * n]), all_columns(halves[2 * n + 1])], axis=0
        )
        part = dot(rows, gap, 1, 1)
        cut = pl.ds(256 * k, 256)
        side = side_ref[cut, :]
        mine, over = packed(q, (own_ref[cut, :], side[:, :128], part, side[:, 128:]))
        if k == 0:
            outs[n][...] = mine
            outs[n + 1][...] = over.astype(bf16)
        else:
            outs[n][:, :256] = mine.astype(bf16)
            outs[n][:, 256:] = over.astype(bf16)


def value_parts(devices, place, own, side, halves, gaps):
    width = gaps[0].shape[1]
    out_shape = []
    for k in devices:
        if k == 0:
            out_shape.append(jax.ShapeDtypeStruct((256, 256), f32))
            out_shape.append(jax.ShapeDtypeStruct((256, 256), bf16))
        else:
            out_shape.append(jax.ShapeDtypeStruct((256, 512), bf16))
    taken = [half for k in devices for half in halves[2 * k : 2 * k + 2]]
    return pl.pallas_call(
        functools.partial(last_kernel, devices),
        in_specs=scalars() + in_vmem(4 + len(taken)),
        out_specs=in_vmem(len(out_shape)),
        out_shape=out_shape,
        compiler_params=params(),
        cost_estimate=cost(2 * 256 * len(devices) * 128 * width, 1024 * width),
        name="value_parts",
    )(place, own, side, *taken, *gaps)


def join_kernel(place_ref, flag_ref, *refs):
    mine, over, out_ref, held = refs[:4], refs[4:8], refs[8], refs[9]
    c, p, q = place_ref[0], place_ref[1], place_ref[2]
    for d in range(4):
        held[c, (p + d) % 4] = mine[d][:, :256].astype(f32)
        held[1 - c, (q + d) % 4] = over[d][:, -256:].astype(f32)
    flag = flag_ref[...].astype(f32)
    for x in range(4):
        for j in range(2):
            near = held[0, x, :, j * 128 : (j + 1) * 128]
            far = jnp.concatenate(
                [
                    held[1, 2 * j, :, x * 64 : (x + 1) * 64],
                    held[1, 2 * j + 1, :, x * 64 : (x + 1) * 64],
                ],
                axis=1,
            )
            out_ref[:, x * 256 + j * 128 : x * 256 + (j + 1) * 128] = (near + far) * flag


def joined(place, flag, mine, over):
    vmem = pl.BlockSpec(memory_space=pltpu.VMEM)
    return pl.pallas_call(
        join_kernel,
        in_specs=[pl.BlockSpec(memory_space=pltpu.SMEM)] + [vmem] * 9,
        out_specs=vmem,
        out_shape=jax.ShapeDtypeStruct((256, 1024), f32),
        scratch_shapes=[pltpu.VMEM((2, 4, 256, 256), f32)],
        compiler_params=params(),
        name="joined",
    )(place, flag.reshape(256, 1), *mine, *over)


def body(
    fresh, replay_buffer, replay_index, from_replay, cotangent, master, moment1, moment2, teacher
):
    c, x, y = (lax.axis_index(a) for a in ("c", "x", "y"))
    p = jnp.where(c == 0, x, y)
    q = jnp.where(c == 0, y, x)
    place = jnp.stack([c, p, q]).astype(jnp.int32)
    total_rows = fresh.shape[0] * lax.axis_size(ROWS)

    up, down = first_ring(1), first_ring(-1)
    slot = jnp.where(from_replay == 1, replay_index, -1).reshape(1, -1)
    a, b, b_cot, a_cot, cot_own, cot_over = shared(
        place, slot, replay_buffer, fresh, cotangent
    )
    left_a = send(a, up)
    right_b = send(b, down)
    left_b = send(b_cot, up)
    right_a = send(a_cot, down)
    cot_far = send(cot_over, first_ring(2))
    far_a = send(left_a, up)
    far_b = send(right_b, down)
    halves = (a, b, right_a, right_b, left_a, left_b, far_a, far_b)
    near = near_grad(cot_own, halves[:6])
    far = (near, cot_far, far_a, far_b)
    a2, b2 = grad_parts((256, 320), *far)
    am, bm, b1, a1, own = grad_parts((384, 448, 192, 128, 0), *far)

    up2, down2 = second_ring(1), second_ring(-1)
    pass_a = send(a2, up2)
    pass_b = send(b2, down2)
    got_b = send(b1, up2)
    got_a = send(am, down2)
    sum_a = send((a1.astype(f32) + pass_a.astype(f32)).astype(bf16), up2)
    sum_b = send((bm.astype(f32) + pass_b.astype(f32)).astype(bf16), down2)
    ring_sum = jnp.concatenate(
        [
            own[:64] + sum_a.astype(f32) + got_a.astype(f32),
            own[64:] + sum_b.astype(f32) + got_b.astype(f32),
        ],
        axis=0,
    ).astype(bf16)

    width = own.shape[1]
    slices = lax.all_to_all(ring_sum.reshape(8, 16, width), ("zl", "zh"), 0, 0, tiled=True)
    grad = jnp.sum(slices.astype(f32), axis=0)
    grad = grad * (1.0 / math.sqrt(total_rows))
    new_moment1 = beta_one * moment1 + (1.0 - beta_one) * grad
    new_moment2 = beta_two * moment2 + (1.0 - beta_two) * grad * grad
    new_master = master - learn_rate * (new_moment1 / corr_one) / (
        jnp.sqrt(new_moment2 / corr_two) + adam_eps
    )
    new_teacher = ema_decay * teacher + (1.0 - ema_decay) * new_master
    gap_low = (new_master - new_teacher).astype(bf16)

    copies = jnp.broadcast_to(gap_low[None], (8, 16, width))
    column = lax.all_to_all(copies, ("zl", "zh"), 0, 0, tiled=True)
    ga = column[:4].reshape(64, width)
    gb = column[4:].reshape(64, width)
    left_ga = send(ga, up2)
    right_gb = send(gb, down2)
    left_gb = send(gb, up2)
    right_ga = send(ga, down2)
    far_ga = send(left_ga, up2)
    far_gb = send(right_gb, down2)
    first = values(place, halves, (ga, gb))
    side = values(place, halves, (right_ga, right_gb, left_ga, left_gb))
    known = (place, first, side, halves, (far_ga, far_gb))

    (out_far,) = value_parts((3,), *known)
    from_far = send(out_far, first_ring(2))
    out_right, out_left, mine, over = value_parts((1, 2, 0), *known)
    from_left = send(out_right, up)
    from_right = send(out_left, down)
    got = (from_right, from_far, from_left)
    crossed = [send(part, other_core) for part in (over,) + got]
    teacher_out = joined(place, from_replay, (mine,) + got, crossed)
    return (new_master, new_moment1, new_moment2, new_teacher, teacher_out)


def solution(mesh):
    fine = Mesh(mesh.devices.reshape(SIZES), AXES)
    split = P(ROWS, "c")
    return jax.shard_map(
        body,
        mesh=fine,
        in_specs=(split, split, P(ROWS), P(ROWS), P(ROWS, None), split, split, split, split),
        out_specs=(split, split, split, split, split),
        check_vma=False,
    )
```

time: 148 us -> 138 us (0.932)
  waiting for transfers between devices: 41 us -> 30.9 us
  local copies, waits for them, and re-layouts: 5.74 us -> 0.24 us
  Pallas kernels: 17.1 us -> 20.8 us
  blocking collectives: 35.8 us -> 37.5 us
    ppermute x25 -> x26, waiting for transfers between devices: 41 us -> 30.9 us  [send(): return lax.ppermute(array, AXES, perm)]
    unnamed x30 -> x10, local copies, waits for them, and re-layouts: 5.5 us -> 0.03 us
    pallas_call x4 -> x8, Pallas kernels: 15 us -> 18.8 us  [the longest x1 5.03 us: shared(): pl.pallas_call(share_kernel, in_specs=scalars() + in_vmem(1) + [hbm] * 3,...]
    ppermute x25 -> x26, starting transfers between devices: 46.2 us -> 45 us  [send(): return lax.ppermute(array, AXES, perm)]
  transfers between devices with their start and end apart: 25 -> 26, of which waited for: 14 -> 11; matrix products, arithmetic and copies ran while one was open for 0% -> 0% of each run, Pallas kernels for 1% -> 8%
where the time goes in v2:
time: 138 us; the launch traced here: 137 us
  starting transfers between devices  45 us (33%)
  blocking collectives  37.5 us (27%)
  waiting for transfers between devices  30.9 us (22%)
  Pallas kernels  20.8 us (15%)
  other arithmetic  2.13 us (2%)
    ppermute x26, starting transfers between devices, send(): return lax.ppermute(array, AXES, perm)  45 us
    ppermute x26, waiting for transfers between devices, send(): return lax.ppermute(array, AXES, perm)  30.9 us
    all_to_all x1, blocking collectives, body(): lax.all_to_all(ring_sum.reshape(8, 16, width), ('zl', 'zh'), 0, 0, tiled=...  21.7 us
    all_to_all x1, blocking collectives, body(): column = lax.all_to_all(copies, ('zl', 'zh'), 0, 0, tiled=True)  15.8 us
    pallas_call x1, Pallas kernels, shared(): pl.pallas_call(share_kernel, in_specs=scalars() + in_vmem(1) + [hbm] * 3,...  5.03 us
    pallas_call x2, Pallas kernels, values(): pl.pallas_call(functools.partial(values_kernel, groups), in_specs=scalars...  3.88 us
    pallas_call x2, Pallas kernels, grad_parts(): pl.pallas_call(functools.partial(far_kernel, starts), in_specs=in_vmem(4)...  3.46 us
    pallas_call x1, Pallas kernels, near_grad(): pl.pallas_call(near_kernel, in_specs=in_vmem(7), out_specs=in_vmem(1)[0],...  3.4 us
  transfers between devices with their start and end apart: 26, of which 11 were waited for; matrix products, arithmetic and copies ran while one was open for 0% of the time, Pallas kernels for 8%

profile of v2, /device:TPU:1, one launch (start us, length us, event | category | flops | bytes accessed | tf_op | source)
XLA Modules:
  0.0 137.4 jit_solution(3741457969744940465)
XLA Ops:
  0.6 0.7 compare_select_fusion
  1.3 0.1 pad_add_fusion.refs_0_.place_ref
  1.4 5.0 %shared.1 = (bf16[1152,256]{1,0:T(8,128)(2,1)S(1)}, bf16[1152,256]{1,0:T(8,128)(2,1)S(1)}, bf16[1664,256]{1,0:T(8,128)(2,1)}, bf16[1664,256]{1,0:T(8,128)(2,1)},...) custom-call(s32[3]{0:T(128)S(1)} %pad_add_fusion.refs_0_.place_ref, s32[1,256]{1,0:T(1,128)S(1)} %bitcast.14, ...), custom_call_target="tpu_custom_call" | custom-call | flops 905969664 | bytes 4718592 | tf_op jit(solution)/shard_map/shared/pallas_call | solution.py:154
  6.5 2.2 %collective-permute-start.2 = (bf16[1152,256]{1,0:T(8,128)(2,1)S(1)}, bf16[1152,256]{1,0:T(8,128)(2,1)S(1)}, u32[]{:S(2)}, u32[]{:S(2)}) collective-permute-start(bf16[1152,256]{1,0:T(8,128)(2,1)S(1)} %get-tuple-element.23.refs_0_.refs_4_), channel_id=1, source_target_pairs={{0,32},{1,9},{2,34},{3,11},{4,36},{5,13},{6,38},{7,15},{8,40},{9,1... | collective-permute-start | bytes 1769480 | tf_op jit(solution)/shard_map/ppermute | solution.py:59
  8.7 1.5 %collective-permute-start.1 = (bf16[1152,256]{1,0:T(8,128)(2,1)S(1)}, bf16[1152,256]{1,0:T(8,128)(2,1)S(1)}, u32[]{:S(2)}, u32[]{:S(2)}) collective-permute-start(bf16[1152,256]{1,0:T(8,128)(2,1)S(1)} %get-tuple-element.24.refs_1_.refs_5_), channel_id=1, source_target_pairs={{0,96},{1,25},{2,98},{3,27},{4,100},{5,29},{6,102},{7,31},{8,104},... | collective-permute-start | bytes 1769480 | tf_op jit(solution)/shard_map/ppermute | solution.py:59
  10.2 1.4 %collective-permute-start = (bf16[1664,256]{1,0:T(8,128)(2,1)}, bf16[1664,256]{1,0:T(8,128)(2,1)S(1)}, u32[]{:S(2)}, u32[]{:S(2)}) collective-permute-start(bf16[1664,256]{1,0:T(8,128)(2,1)} %get-tuple-element.25), channel_id=1, source_target_pairs={{0,96},{1,25},{2,98},{3,27},{4,100},{5,29},{6,102},{7,31},{8,104},... | collective-permute-start | bytes 2555912 | tf_op jit(solution)/shard_map/ppermute | solution.py:59
  11.6 0.1 collective-permute-start.3
  11.7 6.0 %collective-permute-done.2.refs_4_.refs_2_ = bf16[1152,256]{1,0:T(8,128)(2,1)S(1)} collective-permute-done((bf16[1152,256]{1,0:T(8,128)(2,1)S(1)}, bf16[1152,256]{1,0:T(8,128)(2,1)S(1)}, u32[]{:S(2)}, u32[]{:S(2)}) %collective-permute-start.2) | collective-permute-done | bytes 589856 | tf_op jit(solution)/shard_map/ppermute | solution.py:59
  17.7 0.0 collective-permute-start.5
  17.7 2.7 %collective-permute-start.6 = (bf16[1152,256]{1,0:T(8,128)(2,1)S(1)}, bf16[1152,256]{1,0:T(8,128)(2,1)S(1)}, u32[]{:S(2)}, u32[]{:S(2)}) collective-permute-start(bf16[1152,256]{1,0:T(8,128)(2,1)S(1)} %collective-permute-done.1.refs_3_.refs_1_), channel_id=1, source_target_pairs={{0,96},{1,25},{2,98},{3,27},{4,100},{5,29},{6,102},{7,31},{8,104},... | collective-permute-start | bytes 1769480 | tf_op jit(solution)/shard_map/ppermute | solution.py:59
  20.4 0.3 collective-permute-start.4
  20.8 6.0 %collective-permute-done.refs_2_.refs_0_ = bf16[1664,256]{1,0:T(8,128)(2,1)S(1)} collective-permute-done((bf16[1664,256]{1,0:T(8,128)(2,1)}, bf16[1664,256]{1,0:T(8,128)(2,1)S(1)}, u32[]{:S(2)}, u32[]{:S(2)}) %collective-permute-start) | collective-permute-done | bytes 852000 | tf_op jit(solution)/shard_map/ppermute | solution.py:59
  26.8 0.0 collective-permute-done.3.refs_5_.refs_3_
  26.8 3.4 %near_grad.1.near_ref = f32[512,2304]{1,0:T(8,128)S(1)} custom-call(bf16[512,256]{1,0:T(8,128)(2,1)S(1)} %get-tuple-element.22.own_ref, bf16[1152,256]{1,0:T(8,128)(2,1)S(1)} %get-tuple-element.23.refs_0_.refs_4_, bf16[1152,256]{1,0:T(8,128)(2,1)S(1)} %get-tuple-element.24.refs_1_.refs_5_, bf16[1664,256]{1,0:T(8,128)(2,1)S(1)} %collective-permute-done.refs_2_.refs_0_, ...), custom_call_target="tpu_custom_call" | custom-call | flops 1811939328 | bytes 9437184 | tf_op jit(solution)/shard_map/near_grad/pallas_call | solution.py:199
  30.2 6.9 %collective-permute-done.4.cot_ref = bf16[512,256]{1,0:T(8,128)(2,1)S(1)} collective-permute-done((bf16[512,256]{1,0:T(8,128)(2,1)S(1)}, bf16[512,256]{1,0:T(8,128)(2,1)S(1)}, u32[]{:S(2)}, u32[]{:S(2)}) %collective-permute-start.4) | collective-permute-done | bytes 262176 | tf_op jit(solution)/shard_map/ppermute | solution.py:59
  37.1 0.0 collective-permute-done.5.a_ref.refs_6_.refs_0_
  37.1 0.0 collective-permute-done.6.b_ref.refs_7_.refs_1_
  37.1 1.5 %grad_parts.3 = (bf16[64,2304]{1,0:T(8,128)(2,1)S(1)}, bf16[64,2304]{1,0:T(8,128)(2,1)S(1)}) custom-call(f32[512,2304]{1,0:T(8,128)S(1)} %near_grad.1.near_ref, bf16[512,256]{1,0:T(8,128)(2,1)S(1)} %collective-permute-done.4.cot_ref, bf16[1152,256]{1,0:T(8,128)(2,1)S(1)} %collective-permute-done.5.a_ref.refs_6_.refs_0_, ...), custom_call_target="tpu_custom_call" | custom-call | flops 150994944 | bytes 4718592 | tf_op jit(solution)/shard_map/grad_parts/pallas_call | solution.py:232
  38.6 2.6 %collective-permute-start.10 = (bf16[64,2304]{1,0:T(8,128)(2,1)S(1)}, bf16[64,2304]{1,0:T(8,128)(2,1)S(1)}, u32[]{:S(2)}, u32[]{:S(2)}) collective-permute-start(bf16[64,2304]{1,0:T(8,128)(2,1)S(1)} %get-tuple-element.33), channel_id=1, source_target_pairs={{0,24},{1,97},{2,26},{3,99},{4,28},{5,101},{6,30},{7,103},{8,0},{9... | collective-permute-start | bytes 884744 | tf_op jit(solution)/shard_map/ppermute | solution.py:59
  41.2 0.0 collective-permute-start.7
  41.2 1.9 %grad_parts.2 = (bf16[64,2304]{1,0:T(8,128)(2,1)S(1)}, bf16[64,2304]{1,0:T(8,128)(2,1)S(1)}, bf16[64,2304]{1,0:T(8,128)(2,1)S(1)}, bf16[64,2304]{1,0:T(8,128)(2,1)S(1)}, f32[128,2304]{1,0:T(8,128)S(1)}) custom-call(f32[512,2304]{1,0:T(8,128)S(1)} %near_grad.1.near_ref, bf16[512,256]{1,0:T(8,128)(2,1)S(1)} %collective-permute-done.4.cot_ref, ...), custom_call_target="tpu_custom_call" | custom-call | flops 377487360 | bytes 4718592 | tf_op jit(solution)/shard_map/grad_parts/pallas_call | solution.py:232
  43.1 0.1 collective-permute-start.12
  43.2 2.8 %collective-permute-start.9 = (bf16[64,2304]{1,0:T(8,128)(2,1)S(1)}, bf16[64,2304]{1,0:T(8,128)(2,1)S(1)}, u32[]{:S(2)}, u32[]{:S(2)}) collective-permute-start(bf16[64,2304]{1,0:T(8,128)(2,1)S(1)} %get-tuple-element.31), channel_id=1, source_target_pairs={{0,24},{1,97},{2,26},{3,99},{4,28},{5,101},{6,30},{7,103},{8,0},{9... | collective-permute-start | bytes 884744 | tf_op jit(solution)/shard_map/ppermute | solution.py:59
  46.0 0.1 add_convert_fusion.1
  46.1 2.1 %collective-permute-start.11 = (bf16[64,2304]{1,0:T(8,128)(2,1)S(1)}, bf16[64,2304]{1,0:T(8,128)(2,1)S(1)}, u32[]{:S(2)}, u32[]{:S(2)}) collective-permute-start(bf16[64,2304]{1,0:T(8,128)(2,1)S(1)} %add_convert_fusion.1), channel_id=1, source_target_pairs={{0,24},{1,97},{2,26},{3,99},{4,28},{5,101},{6,30},{7,103},{8,0},{9... | collective-permute-start | bytes 884744 | tf_op jit(solution)/shard_map/ppermute | solution.py:59
  48.1 0.1 collective-permute-done.7
  48.3 0.1 add_convert_fusion.3
  48.3 0.3 collective-permute-start.8
  48.6 2.8 %collective-permute-done.12 = bf16[64,2304]{1,0:T(8,128)(2,1)S(1)} collective-permute-done((bf16[64,2304]{1,0:T(8,128)(2,1)S(1)}, bf16[64,2304]{1,0:T(8,128)(2,1)S(1)}, u32[]{:S(2)}, u32[]{:S(2)}) %collective-permute-start.12) | collective-permute-done | bytes 294944 | tf_op jit(solution)/shard_map/ppermute | solution.py:59
  51.4 1.4 %collective-permute-done.11 = bf16[64,2304]{1,0:T(8,128)(2,1)S(1)} collective-permute-done((bf16[64,2304]{1,0:T(8,128)(2,1)S(1)}, bf16[64,2304]{1,0:T(8,128)(2,1)S(1)}, u32[]{:S(2)}, u32[]{:S(2)}) %collective-permute-start.11) | collective-permute-done | bytes 294944 | tf_op jit(solution)/shard_map/ppermute | solution.py:59
  52.8 2.6 %collective-permute-done.8 = bf16[64,2304]{1,0:T(8,128)(2,1)S(1)} collective-permute-done((bf16[64,2304]{1,0:T(8,128)(2,1)S(1)}, bf16[64,2304]{1,0:T(8,128)(2,1)S(1)}, u32[]{:S(2)}, u32[]{:S(2)}) %collective-permute-start.8) | collective-permute-done | bytes 294944 | tf_op jit(solution)/shard_map/ppermute | solution.py:59
  55.4 0.2 add_convert_fusion.2
  55.6 0.0 copy-start
  55.7 0.0 copy-start.1
  55.7 0.0 copy-start.2
  55.7 0.0 copy-start.3
  55.7 21.7 %all_to_all.10 = bf16[8,16,2304]{2,1,0:T(8,128)(2,1)S(1)} all-to-all(bf16[8,16,2304]{2,1,0:T(8,128)(2,1)S(1)} %bitcast.15), channel_id=1, replica_groups=mesh['zl'=2,'x'=4,'y'=4,'zh'=4,'c'=2] {'zl','zh'}, dimensions={0} | all-to-all | bytes 1179648 | tf_op jit(solution)/shard_map/all_to_all | solution.py:405
  77.4 0.1 convert_reduce_fusion
  77.5 0.9 subtract_convert_fusion
  78.4 15.8 %all_to_all.11 = bf16[8,16,2304]{2,1,0:T(8,128)(2,1)S(1)} all-to-all(bf16[8,16,2304]{2,1,0:T(8,128)(2,1)S(1)} %broadcast_in_dim.11), channel_id=1, replica_groups=mesh['zl'=2,'x'=4,'y'=4,'zh'=4,'c'=2] {'zl','zh'}, dimensions={0} | all-to-all | bytes 1179648 | tf_op jit(solution)/shard_map/all_to_all | solution.py:417
  94.3 0.1 collective-permute-start.15
  94.3 2.7 %collective-permute-start.14 = (bf16[64,2304]{1,0:T(8,128)(2,1)S(1)}, bf16[64,2304]{1,0:T(8,128)(2,1)S(1)}, u32[]{:S(2)}, u32[]{:S(2)}) collective-permute-start(bf16[64,2304]{1,0:T(8,128)(2,1)S(1)} %bitcast.8), channel_id=1, source_target_pairs={{0,24},{1,97},{2,26},{3,99},{4,28},{5,101},{6,30},{7,103},{8,0},{9... | collective-permute-start | bytes 884744 | tf_op jit(solution)/shard_map/ppermute | solution.py:59
  97.0 0.0 collective-permute-start.13
  97.0 1.4 %collective-permute-start.16 = (bf16[64,2304]{1,0:T(8,128)(2,1)S(1)}, bf16[64,2304]{1,0:T(8,128)(2,1)S(1)}, u32[]{:S(2)}, u32[]{:S(2)}) collective-permute-start(bf16[64,2304]{1,0:T(8,128)(2,1)S(1)} %bitcast.9), channel_id=1, source_target_pairs={{0,8},{1,33},{2,10},{3,35},{4,12},{5,37},{6,14},{7,39},{8,16},{9,4... | collective-permute-start | bytes 884744 | tf_op jit(solution)/shard_map/ppermute | solution.py:59
  98.5 2.6 %collective-permute-done.15.refs_10_ = bf16[64,2304]{1,0:T(8,128)(2,1)S(1)} collective-permute-done((bf16[64,2304]{1,0:T(8,128)(2,1)S(1)}, bf16[64,2304]{1,0:T(8,128)(2,1)S(1)}, u32[]{:S(2)}, u32[]{:S(2)}) %collective-permute-start.15) | collective-permute-done | bytes 294944 | tf_op jit(solution)/shard_map/ppermute | solution.py:59
  101.1 0.0 collective-permute-start.17
  101.1 0.0 collective-permute-done.14.refs_9_
  101.1 2.7 %collective-permute-start.18 = (bf16[64,2304]{1,0:T(8,128)(2,1)S(1)}, bf16[64,2304]{1,0:T(8,128)(2,1)S(1)}, u32[]{:S(2)}, u32[]{:S(2)}) collective-permute-start(bf16[64,2304]{1,0:T(8,128)(2,1)S(1)} %collective-permute-done.14.refs_9_), channel_id=1, source_target_pairs={{0,24},{1,97},{2,26},{3,99},{4,28},{5,101},{6,30},{7,103},{8,0},{9... | collective-permute-start | bytes 884744 | tf_op jit(solution)/shard_map/ppermute | solution.py:59
  103.8 1.9 %values.2.own_ref = f32[1024,128]{1,0:T(8,128)S(1)} custom-call(s32[3]{0:T(128)S(1)} %pad_add_fusion.refs_0_.place_ref, bf16[1152,256]{1,0:T(8,128)(2,1)S(1)} %get-tuple-element.23.refs_0_.refs_4_, bf16[1152,256]{1,0:T(8,128)(2,1)S(1)} %get-tuple-element.24.refs_1_.refs_5_, bf16[1664,256]{1,0:T(8,128)(2,1)S(1)} %collective-permute-done.refs_2_.refs_0_, ...), custom_call_target="tpu_custom_call" | custom-call | flops 603979776 | bytes 9437184 | tf_op jit(solution)/shard_map/values/pallas_call | solution.py:263
  105.7 2.0 %values.3.side_ref = f32[1024,256]{1,0:T(8,128)S(1)} custom-call(s32[3]{0:T(128)S(1)} %pad_add_fusion.refs_0_.place_ref, bf16[1152,256]{1,0:T(8,128)(2,1)S(1)} %get-tuple-element.23.refs_0_.refs_4_, bf16[1152,256]{1,0:T(8,128)(2,1)S(1)} %get-tuple-element.24.refs_1_.refs_5_, bf16[1664,256]{1,0:T(8,128)(2,1)S(1)} %collective-permute-done.refs_2_.refs_0_, ...), custom_call_target="tpu_custom_call" | custom-call | flops 1207959552 | bytes 9437184 | tf_op jit(solution)/shard_map/values/pallas_call | solution.py:263
  107.7 0.5 collective-permute-done.17.refs_6_.refs_2_
  108.2 1.2 value_parts.3
  109.4 0.0 copy-start.4
  109.4 1.6 %collective-permute-start.20 = (bf16[256,512]{1,0:T(8,128)(2,1)S(1)}, bf16[256,512]{1,0:T(8,128)(2,1)S(1)}, u32[]{:S(2)}, u32[]{:S(2)}) collective-permute-start(bf16[256,512]{1,0:T(8,128)(2,1)S(1)} %value_parts.3), channel_id=1, source_target_pairs={{0,64},{1,17},{2,66},{3,19},{4,68},{5,21},{6,70},{7,23},{8,72},{9,... | collective-permute-start | bytes 786440 | tf_op jit(solution)/shard_map/ppermute | solution.py:59
  110.9 1.8 %value_parts.2 = (bf16[256,512]{1,0:T(8,128)(2,1)S(1)}, bf16[256,512]{1,0:T(8,128)(2,1)S(1)}, f32[256,256]{1,0:T(8,128)S(1)}, bf16[256,256]{1,0:T(8,128)(2,1)S(1)}) custom-call(s32[3]{0:T(128)S(1)} %pad_add_fusion.refs_0_.place_ref, f32[1024,128]{1,0:T(8,128)S(1)} %values.2.own_ref, f32[1024,256]{1,0:T(8,128)S(1)} %values.3.side_ref, ...), custom_call_target="tpu_custom_call" | custom-call | flops 452984832 | bytes 2359296 | tf_op jit(solution)/shard_map/value_parts/pallas_call | solution.py:318
  112.8 5.6 %collective-permute-start.19 = (bf16[256,512]{1,0:T(8,128)(2,1)S(1)}, bf16[256,512]{1,0:T(8,128)(2,1)S(1)}, u32[]{:S(2)}, u32[]{:S(2)}) collective-permute-start(bf16[256,512]{1,0:T(8,128)(2,1)S(1)} %get-tuple-element.36), channel_id=1, source_target_pairs={{0,96},{1,25},{2,98},{3,27},{4,100},{5,29},{6,102},{7,31},{8,104},... | collective-permute-start | bytes 786440 | tf_op jit(solution)/shard_map/ppermute | solution.py:59
  118.4 0.7 collective-permute-done.20.refs_2_
  119.1 12.2 %collective-permute-start.24 = (bf16[256,512]{1,0:T(8,128)(2,1)S(1)}, bf16[256,512]{1,0:T(8,128)(2,1)S(1)}, u32[]{:S(2)}, u32[]{:S(2)}) collective-permute-start(bf16[256,512]{1,0:T(8,128)(2,1)S(1)} %collective-permute-done.20.refs_2_), channel_id=1, source_target_pairs={{0,1},{1,0},{2,3},{3,2},{4,5},{5,4},{6,7},{7,6},{8,9},{9,8},{10,11... | collective-permute-start | bytes 786440 | tf_op jit(solution)/shard_map/ppermute | solution.py:59
  131.2 0.4 collective-permute-start.23
  131.7 2.4 %collective-permute-start.25 = (bf16[256,512]{1,0:T(8,128)(2,1)S(1)}, bf16[256,512]{1,0:T(8,128)(2,1)S(1)}, u32[]{:S(2)}, u32[]{:S(2)}) collective-permute-start(bf16[256,512]{1,0:T(8,128)(2,1)S(1)} %collective-permute-done.21.refs_3_), channel_id=1, source_target_pairs={{0,1},{1,0},{2,3},{3,2},{4,5},{5,4},{6,7},{7,6},{8,9},{9,8},{10,11... | collective-permute-start | bytes 786440 | tf_op jit(solution)/shard_map/ppermute | solution.py:59
  134.0 0.0 collective-permute-start.22
  134.0 0.1 copy.14.flag_ref
  134.2 1.2 collective-permute-done.22.refs_4_
  135.4 2.0 %joined.1 = f32[256,1024]{1,0:T(8,128)} custom-call(s32[3]{0:T(128)S(1)} %pad_add_fusion.refs_0_.place_ref, s32[256,1]{1,0:T(8,128)S(1)} %copy.14.flag_ref, f32[256,256]{1,0:T(8,128)S(1)} %get-tuple-element.35.refs_0_, bf16[256,512]{1,0:T(8,128)(2,1)S(1)} %collective-permute-done.19.refs_1_, bf16[256,512]{1,0:T(8,128)(2,1)S(1)} %collective-permute-done.20.refs_2_, ...), custom_call_target="tpu_custom_call" | custom-call | tf_op jit(solution)/shard_map/joined/pallas_call | solution.py:351
  (20 shorter events, 0.2 us)
Async XLA Ops:
  6.5 11.2 %collective-permute-start.2 = (bf16[1152,256]{1,0:T(8,128)(2,1)S(1)}, bf16[1152,256]{1,0:T(8,128)(2,1)S(1)}, u32[]{:S(2)}, u32[]{:S(2)}) collective-permute-start(bf16[1152,256]{1,0:T(8,128)(2,1)S(1)} %get-tuple-element.23.refs_0_.refs_4_), channel_id=1, source_target_pairs={{0,32},{1,9},{2,34},{3,11},{4,36},{5,13},{6,38},{7,15},{8,40},{9,1... | collective-permute-start | bytes 1769480 | tf_op jit(solution)/shard_map/ppermute | solution.py:59
  8.7 9.0 %collective-permute-start.1 = (bf16[1152,256]{1,0:T(8,128)(2,1)S(1)}, bf16[1152,256]{1,0:T(8,128)(2,1)S(1)}, u32[]{:S(2)}, u32[]{:S(2)}) collective-permute-start(bf16[1152,256]{1,0:T(8,128)(2,1)S(1)} %get-tuple-element.24.refs_1_.refs_5_), channel_id=1, source_target_pairs={{0,96},{1,25},{2,98},{3,27},{4,100},{5,29},{6,102},{7,31},{8,104},... | collective-permute-start | bytes 1769480 | tf_op jit(solution)/shard_map/ppermute | solution.py:59
  10.2 16.6 %collective-permute-start = (bf16[1664,256]{1,0:T(8,128)(2,1)}, bf16[1664,256]{1,0:T(8,128)(2,1)S(1)}, u32[]{:S(2)}, u32[]{:S(2)}) collective-permute-start(bf16[1664,256]{1,0:T(8,128)(2,1)} %get-tuple-element.25), channel_id=1, source_target_pairs={{0,96},{1,25},{2,98},{3,27},{4,100},{5,29},{6,102},{7,31},{8,104},... | collective-permute-start | bytes 2555912 | tf_op jit(solution)/shard_map/ppermute | solution.py:59
  11.6 15.3 %collective-permute-start.3 = (bf16[1664,256]{1,0:T(8,128)(2,1)}, bf16[1664,256]{1,0:T(8,128)(2,1)S(1)}, u32[]{:S(2)}, u32[]{:S(2)}) collective-permute-start(bf16[1664,256]{1,0:T(8,128)(2,1)} %get-tuple-element.26), channel_id=1, source_target_pairs={{0,32},{1,9},{2,34},{3,11},{4,36},{5,13},{6,38},{7,15},{8,40},{9,1... | collective-permute-start | bytes 2555912 | tf_op jit(solution)/shard_map/ppermute | solution.py:59
  17.7 19.4 %collective-permute-start.5 = (bf16[1152,256]{1,0:T(8,128)(2,1)S(1)}, bf16[1152,256]{1,0:T(8,128)(2,1)S(1)}, u32[]{:S(2)}, u32[]{:S(2)}) collective-permute-start(bf16[1152,256]{1,0:T(8,128)(2,1)S(1)} %collective-permute-done.2.refs_4_.refs_2_), channel_id=1, source_target_pairs={{0,32},{1,9},{2,34},{3,11},{4,36},{5,13},{6,38},{7,15},{8,40},{9,1... | collective-permute-start | bytes 1769480 | tf_op jit(solution)/shard_map/ppermute | solution.py:59
  17.7 19.4 %collective-permute-start.6 = (bf16[1152,256]{1,0:T(8,128)(2,1)S(1)}, bf16[1152,256]{1,0:T(8,128)(2,1)S(1)}, u32[]{:S(2)}, u32[]{:S(2)}) collective-permute-start(bf16[1152,256]{1,0:T(8,128)(2,1)S(1)} %collective-permute-done.1.refs_3_.refs_1_), channel_id=1, source_target_pairs={{0,96},{1,25},{2,98},{3,27},{4,100},{5,29},{6,102},{7,31},{8,104},... | collective-permute-start | bytes 1769480 | tf_op jit(solution)/shard_map/ppermute | solution.py:59
  20.4 16.7 %collective-permute-start.4 = (bf16[512,256]{1,0:T(8,128)(2,1)S(1)}, bf16[512,256]{1,0:T(8,128)(2,1)S(1)}, u32[]{:S(2)}, u32[]{:S(2)}) collective-permute-start(bf16[512,256]{1,0:T(8,128)(2,1)S(1)} %get-tuple-element.27), channel_id=1, source_target_pairs={{0,64},{1,17},{2,66},{3,19},{4,68},{5,21},{6,70},{7,23},{8,72},{9,... | collective-permute-start | bytes 786440 | tf_op jit(solution)/shard_map/ppermute | solution.py:59
  38.6 7.4 %collective-permute-start.10 = (bf16[64,2304]{1,0:T(8,128)(2,1)S(1)}, bf16[64,2304]{1,0:T(8,128)(2,1)S(1)}, u32[]{:S(2)}, u32[]{:S(2)}) collective-permute-start(bf16[64,2304]{1,0:T(8,128)(2,1)S(1)} %get-tuple-element.33), channel_id=1, source_target_pairs={{0,24},{1,97},{2,26},{3,99},{4,28},{5,101},{6,30},{7,103},{8,0},{9... | collective-permute-start | bytes 884744 | tf_op jit(solution)/shard_map/ppermute | solution.py:59
  41.2 7.1 %collective-permute-start.7 = (bf16[64,2304]{1,0:T(8,128)(2,1)S(1)}, bf16[64,2304]{1,0:T(8,128)(2,1)S(1)}, u32[]{:S(2)}, u32[]{:S(2)}) collective-permute-start(bf16[64,2304]{1,0:T(8,128)(2,1)S(1)} %get-tuple-element.30), channel_id=1, source_target_pairs={{0,8},{1,33},{2,10},{3,35},{4,12},{5,37},{6,14},{7,39},{8,16},{9,4... | collective-permute-start | bytes 884744 | tf_op jit(solution)/shard_map/ppermute | solution.py:59
  43.1 8.3 %collective-permute-start.12 = (bf16[64,2304]{1,0:T(8,128)(2,1)S(1)}, bf16[64,2304]{1,0:T(8,128)(2,1)S(1)}, u32[]{:S(2)}, u32[]{:S(2)}) collective-permute-start(bf16[64,2304]{1,0:T(8,128)(2,1)S(1)} %get-tuple-element.34), channel_id=1, source_target_pairs={{0,8},{1,33},{2,10},{3,35},{4,12},{5,37},{6,14},{7,39},{8,16},{9,4... | collective-permute-start | bytes 884744 | tf_op jit(solution)/shard_map/ppermute | solution.py:59
  43.2 8.2 %collective-permute-start.9 = (bf16[64,2304]{1,0:T(8,128)(2,1)S(1)}, bf16[64,2304]{1,0:T(8,128)(2,1)S(1)}, u32[]{:S(2)}, u32[]{:S(2)}) collective-permute-start(bf16[64,2304]{1,0:T(8,128)(2,1)S(1)} %get-tuple-element.31), channel_id=1, source_target_pairs={{0,24},{1,97},{2,26},{3,99},{4,28},{5,101},{6,30},{7,103},{8,0},{9... | collective-permute-start | bytes 884744 | tf_op jit(solution)/shard_map/ppermute | solution.py:59
  46.1 6.8 %collective-permute-start.11 = (bf16[64,2304]{1,0:T(8,128)(2,1)S(1)}, bf16[64,2304]{1,0:T(8,128)(2,1)S(1)}, u32[]{:S(2)}, u32[]{:S(2)}) collective-permute-start(bf16[64,2304]{1,0:T(8,128)(2,1)S(1)} %add_convert_fusion.1), channel_id=1, source_target_pairs={{0,24},{1,97},{2,26},{3,99},{4,28},{5,101},{6,30},{7,103},{8,0},{9... | collective-permute-start | bytes 884744 | tf_op jit(solution)/shard_map/ppermute | solution.py:59
  48.3 7.0 %collective-permute-start.8 = (bf16[64,2304]{1,0:T(8,128)(2,1)S(1)}, bf16[64,2304]{1,0:T(8,128)(2,1)S(1)}, u32[]{:S(2)}, u32[]{:S(2)}) collective-permute-start(bf16[64,2304]{1,0:T(8,128)(2,1)S(1)} %add_convert_fusion.3), channel_id=1, source_target_pairs={{0,8},{1,33},{2,10},{3,35},{4,12},{5,37},{6,14},{7,39},{8,16},{9,4... | collective-permute-start | bytes 884744 | tf_op jit(solution)/shard_map/ppermute | solution.py:59
  55.6 21.8 %copy-start = (f32[16,2304]{1,0:T(8,128)S(1)}, f32[16,2304]{1,0:T(8,128)}, u32[]{:S(2)}) copy-start(f32[16,2304]{1,0:T(8,128)} %param.17) | copy-start | bytes 442372
  55.7 21.8 %copy-start.1 = (f32[16,2304]{1,0:T(8,128)S(1)}, f32[16,2304]{1,0:T(8,128)}, u32[]{:S(2)}) copy-start(f32[16,2304]{1,0:T(8,128)} %param.14) | copy-start | bytes 442372
  55.7 21.8 %copy-start.2 = (f32[16,2304]{1,0:T(8,128)S(1)}, f32[16,2304]{1,0:T(8,128)}, u32[]{:S(2)}) copy-start(f32[16,2304]{1,0:T(8,128)} %param.15) | copy-start | bytes 442372
  55.7 21.8 %copy-start.3 = (f32[16,2304]{1,0:T(8,128)S(1)}, f32[16,2304]{1,0:T(8,128)}, u32[]{:S(2)}) copy-start(f32[16,2304]{1,0:T(8,128)} %param.16) | copy-start | bytes 442372
  94.3 6.9 %collective-permute-start.15 = (bf16[64,2304]{1,0:T(8,128)(2,1)S(1)}, bf16[64,2304]{1,0:T(8,128)(2,1)S(1)}, u32[]{:S(2)}, u32[]{:S(2)}) collective-permute-start(bf16[64,2304]{1,0:T(8,128)(2,1)S(1)} %bitcast.11), channel_id=1, source_target_pairs={{0,8},{1,33},{2,10},{3,35},{4,12},{5,37},{6,14},{7,39},{8,16},{9,4... | collective-permute-start | bytes 884744 | tf_op jit(solution)/shard_map/ppermute | solution.py:59
  94.3 6.8 %collective-permute-start.14 = (bf16[64,2304]{1,0:T(8,128)(2,1)S(1)}, bf16[64,2304]{1,0:T(8,128)(2,1)S(1)}, u32[]{:S(2)}, u32[]{:S(2)}) collective-permute-start(bf16[64,2304]{1,0:T(8,128)(2,1)S(1)} %bitcast.8), channel_id=1, source_target_pairs={{0,24},{1,97},{2,26},{3,99},{4,28},{5,101},{6,30},{7,103},{8,0},{9... | collective-permute-start | bytes 884744 | tf_op jit(solution)/shard_map/ppermute | solution.py:59
  97.0 8.7 %collective-permute-start.13 = (bf16[64,2304]{1,0:T(8,128)(2,1)S(1)}, bf16[64,2304]{1,0:T(8,128)(2,1)S(1)}, u32[]{:S(2)}, u32[]{:S(2)}) collective-permute-start(bf16[64,2304]{1,0:T(8,128)(2,1)S(1)} %bitcast.12), channel_id=1, source_target_pairs={{0,24},{1,97},{2,26},{3,99},{4,28},{5,101},{6,30},{7,103},{8,0},{9... | collective-permute-start | bytes 884744 | tf_op jit(solution)/shard_map/ppermute | solution.py:59
  97.0 8.7 %collective-permute-start.16 = (bf16[64,2304]{1,0:T(8,128)(2,1)S(1)}, bf16[64,2304]{1,0:T(8,128)(2,1)S(1)}, u32[]{:S(2)}, u32[]{:S(2)}) collective-permute-start(bf16[64,2304]{1,0:T(8,128)(2,1)S(1)} %bitcast.9), channel_id=1, source_target_pairs={{0,8},{1,33},{2,10},{3,35},{4,12},{5,37},{6,14},{7,39},{8,16},{9,4... | collective-permute-start | bytes 884744 | tf_op jit(solution)/shard_map/ppermute | solution.py:59
  101.1 7.1 %collective-permute-start.17 = (bf16[64,2304]{1,0:T(8,128)(2,1)S(1)}, bf16[64,2304]{1,0:T(8,128)(2,1)S(1)}, u32[]{:S(2)}, u32[]{:S(2)}) collective-permute-start(bf16[64,2304]{1,0:T(8,128)(2,1)S(1)} %collective-permute-done.15.refs_10_), channel_id=1, source_target_pairs={{0,8},{1,33},{2,10},{3,35},{4,12},{5,37},{6,14},{7,39},{8,16},{9,4... | collective-permute-start | bytes 884744 | tf_op jit(solution)/shard_map/ppermute | solution.py:59
  101.1 7.1 %collective-permute-start.18 = (bf16[64,2304]{1,0:T(8,128)(2,1)S(1)}, bf16[64,2304]{1,0:T(8,128)(2,1)S(1)}, u32[]{:S(2)}, u32[]{:S(2)}) collective-permute-start(bf16[64,2304]{1,0:T(8,128)(2,1)S(1)} %collective-permute-done.14.refs_9_), channel_id=1, source_target_pairs={{0,24},{1,97},{2,26},{3,99},{4,28},{5,101},{6,30},{7,103},{8,0},{9... | collective-permute-start | bytes 884744 | tf_op jit(solution)/shard_map/ppermute | solution.py:59
  109.4 24.7 %copy-start.4 = (s32[256]{0:T(256)S(1)}, s32[256]{0:T(256)}, u32[]{:S(2)}) copy-start(s32[256]{0:T(256)} %param.12) | copy-start | bytes 3076
  109.4 9.7 %collective-permute-start.20 = (bf16[256,512]{1,0:T(8,128)(2,1)S(1)}, bf16[256,512]{1,0:T(8,128)(2,1)S(1)}, u32[]{:S(2)}, u32[]{:S(2)}) collective-permute-start(bf16[256,512]{1,0:T(8,128)(2,1)S(1)} %value_parts.3), channel_id=1, source_target_pairs={{0,64},{1,17},{2,66},{3,19},{4,68},{5,21},{6,70},{7,23},{8,72},{9,... | collective-permute-start | bytes 786440 | tf_op jit(solution)/shard_map/ppermute | solution.py:59
  112.8 18.5 %collective-permute-start.19 = (bf16[256,512]{1,0:T(8,128)(2,1)S(1)}, bf16[256,512]{1,0:T(8,128)(2,1)S(1)}, u32[]{:S(2)}, u32[]{:S(2)}) collective-permute-start(bf16[256,512]{1,0:T(8,128)(2,1)S(1)} %get-tuple-element.36), channel_id=1, source_target_pairs={{0,96},{1,25},{2,98},{3,27},{4,100},{5,29},{6,102},{7,31},{8,104},... | collective-permute-start | bytes 786440 | tf_op jit(solution)/shard_map/ppermute | solution.py:59
  118.4 13.3 %collective-permute-start.21 = (bf16[256,512]{1,0:T(8,128)(2,1)S(1)}, bf16[256,512]{1,0:T(8,128)(2,1)S(1)}, u32[]{:S(2)}, u32[]{:S(2)}) collective-permute-start(bf16[256,512]{1,0:T(8,128)(2,1)S(1)} %get-tuple-element.37), channel_id=1, source_target_pairs={{0,32},{1,9},{2,34},{3,11},{4,36},{5,13},{6,38},{7,15},{8,40},{9,1... | collective-permute-start | bytes 786440 | tf_op jit(solution)/shard_map/ppermute | solution.py:59
  119.1 16.3 %collective-permute-start.24 = (bf16[256,512]{1,0:T(8,128)(2,1)S(1)}, bf16[256,512]{1,0:T(8,128)(2,1)S(1)}, u32[]{:S(2)}, u32[]{:S(2)}) collective-permute-start(bf16[256,512]{1,0:T(8,128)(2,1)S(1)} %collective-permute-done.20.refs_2_), channel_id=1, source_target_pairs={{0,1},{1,0},{2,3},{3,2},{4,5},{5,4},{6,7},{7,6},{8,9},{9,8},{10,11... | collective-permute-start | bytes 786440 | tf_op jit(solution)/shard_map/ppermute | solution.py:59
  131.2 4.1 %collective-permute-start.23 = (bf16[256,512]{1,0:T(8,128)(2,1)S(1)}, bf16[256,512]{1,0:T(8,128)(2,1)S(1)}, u32[]{:S(2)}, u32[]{:S(2)}) collective-permute-start(bf16[256,512]{1,0:T(8,128)(2,1)S(1)} %collective-permute-done.19.refs_1_), channel_id=1, source_target_pairs={{0,1},{1,0},{2,3},{3,2},{4,5},{5,4},{6,7},{7,6},{8,9},{9,8},{10,11... | collective-permute-start | bytes 786440 | tf_op jit(solution)/shard_map/ppermute | solution.py:59
  131.7 3.7 %collective-permute-start.25 = (bf16[256,512]{1,0:T(8,128)(2,1)S(1)}, bf16[256,512]{1,0:T(8,128)(2,1)S(1)}, u32[]{:S(2)}, u32[]{:S(2)}) collective-permute-start(bf16[256,512]{1,0:T(8,128)(2,1)S(1)} %collective-permute-done.21.refs_3_), channel_id=1, source_target_pairs={{0,1},{1,0},{2,3},{3,2},{4,5},{5,4},{6,7},{7,6},{8,9},{9,8},{10,11... | collective-permute-start | bytes 786440 | tf_op jit(solution)/shard_map/ppermute | solution.py:59
  134.0 1.3 collective-permute-start.22

commit v3 on v2

--- a/solution.py
+++ b/solution.py
@@ -22,7 +22,7 @@
 SIZES = (2, 4, 4, 4, 2)
 ROWS = tuple(AXES[:4])
 VMEM_LIMIT = 16 * 1024 * 1024
-SHARE_LIMIT = 52 * 1024 * 1024
+SHARE_LIMIT = 50 * 1024 * 1024
 
 
 def flat(zl, x, y, zh, c):
@@ -82,12 +82,14 @@
 
 
 COLS = 256
+WIDTH = 2304
+TALL = WIDTH // COLS * 128
 
 
 def share_kernel(*refs):
     place_ref, slot_ref, buffer_hbm, fresh_hbm, cot_hbm = refs[:5]
-    a_ref, b_ref, up_ref, down_ref, own_ref, far_ref = refs[5:11]
-    buffer_ref, fresh_ref, cot_ref, turned, sems = refs[11:]
+    a_ref, b_ref, up_ref, down_ref, own_ref = refs[5:10]
+    buffer_ref, fresh_ref, cot_ref, turned, sems = refs[10:]
     slots, rows = buffer_ref.shape[0], fresh_ref.shape[0]
     width, half = fresh_ref.shape[1], fresh_ref.shape[0] // 2
     third = width // 3
@@ -116,21 +118,21 @@
     turned[...] = cot_ref[...].T
     c, p, q = place_ref[0], place_ref[1], place_ref[2]
     blocks = width // COLS
-    cots = (
-        own_ref,
-        up_ref.at[pl.ds(blocks * half, 512)],
-        far_ref,
-        down_ref.at[pl.ds(blocks * half, 512)],
-    )
     for k in range(4):
         pk = (p + k) % 4
         for d in range(4):
             qd = (q + d) % 4
             x = jnp.where(c == 0, pk, qd)
             y = jnp.where(c == 0, qd, pk)
+            if k == 2:
+                target, base = (a_ref, b_ref)[d // 2], TALL + d % 2 * 128
+            elif k == 0:
+                target, base = own_ref, d * 128
+            else:
+                target, base = up_ref if k == 1 else down_ref, TALL + d * 128
             for zl in range(2):
                 start = pl.multiple_of(zl * 1024 + x * 256 + y * 64, 64)
-                cots[k][pl.ds(d * 128 + zl * 64, 64), :] = turned[pl.ds(start, 64), :]
+                target[pl.ds(base + zl * 64, 64), :] = turned[pl.ds(start, 64), :]
 
     for j in range(blocks):
         if j % (blocks // 3) == 0:
@@ -148,13 +150,12 @@
 
 def shared(place, slot, buffer, fresh, cot):
     rows, width = fresh.shape
-    tall = width // COLS * (rows // 2)
-    shapes = [(tall, COLS)] * 2 + [(tall + 512, COLS)] * 2 + [(512, rows)] * 2
+    shapes = [(TALL + 256, COLS)] * 2 + [(TALL + 512, COLS)] * 2 + [(512, rows)]
     hbm = pl.BlockSpec(memory_space=pl.ANY)
     return pl.pallas_call(
         share_kernel,
         in_specs=scalars() + in_vmem(1) + [hbm] * 3,
-        out_specs=in_vmem(6),
+        out_specs=in_vmem(5),
         out_shape=[jax.ShapeDtypeStruct(shape, bf16) for shape in shapes],
         scratch_shapes=[
             pltpu.VMEM(buffer.shape, bf16),
@@ -179,8 +180,7 @@
 
 def near_kernel(own_ref, *refs):
     halves, out_ref = refs[:6], refs[6]
-    carried = halves[0].shape[0]
-    cots = (own_ref, halves[2].at[pl.ds(carried, 512)], halves[5].at[pl.ds(carried, 512)])
+    cots = (own_ref, halves[2].at[pl.ds(TALL, 512)], halves[5].at[pl.ds(TALL, 512)])
 
     @pl.loop(0, out_ref.shape[1] // COLS)
     def _(j):
@@ -195,7 +195,7 @@
 
 
 def near_grad(cot, halves):
-    width = halves[0].shape[0] // 128 * COLS
+    width = WIDTH
     return pl.pallas_call(
         near_kernel,
         in_specs=in_vmem(7),
@@ -207,7 +207,7 @@
     )(cot, *halves)
 
 
-def far_kernel(starts, near_ref, cot_ref, a_ref, b_ref, *outs):
+def far_kernel(starts, near_ref, a_ref, b_ref, *outs):
     @pl.loop(0, near_ref.shape[1] // COLS)
     def _(j):
         cut = (slice(None), pl.ds(pl.multiple_of(j * COLS, COLS), COLS))
@@ -217,11 +217,12 @@
             chunk, low = start // 128, start % 128
             if chunk not in sums:
                 at = slice(128 * chunk, 128 * chunk + 128)
-                sums[chunk] = near_ref[at, cut[1]] + dot(cot_ref[at, :], rows, 1, 0)
+                cot = (a_ref, b_ref)[chunk // 2][pl.ds(TALL + chunk % 2 * 128, 128), :]
+                sums[chunk] = near_ref[at, cut[1]] + dot(cot, rows, 1, 0)
             out[cut] = sums[chunk][low : low + out.shape[0]].astype(out.dtype)
 
 
-def grad_parts(starts, near, cot, a, b):
+def grad_parts(starts, near, a, b):
     width = near.shape[1]
     out_shape = [
         jax.ShapeDtypeStruct((64, width), bf16)
@@ -231,13 +232,13 @@
     ]
     return pl.pallas_call(
         functools.partial(far_kernel, starts),
-        in_specs=in_vmem(4),
+        in_specs=in_vmem(3),
         out_specs=in_vmem(len(starts)),
         out_shape=out_shape,
         compiler_params=params(),
         cost_estimate=cost(2 * 256 * 64 * len(starts) * width, 4 * 512 * width),
         name="grad_parts",
-    )(near, cot, a, b)
+    )(near, a, b)
 
 
 def own_first(c, a, b):
@@ -370,19 +371,18 @@
 
     up, down = first_ring(1), first_ring(-1)
     slot = jnp.where(from_replay == 1, replay_index, -1).reshape(1, -1)
-    a, b, b_cot, a_cot, cot_own, cot_over = shared(
+    a, b, b_cot, a_cot, cot_own = shared(
         place, slot, replay_buffer, fresh, cotangent
     )
     left_a = send(a, up)
     right_b = send(b, down)
     left_b = send(b_cot, up)
     right_a = send(a_cot, down)
-    cot_far = send(cot_over, first_ring(2))
     far_a = send(left_a, up)
     far_b = send(right_b, down)
     halves = (a, b, right_a, right_b, left_a, left_b, far_a, far_b)
     near = near_grad(cot_own, halves[:6])
-    far = (near, cot_far, far_a, far_b)
+    far = (near, far_a, far_b)
     a2, b2 = grad_parts((256, 320), *far)
     am, bm, b1, a1, own = grad_parts((384, 448, 192, 128, 0), *far)
 

time: 138 us -> 137 us (level)
    ppermute x26 -> x25, starting transfers between devices: 45 us -> 45.7 us  [send(): return lax.ppermute(array, AXES, perm)]
    ppermute x26 -> x25, waiting for transfers between devices: 30.9 us -> 30.8 us  [send(): return lax.ppermute(array, AXES, perm)]
  transfers between devices with their start and end apart: 26 -> 25, of which waited for: 11 -> 11; matrix products, arithmetic and copies ran while one was open for 0% -> 0% of each run, Pallas kernels for 8% -> 8%
where the time goes in v3:
time: 137 us
  starting transfers between devices  45.7 us (33%)
  blocking collectives  37.4 us (27%)
  waiting for transfers between devices  30.8 us (22%)
  Pallas kernels  19.7 us (14%)
  other arithmetic  2.13 us (2%)
    ppermute x25, starting transfers between devices, send(): return lax.ppermute(array, AXES, perm)  45.7 us
    ppermute x25, waiting for transfers between devices, send(): return lax.ppermute(array, AXES, perm)  30.8 us
    all_to_all x1, blocking collectives, body(): lax.all_to_all(ring_sum.reshape(8, 16, width), ('zl', 'zh'), 0, 0, tiled=...  21.2 us
    all_to_all x1, blocking collectives, body(): column = lax.all_to_all(copies, ('zl', 'zh'), 0, 0, tiled=True)  16.3 us
    pallas_call x1, Pallas kernels, shared(): pl.pallas_call(share_kernel, in_specs=scalars() + in_vmem(1) + [hbm] * 3,...  3.89 us
    pallas_call x2, Pallas kernels, values(): pl.pallas_call(functools.partial(values_kernel, groups), in_specs=scalars...  3.87 us
    pallas_call x2, Pallas kernels, grad_parts(): pl.pallas_call(functools.partial(far_kernel, starts), in_specs=in_vmem(3)...  3.45 us
    pallas_call x1, Pallas kernels, near_grad(): pl.pallas_call(near_kernel, in_specs=in_vmem(7), out_specs=in_vmem(1)[0],...  3.41 us
  transfers between devices with their start and end apart: 25, of which 11 were waited for; matrix products, arithmetic and copies ran while one was open for 0% of the time, Pallas kernels for 8%

profile of v3, /device:TPU:1, one launch (start us, length us, event | category | flops | bytes accessed | tf_op | source)
XLA Modules:
  0.0 136.7 jit_solution(14372086043998524849)
XLA Ops:
  0.6 0.7 compare_select_fusion
  1.3 0.1 pad_add_fusion.refs_0_.place_ref
  1.4 3.9 %shared.1 = (bf16[1408,256]{1,0:T(8,128)(2,1)S(1)}, bf16[1408,256]{1,0:T(8,128)(2,1)S(1)}, bf16[1664,256]{1,0:T(8,128)(2,1)S(1)}, bf16[1664,256]{1,0:T(8,128)(2,1)S(1)}, bf16[512,256]{1,0:T(8,128)(2,1)S(1)}) custom-call(s32[3]{0:T(128)S(1)} %pad_add_fusion.refs_0_.place_ref, s32[1,256]{1,0:T(1,128)S(1)} %bitcast.14, bf16[512,2304]{1,0:T(8,128)(2,1)} %refs_2_.1, ...), custom_call_target="tpu_custom_call" | custom-call | flops 905969664 | bytes 4718592 | tf_op jit(solution)/shard_map/shared/pallas_call | solution.py:155
  5.3 2.2 %collective-permute-start.2 = (bf16[1408,256]{1,0:T(8,128)(2,1)S(1)}, bf16[1408,256]{1,0:T(8,128)(2,1)S(1)}, u32[]{:S(2)}, u32[]{:S(2)}) collective-permute-start(bf16[1408,256]{1,0:T(8,128)(2,1)S(1)} %get-tuple-element.22.refs_0_.refs_4_), channel_id=1, source_target_pairs={{0,32},{1,9},{2,34},{3,11},{4,36},{5,13},{6,38},{7,15},{8,40},{9,1... | collective-permute-start | bytes 2162696 | tf_op jit(solution)/shard_map/ppermute | solution.py:59
  7.5 1.5 %collective-permute-start.1 = (bf16[1408,256]{1,0:T(8,128)(2,1)S(1)}, bf16[1408,256]{1,0:T(8,128)(2,1)S(1)}, u32[]{:S(2)}, u32[]{:S(2)}) collective-permute-start(bf16[1408,256]{1,0:T(8,128)(2,1)S(1)} %get-tuple-element.23.refs_1_.refs_5_), channel_id=1, source_target_pairs={{0,96},{1,25},{2,98},{3,27},{4,100},{5,29},{6,102},{7,31},{8,104},... | collective-permute-start | bytes 2162696 | tf_op jit(solution)/shard_map/ppermute | solution.py:59
  9.0 1.4 %collective-permute-start = (bf16[1664,256]{1,0:T(8,128)(2,1)S(1)}, bf16[1664,256]{1,0:T(8,128)(2,1)S(1)}, u32[]{:S(2)}, u32[]{:S(2)}) collective-permute-start(bf16[1664,256]{1,0:T(8,128)(2,1)S(1)} %get-tuple-element.24), channel_id=1, source_target_pairs={{0,96},{1,25},{2,98},{3,27},{4,100},{5,29},{6,102},{7,31},{8,104},... | collective-permute-start | bytes 2555912 | tf_op jit(solution)/shard_map/ppermute | solution.py:59
  10.4 0.1 collective-permute-start.3
  10.5 7.4 %collective-permute-done.2.refs_4_.refs_2_ = bf16[1408,256]{1,0:T(8,128)(2,1)S(1)} collective-permute-done((bf16[1408,256]{1,0:T(8,128)(2,1)S(1)}, bf16[1408,256]{1,0:T(8,128)(2,1)S(1)}, u32[]{:S(2)}, u32[]{:S(2)}) %collective-permute-start.2) | collective-permute-done | bytes 720928 | tf_op jit(solution)/shard_map/ppermute | solution.py:59
  17.9 0.0 collective-permute-start.4
  17.9 2.7 %collective-permute-start.5 = (bf16[1408,256]{1,0:T(8,128)(2,1)S(1)}, bf16[1408,256]{1,0:T(8,128)(2,1)S(1)}, u32[]{:S(2)}, u32[]{:S(2)}) collective-permute-start(bf16[1408,256]{1,0:T(8,128)(2,1)S(1)} %collective-permute-done.1.refs_3_.refs_1_), channel_id=1, source_target_pairs={{0,96},{1,25},{2,98},{3,27},{4,100},{5,29},{6,102},{7,31},{8,104},... | collective-permute-start | bytes 2162696 | tf_op jit(solution)/shard_map/ppermute | solution.py:59
  20.7 6.4 %collective-permute-done.refs_2_.refs_0_ = bf16[1664,256]{1,0:T(8,128)(2,1)S(1)} collective-permute-done((bf16[1664,256]{1,0:T(8,128)(2,1)S(1)}, bf16[1664,256]{1,0:T(8,128)(2,1)S(1)}, u32[]{:S(2)}, u32[]{:S(2)}) %collective-permute-start) | collective-permute-done | bytes 852000 | tf_op jit(solution)/shard_map/ppermute | solution.py:59
  27.1 0.0 collective-permute-done.3.refs_5_.refs_3_
  27.1 3.4 %near_grad.1.near_ref = f32[512,2304]{1,0:T(8,128)S(1)} custom-call(bf16[512,256]{1,0:T(8,128)(2,1)S(1)} %get-tuple-element.21.own_ref, bf16[1408,256]{1,0:T(8,128)(2,1)S(1)} %get-tuple-element.22.refs_0_.refs_4_, bf16[1408,256]{1,0:T(8,128)(2,1)S(1)} %get-tuple-element.23.refs_1_.refs_5_, bf16[1664,256]{1,0:T(8,128)(2,1)S(1)} %collective-permute-done.refs_2_.refs_0_, ...), custom_call_target="tpu_custom_call" | custom-call | flops 1811939328 | bytes 9437184 | tf_op jit(solution)/shard_map/near_grad/pallas_call | solution.py:199
  30.5 4.3 %collective-permute-done.4.a_ref.refs_6_.refs_0_ = bf16[1408,256]{1,0:T(8,128)(2,1)S(1)} collective-permute-done((bf16[1408,256]{1,0:T(8,128)(2,1)S(1)}, bf16[1408,256]{1,0:T(8,128)(2,1)S(1)}, u32[]{:S(2)}, u32[]{:S(2)}) %collective-permute-start.4) | collective-permute-done | bytes 720928 | tf_op jit(solution)/shard_map/ppermute | solution.py:59
  34.8 0.0 collective-permute-done.5.b_ref.refs_7_.refs_1_
  34.8 1.5 %grad_parts.3 = (bf16[64,2304]{1,0:T(8,128)(2,1)S(1)}, bf16[64,2304]{1,0:T(8,128)(2,1)S(1)}) custom-call(f32[512,2304]{1,0:T(8,128)S(1)} %near_grad.1.near_ref, bf16[1408,256]{1,0:T(8,128)(2,1)S(1)} %collective-permute-done.4.a_ref.refs_6_.refs_0_, bf16[1408,256]{1,0:T(8,128)(2,1)S(1)} %collective-permute-done.5.b_ref.refs_7_.refs_1_), custom_call_target="tpu_custom_call" | custom-call | flops 150994944 | bytes 4718592 | tf_op jit(solution)/shard_map/grad_parts/pallas_call | solution.py:233
  36.3 2.6 %collective-permute-start.9 = (bf16[64,2304]{1,0:T(8,128)(2,1)S(1)}, bf16[64,2304]{1,0:T(8,128)(2,1)S(1)}, u32[]{:S(2)}, u32[]{:S(2)}) collective-permute-start(bf16[64,2304]{1,0:T(8,128)(2,1)S(1)} %get-tuple-element.31), channel_id=1, source_target_pairs={{0,24},{1,97},{2,26},{3,99},{4,28},{5,101},{6,30},{7,103},{8,0},{9... | collective-permute-start | bytes 884744 | tf_op jit(solution)/shard_map/ppermute | solution.py:59
  38.9 0.0 collective-permute-start.6
  38.9 1.9 %grad_parts.2 = (bf16[64,2304]{1,0:T(8,128)(2,1)S(1)}, bf16[64,2304]{1,0:T(8,128)(2,1)S(1)}, bf16[64,2304]{1,0:T(8,128)(2,1)S(1)}, bf16[64,2304]{1,0:T(8,128)(2,1)S(1)}, f32[128,2304]{1,0:T(8,128)S(1)}) custom-call(f32[512,2304]{1,0:T(8,128)S(1)} %near_grad.1.near_ref, bf16[1408,256]{1,0:T(8,128)(2,1)S(1)} %collective-permute-done.4.a_ref.refs_6_.refs_0_, ...), custom_call_target="tpu_custom_call" | custom-call | flops 377487360 | bytes 4718592 | tf_op jit(solution)/shard_map/grad_parts/pallas_call | solution.py:233
  40.8 0.3 collective-permute-start.11
  41.1 2.6 %collective-permute-start.8 = (bf16[64,2304]{1,0:T(8,128)(2,1)S(1)}, bf16[64,2304]{1,0:T(8,128)(2,1)S(1)}, u32[]{:S(2)}, u32[]{:S(2)}) collective-permute-start(bf16[64,2304]{1,0:T(8,128)(2,1)S(1)} %get-tuple-element.29), channel_id=1, source_target_pairs={{0,24},{1,97},{2,26},{3,99},{4,28},{5,101},{6,30},{7,103},{8,0},{9... | collective-permute-start | bytes 884744 | tf_op jit(solution)/shard_map/ppermute | solution.py:59
  43.7 0.1 add_convert_fusion.1
  43.8 2.1 %collective-permute-start.10 = (bf16[64,2304]{1,0:T(8,128)(2,1)S(1)}, bf16[64,2304]{1,0:T(8,128)(2,1)S(1)}, u32[]{:S(2)}, u32[]{:S(2)}) collective-permute-start(bf16[64,2304]{1,0:T(8,128)(2,1)S(1)} %add_convert_fusion.1), channel_id=1, source_target_pairs={{0,24},{1,97},{2,26},{3,99},{4,28},{5,101},{6,30},{7,103},{8,0},{9... | collective-permute-start | bytes 884744 | tf_op jit(solution)/shard_map/ppermute | solution.py:59
  45.8 0.1 collective-permute-done.6
  46.0 0.1 add_convert_fusion.3
  46.0 0.1 collective-permute-start.7
  46.1 3.0 %collective-permute-done.11 = bf16[64,2304]{1,0:T(8,128)(2,1)S(1)} collective-permute-done((bf16[64,2304]{1,0:T(8,128)(2,1)S(1)}, bf16[64,2304]{1,0:T(8,128)(2,1)S(1)}, u32[]{:S(2)}, u32[]{:S(2)}) %collective-permute-start.11) | collective-permute-done | bytes 294944 | tf_op jit(solution)/shard_map/ppermute | solution.py:59
  49.1 1.4 %collective-permute-done.10 = bf16[64,2304]{1,0:T(8,128)(2,1)S(1)} collective-permute-done((bf16[64,2304]{1,0:T(8,128)(2,1)S(1)}, bf16[64,2304]{1,0:T(8,128)(2,1)S(1)}, u32[]{:S(2)}, u32[]{:S(2)}) %collective-permute-start.10) | collective-permute-done | bytes 294944 | tf_op jit(solution)/shard_map/ppermute | solution.py:59
  50.5 2.4 %collective-permute-done.7 = bf16[64,2304]{1,0:T(8,128)(2,1)S(1)} collective-permute-done((bf16[64,2304]{1,0:T(8,128)(2,1)S(1)}, bf16[64,2304]{1,0:T(8,128)(2,1)S(1)}, u32[]{:S(2)}, u32[]{:S(2)}) %collective-permute-start.7) | collective-permute-done | bytes 294944 | tf_op jit(solution)/shard_map/ppermute | solution.py:59
  52.9 0.2 add_convert_fusion.2
  53.1 0.0 copy-start
  53.2 0.0 copy-start.1
  53.2 0.0 copy-start.2
  53.2 0.0 copy-start.3
  53.2 21.2 %all_to_all.10 = bf16[8,16,2304]{2,1,0:T(8,128)(2,1)S(1)} all-to-all(bf16[8,16,2304]{2,1,0:T(8,128)(2,1)S(1)} %bitcast.15), channel_id=1, replica_groups=mesh['zl'=2,'x'=4,'y'=4,'zh'=4,'c'=2] {'zl','zh'}, dimensions={0} | all-to-all | bytes 1179648 | tf_op jit(solution)/shard_map/all_to_all | solution.py:405
  74.3 0.1 convert_reduce_fusion
  74.5 0.9 subtract_convert_fusion
  75.4 16.3 %all_to_all.11 = bf16[8,16,2304]{2,1,0:T(8,128)(2,1)S(1)} all-to-all(bf16[8,16,2304]{2,1,0:T(8,128)(2,1)S(1)} %broadcast_in_dim.11), channel_id=1, replica_groups=mesh['zl'=2,'x'=4,'y'=4,'zh'=4,'c'=2] {'zl','zh'}, dimensions={0} | all-to-all | bytes 1179648 | tf_op jit(solution)/shard_map/all_to_all | solution.py:417
  91.7 0.1 collective-permute-start.14
  91.8 2.7 %collective-permute-start.13 = (bf16[64,2304]{1,0:T(8,128)(2,1)S(1)}, bf16[64,2304]{1,0:T(8,128)(2,1)S(1)}, u32[]{:S(2)}, u32[]{:S(2)}) collective-permute-start(bf16[64,2304]{1,0:T(8,128)(2,1)S(1)} %bitcast.8), channel_id=1, source_target_pairs={{0,24},{1,97},{2,26},{3,99},{4,28},{5,101},{6,30},{7,103},{8,0},{9... | collective-permute-start | bytes 884744 | tf_op jit(solution)/shard_map/ppermute | solution.py:59
  94.5 0.0 collective-permute-start.12
  94.5 1.4 %collective-permute-start.15 = (bf16[64,2304]{1,0:T(8,128)(2,1)S(1)}, bf16[64,2304]{1,0:T(8,128)(2,1)S(1)}, u32[]{:S(2)}, u32[]{:S(2)}) collective-permute-start(bf16[64,2304]{1,0:T(8,128)(2,1)S(1)} %bitcast.9), channel_id=1, source_target_pairs={{0,8},{1,33},{2,10},{3,35},{4,12},{5,37},{6,14},{7,39},{8,16},{9,4... | collective-permute-start | bytes 884744 | tf_op jit(solution)/shard_map/ppermute | solution.py:59
  95.9 2.6 %collective-permute-done.14.refs_10_ = bf16[64,2304]{1,0:T(8,128)(2,1)S(1)} collective-permute-done((bf16[64,2304]{1,0:T(8,128)(2,1)S(1)}, bf16[64,2304]{1,0:T(8,128)(2,1)S(1)}, u32[]{:S(2)}, u32[]{:S(2)}) %collective-permute-start.14) | collective-permute-done | bytes 294944 | tf_op jit(solution)/shard_map/ppermute | solution.py:59
  98.6 0.0 collective-permute-start.16
  98.6 0.0 collective-permute-done.13.refs_9_
  98.6 2.7 %collective-permute-start.17 = (bf16[64,2304]{1,0:T(8,128)(2,1)S(1)}, bf16[64,2304]{1,0:T(8,128)(2,1)S(1)}, u32[]{:S(2)}, u32[]{:S(2)}) collective-permute-start(bf16[64,2304]{1,0:T(8,128)(2,1)S(1)} %collective-permute-done.13.refs_9_), channel_id=1, source_target_pairs={{0,24},{1,97},{2,26},{3,99},{4,28},{5,101},{6,30},{7,103},{8,0},{9... | collective-permute-start | bytes 884744 | tf_op jit(solution)/shard_map/ppermute | solution.py:59
  101.3 1.9 %values.2.own_ref = f32[1024,128]{1,0:T(8,128)S(1)} custom-call(s32[3]{0:T(128)S(1)} %pad_add_fusion.refs_0_.place_ref, bf16[1408,256]{1,0:T(8,128)(2,1)S(1)} %get-tuple-element.22.refs_0_.refs_4_, bf16[1408,256]{1,0:T(8,128)(2,1)S(1)} %get-tuple-element.23.refs_1_.refs_5_, bf16[1664,256]{1,0:T(8,128)(2,1)S(1)} %collective-permute-done.refs_2_.refs_0_, ...), custom_call_target="tpu_custom_call" | custom-call | flops 603979776 | bytes 9437184 | tf_op jit(solution)/shard_map/values/pallas_call | solution.py:264
  103.2 0.0 collective-permute-done.12.refs_8_
  103.2 2.0 %values.3.side_ref = f32[1024,256]{1,0:T(8,128)S(1)} custom-call(s32[3]{0:T(128)S(1)} %pad_add_fusion.refs_0_.place_ref, bf16[1408,256]{1,0:T(8,128)(2,1)S(1)} %get-tuple-element.22.refs_0_.refs_4_, bf16[1408,256]{1,0:T(8,128)(2,1)S(1)} %get-tuple-element.23.refs_1_.refs_5_, bf16[1664,256]{1,0:T(8,128)(2,1)S(1)} %collective-permute-done.refs_2_.refs_0_, ...), custom_call_target="tpu_custom_call" | custom-call | flops 1207959552 | bytes 9437184 | tf_op jit(solution)/shard_map/values/pallas_call | solution.py:264
  105.2 0.2 collective-permute-done.16.refs_6_.refs_2_
  105.4 1.2 value_parts.3
  106.5 0.0 copy-start.4
  106.5 5.6 %collective-permute-start.19 = (bf16[256,512]{1,0:T(8,128)(2,1)S(1)}, bf16[256,512]{1,0:T(8,128)(2,1)S(1)}, u32[]{:S(2)}, u32[]{:S(2)}) collective-permute-start(bf16[256,512]{1,0:T(8,128)(2,1)S(1)} %value_parts.3), channel_id=1, source_target_pairs={{0,64},{1,17},{2,66},{3,19},{4,68},{5,21},{6,70},{7,23},{8,72},{9,... | collective-permute-start | bytes 786440 | tf_op jit(solution)/shard_map/ppermute | solution.py:59
  112.1 1.8 %value_parts.2 = (bf16[256,512]{1,0:T(8,128)(2,1)S(1)}, bf16[256,512]{1,0:T(8,128)(2,1)S(1)}, f32[256,256]{1,0:T(8,128)S(1)}, bf16[256,256]{1,0:T(8,128)(2,1)S(1)}) custom-call(s32[3]{0:T(128)S(1)} %pad_add_fusion.refs_0_.place_ref, f32[1024,128]{1,0:T(8,128)S(1)} %values.2.own_ref, f32[1024,256]{1,0:T(8,128)S(1)} %values.3.side_ref, ...), custom_call_target="tpu_custom_call" | custom-call | flops 452984832 | bytes 2359296 | tf_op jit(solution)/shard_map/value_parts/pallas_call | solution.py:319
  114.0 2.5 %collective-permute-start.18 = (bf16[256,512]{1,0:T(8,128)(2,1)S(1)}, bf16[256,512]{1,0:T(8,128)(2,1)S(1)}, u32[]{:S(2)}, u32[]{:S(2)}) collective-permute-start(bf16[256,512]{1,0:T(8,128)(2,1)S(1)} %get-tuple-element.34), channel_id=1, source_target_pairs={{0,96},{1,25},{2,98},{3,27},{4,100},{5,29},{6,102},{7,31},{8,104},... | collective-permute-start | bytes 786440 | tf_op jit(solution)/shard_map/ppermute | solution.py:59
  116.5 0.7 collective-permute-start.20
  117.1 1.7 %collective-permute-done.19.refs_2_ = bf16[256,512]{1,0:T(8,128)(2,1)S(1)} collective-permute-done((bf16[256,512]{1,0:T(8,128)(2,1)S(1)}, bf16[256,512]{1,0:T(8,128)(2,1)S(1)}, u32[]{:S(2)}, u32[]{:S(2)}) %collective-permute-start.19) | collective-permute-done | bytes 262176 | tf_op jit(solution)/shard_map/ppermute | solution.py:59
  118.8 11.8 %collective-permute-start.23 = (bf16[256,512]{1,0:T(8,128)(2,1)S(1)}, bf16[256,512]{1,0:T(8,128)(2,1)S(1)}, u32[]{:S(2)}, u32[]{:S(2)}) collective-permute-start(bf16[256,512]{1,0:T(8,128)(2,1)S(1)} %collective-permute-done.19.refs_2_), channel_id=1, source_target_pairs={{0,1},{1,0},{2,3},{3,2},{4,5},{5,4},{6,7},{7,6},{8,9},{9,8},{10,11... | collective-permute-start | bytes 786440 | tf_op jit(solution)/shard_map/ppermute | solution.py:59
  130.6 0.4 collective-permute-start.22
  131.0 2.4 %collective-permute-start.24 = (bf16[256,512]{1,0:T(8,128)(2,1)S(1)}, bf16[256,512]{1,0:T(8,128)(2,1)S(1)}, u32[]{:S(2)}, u32[]{:S(2)}) collective-permute-start(bf16[256,512]{1,0:T(8,128)(2,1)S(1)} %collective-permute-done.20.refs_3_), channel_id=1, source_target_pairs={{0,1},{1,0},{2,3},{3,2},{4,5},{5,4},{6,7},{7,6},{8,9},{9,8},{10,11... | collective-permute-start | bytes 786440 | tf_op jit(solution)/shard_map/ppermute | solution.py:59
  133.3 0.0 collective-permute-start.21
  133.4 0.1 copy.14.flag_ref
  133.5 1.2 collective-permute-done.21.refs_4_
  134.7 2.0 %joined.1 = f32[256,1024]{1,0:T(8,128)} custom-call(s32[3]{0:T(128)S(1)} %pad_add_fusion.refs_0_.place_ref, s32[256,1]{1,0:T(8,128)S(1)} %copy.14.flag_ref, f32[256,256]{1,0:T(8,128)S(1)} %get-tuple-element.33.refs_0_, bf16[256,512]{1,0:T(8,128)(2,1)S(1)} %collective-permute-done.18.refs_1_, bf16[256,512]{1,0:T(8,128)(2,1)S(1)} %collective-permute-done.19.refs_2_, ...), custom_call_target="tpu_custom_call" | custom-call | tf_op jit(solution)/shard_map/joined/pallas_call | solution.py:352
  (18 shorter events, 0.2 us)
Async XLA Ops:
  5.3 12.6 %collective-permute-start.2 = (bf16[1408,256]{1,0:T(8,128)(2,1)S(1)}, bf16[1408,256]{1,0:T(8,128)(2,1)S(1)}, u32[]{:S(2)}, u32[]{:S(2)}) collective-permute-start(bf16[1408,256]{1,0:T(8,128)(2,1)S(1)} %get-tuple-element.22.refs_0_.refs_4_), channel_id=1, source_target_pairs={{0,32},{1,9},{2,34},{3,11},{4,36},{5,13},{6,38},{7,15},{8,40},{9,1... | collective-permute-start | bytes 2162696 | tf_op jit(solution)/shard_map/ppermute | solution.py:59
  7.5 10.4 %collective-permute-start.1 = (bf16[1408,256]{1,0:T(8,128)(2,1)S(1)}, bf16[1408,256]{1,0:T(8,128)(2,1)S(1)}, u32[]{:S(2)}, u32[]{:S(2)}) collective-permute-start(bf16[1408,256]{1,0:T(8,128)(2,1)S(1)} %get-tuple-element.23.refs_1_.refs_5_), channel_id=1, source_target_pairs={{0,96},{1,25},{2,98},{3,27},{4,100},{5,29},{6,102},{7,31},{8,104},... | collective-permute-start | bytes 2162696 | tf_op jit(solution)/shard_map/ppermute | solution.py:59
  9.0 18.0 %collective-permute-start = (bf16[1664,256]{1,0:T(8,128)(2,1)S(1)}, bf16[1664,256]{1,0:T(8,128)(2,1)S(1)}, u32[]{:S(2)}, u32[]{:S(2)}) collective-permute-start(bf16[1664,256]{1,0:T(8,128)(2,1)S(1)} %get-tuple-element.24), channel_id=1, source_target_pairs={{0,96},{1,25},{2,98},{3,27},{4,100},{5,29},{6,102},{7,31},{8,104},... | collective-permute-start | bytes 2555912 | tf_op jit(solution)/shard_map/ppermute | solution.py:59
  10.4 16.7 %collective-permute-start.3 = (bf16[1664,256]{1,0:T(8,128)(2,1)S(1)}, bf16[1664,256]{1,0:T(8,128)(2,1)S(1)}, u32[]{:S(2)}, u32[]{:S(2)}) collective-permute-start(bf16[1664,256]{1,0:T(8,128)(2,1)S(1)} %get-tuple-element.25), channel_id=1, source_target_pairs={{0,32},{1,9},{2,34},{3,11},{4,36},{5,13},{6,38},{7,15},{8,40},{9,1... | collective-permute-start | bytes 2555912 | tf_op jit(solution)/shard_map/ppermute | solution.py:59
  17.9 16.9 %collective-permute-start.4 = (bf16[1408,256]{1,0:T(8,128)(2,1)S(1)}, bf16[1408,256]{1,0:T(8,128)(2,1)S(1)}, u32[]{:S(2)}, u32[]{:S(2)}) collective-permute-start(bf16[1408,256]{1,0:T(8,128)(2,1)S(1)} %collective-permute-done.2.refs_4_.refs_2_), channel_id=1, source_target_pairs={{0,32},{1,9},{2,34},{3,11},{4,36},{5,13},{6,38},{7,15},{8,40},{9,1... | collective-permute-start | bytes 2162696 | tf_op jit(solution)/shard_map/ppermute | solution.py:59
  17.9 16.8 %collective-permute-start.5 = (bf16[1408,256]{1,0:T(8,128)(2,1)S(1)}, bf16[1408,256]{1,0:T(8,128)(2,1)S(1)}, u32[]{:S(2)}, u32[]{:S(2)}) collective-permute-start(bf16[1408,256]{1,0:T(8,128)(2,1)S(1)} %collective-permute-done.1.refs_3_.refs_1_), channel_id=1, source_target_pairs={{0,96},{1,25},{2,98},{3,27},{4,100},{5,29},{6,102},{7,31},{8,104},... | collective-permute-start | bytes 2162696 | tf_op jit(solution)/shard_map/ppermute | solution.py:59
  36.3 7.4 %collective-permute-start.9 = (bf16[64,2304]{1,0:T(8,128)(2,1)S(1)}, bf16[64,2304]{1,0:T(8,128)(2,1)S(1)}, u32[]{:S(2)}, u32[]{:S(2)}) collective-permute-start(bf16[64,2304]{1,0:T(8,128)(2,1)S(1)} %get-tuple-element.31), channel_id=1, source_target_pairs={{0,24},{1,97},{2,26},{3,99},{4,28},{5,101},{6,30},{7,103},{8,0},{9... | collective-permute-start | bytes 884744 | tf_op jit(solution)/shard_map/ppermute | solution.py:59
  38.9 7.1 %collective-permute-start.6 = (bf16[64,2304]{1,0:T(8,128)(2,1)S(1)}, bf16[64,2304]{1,0:T(8,128)(2,1)S(1)}, u32[]{:S(2)}, u32[]{:S(2)}) collective-permute-start(bf16[64,2304]{1,0:T(8,128)(2,1)S(1)} %get-tuple-element.28), channel_id=1, source_target_pairs={{0,8},{1,33},{2,10},{3,35},{4,12},{5,37},{6,14},{7,39},{8,16},{9,4... | collective-permute-start | bytes 884744 | tf_op jit(solution)/shard_map/ppermute | solution.py:59
  40.8 8.3 %collective-permute-start.11 = (bf16[64,2304]{1,0:T(8,128)(2,1)S(1)}, bf16[64,2304]{1,0:T(8,128)(2,1)S(1)}, u32[]{:S(2)}, u32[]{:S(2)}) collective-permute-start(bf16[64,2304]{1,0:T(8,128)(2,1)S(1)} %get-tuple-element.32), channel_id=1, source_target_pairs={{0,8},{1,33},{2,10},{3,35},{4,12},{5,37},{6,14},{7,39},{8,16},{9,4... | collective-permute-start | bytes 884744 | tf_op jit(solution)/shard_map/ppermute | solution.py:59
  41.1 8.0 %collective-permute-start.8 = (bf16[64,2304]{1,0:T(8,128)(2,1)S(1)}, bf16[64,2304]{1,0:T(8,128)(2,1)S(1)}, u32[]{:S(2)}, u32[]{:S(2)}) collective-permute-start(bf16[64,2304]{1,0:T(8,128)(2,1)S(1)} %get-tuple-element.29), channel_id=1, source_target_pairs={{0,24},{1,97},{2,26},{3,99},{4,28},{5,101},{6,30},{7,103},{8,0},{9... | collective-permute-start | bytes 884744 | tf_op jit(solution)/shard_map/ppermute | solution.py:59
  43.8 6.7 %collective-permute-start.10 = (bf16[64,2304]{1,0:T(8,128)(2,1)S(1)}, bf16[64,2304]{1,0:T(8,128)(2,1)S(1)}, u32[]{:S(2)}, u32[]{:S(2)}) collective-permute-start(bf16[64,2304]{1,0:T(8,128)(2,1)S(1)} %add_convert_fusion.1), channel_id=1, source_target_pairs={{0,24},{1,97},{2,26},{3,99},{4,28},{5,101},{6,30},{7,103},{8,0},{9... | collective-permute-start | bytes 884744 | tf_op jit(solution)/shard_map/ppermute | solution.py:59
  46.0 6.9 %collective-permute-start.7 = (bf16[64,2304]{1,0:T(8,128)(2,1)S(1)}, bf16[64,2304]{1,0:T(8,128)(2,1)S(1)}, u32[]{:S(2)}, u32[]{:S(2)}) collective-permute-start(bf16[64,2304]{1,0:T(8,128)(2,1)S(1)} %add_convert_fusion.3), channel_id=1, source_target_pairs={{0,8},{1,33},{2,10},{3,35},{4,12},{5,37},{6,14},{7,39},{8,16},{9,4... | collective-permute-start | bytes 884744 | tf_op jit(solution)/shard_map/ppermute | solution.py:59
  53.1 21.3 %copy-start = (f32[16,2304]{1,0:T(8,128)S(1)}, f32[16,2304]{1,0:T(8,128)}, u32[]{:S(2)}) copy-start(f32[16,2304]{1,0:T(8,128)} %param.17) | copy-start | bytes 442372
  53.2 21.3 %copy-start.1 = (f32[16,2304]{1,0:T(8,128)S(1)}, f32[16,2304]{1,0:T(8,128)}, u32[]{:S(2)}) copy-start(f32[16,2304]{1,0:T(8,128)} %param.14) | copy-start | bytes 442372
  53.2 21.3 %copy-start.2 = (f32[16,2304]{1,0:T(8,128)S(1)}, f32[16,2304]{1,0:T(8,128)}, u32[]{:S(2)}) copy-start(f32[16,2304]{1,0:T(8,128)} %param.15) | copy-start | bytes 442372
  53.2 21.3 %copy-start.3 = (f32[16,2304]{1,0:T(8,128)S(1)}, f32[16,2304]{1,0:T(8,128)}, u32[]{:S(2)}) copy-start(f32[16,2304]{1,0:T(8,128)} %param.16) | copy-start | bytes 442372
  91.7 6.9 %collective-permute-start.14 = (bf16[64,2304]{1,0:T(8,128)(2,1)S(1)}, bf16[64,2304]{1,0:T(8,128)(2,1)S(1)}, u32[]{:S(2)}, u32[]{:S(2)}) collective-permute-start(bf16[64,2304]{1,0:T(8,128)(2,1)S(1)} %bitcast.11), channel_id=1, source_target_pairs={{0,8},{1,33},{2,10},{3,35},{4,12},{5,37},{6,14},{7,39},{8,16},{9,4... | collective-permute-start | bytes 884744 | tf_op jit(solution)/shard_map/ppermute | solution.py:59
  91.8 6.8 %collective-permute-start.13 = (bf16[64,2304]{1,0:T(8,128)(2,1)S(1)}, bf16[64,2304]{1,0:T(8,128)(2,1)S(1)}, u32[]{:S(2)}, u32[]{:S(2)}) collective-permute-start(bf16[64,2304]{1,0:T(8,128)(2,1)S(1)} %bitcast.8), channel_id=1, source_target_pairs={{0,24},{1,97},{2,26},{3,99},{4,28},{5,101},{6,30},{7,103},{8,0},{9... | collective-permute-start | bytes 884744 | tf_op jit(solution)/shard_map/ppermute | solution.py:59
  94.5 8.7 %collective-permute-start.12 = (bf16[64,2304]{1,0:T(8,128)(2,1)S(1)}, bf16[64,2304]{1,0:T(8,128)(2,1)S(1)}, u32[]{:S(2)}, u32[]{:S(2)}) collective-permute-start(bf16[64,2304]{1,0:T(8,128)(2,1)S(1)} %bitcast.12), channel_id=1, source_target_pairs={{0,24},{1,97},{2,26},{3,99},{4,28},{5,101},{6,30},{7,103},{8,0},{9... | collective-permute-start | bytes 884744 | tf_op jit(solution)/shard_map/ppermute | solution.py:59
  94.5 8.7 %collective-permute-start.15 = (bf16[64,2304]{1,0:T(8,128)(2,1)S(1)}, bf16[64,2304]{1,0:T(8,128)(2,1)S(1)}, u32[]{:S(2)}, u32[]{:S(2)}) collective-permute-start(bf16[64,2304]{1,0:T(8,128)(2,1)S(1)} %bitcast.9), channel_id=1, source_target_pairs={{0,8},{1,33},{2,10},{3,35},{4,12},{5,37},{6,14},{7,39},{8,16},{9,4... | collective-permute-start | bytes 884744 | tf_op jit(solution)/shard_map/ppermute | solution.py:59
  98.6 6.8 %collective-permute-start.16 = (bf16[64,2304]{1,0:T(8,128)(2,1)S(1)}, bf16[64,2304]{1,0:T(8,128)(2,1)S(1)}, u32[]{:S(2)}, u32[]{:S(2)}) collective-permute-start(bf16[64,2304]{1,0:T(8,128)(2,1)S(1)} %collective-permute-done.14.refs_10_), channel_id=1, source_target_pairs={{0,8},{1,33},{2,10},{3,35},{4,12},{5,37},{6,14},{7,39},{8,16},{9,4... | collective-permute-start | bytes 884744 | tf_op jit(solution)/shard_map/ppermute | solution.py:59
  98.6 6.8 %collective-permute-start.17 = (bf16[64,2304]{1,0:T(8,128)(2,1)S(1)}, bf16[64,2304]{1,0:T(8,128)(2,1)S(1)}, u32[]{:S(2)}, u32[]{:S(2)}) collective-permute-start(bf16[64,2304]{1,0:T(8,128)(2,1)S(1)} %collective-permute-done.13.refs_9_), channel_id=1, source_target_pairs={{0,24},{1,97},{2,26},{3,99},{4,28},{5,101},{6,30},{7,103},{8,0},{9... | collective-permute-start | bytes 884744 | tf_op jit(solution)/shard_map/ppermute | solution.py:59
  106.5 26.8 %copy-start.4 = (s32[256]{0:T(256)S(1)}, s32[256]{0:T(256)}, u32[]{:S(2)}) copy-start(s32[256]{0:T(256)} %param.12) | copy-start | bytes 3076
  106.5 12.2 %collective-permute-start.19 = (bf16[256,512]{1,0:T(8,128)(2,1)S(1)}, bf16[256,512]{1,0:T(8,128)(2,1)S(1)}, u32[]{:S(2)}, u32[]{:S(2)}) collective-permute-start(bf16[256,512]{1,0:T(8,128)(2,1)S(1)} %value_parts.3), channel_id=1, source_target_pairs={{0,64},{1,17},{2,66},{3,19},{4,68},{5,21},{6,70},{7,23},{8,72},{9,... | collective-permute-start | bytes 786440 | tf_op jit(solution)/shard_map/ppermute | solution.py:59
  114.0 16.6 %collective-permute-start.18 = (bf16[256,512]{1,0:T(8,128)(2,1)S(1)}, bf16[256,512]{1,0:T(8,128)(2,1)S(1)}, u32[]{:S(2)}, u32[]{:S(2)}) collective-permute-start(bf16[256,512]{1,0:T(8,128)(2,1)S(1)} %get-tuple-element.34), channel_id=1, source_target_pairs={{0,96},{1,25},{2,98},{3,27},{4,100},{5,29},{6,102},{7,31},{8,104},... | collective-permute-start | bytes 786440 | tf_op jit(solution)/shard_map/ppermute | solution.py:59
  116.5 14.5 %collective-permute-start.20 = (bf16[256,512]{1,0:T(8,128)(2,1)S(1)}, bf16[256,512]{1,0:T(8,128)(2,1)S(1)}, u32[]{:S(2)}, u32[]{:S(2)}) collective-permute-start(bf16[256,512]{1,0:T(8,128)(2,1)S(1)} %get-tuple-element.35), channel_id=1, source_target_pairs={{0,32},{1,9},{2,34},{3,11},{4,36},{5,13},{6,38},{7,15},{8,40},{9,1... | collective-permute-start | bytes 786440 | tf_op jit(solution)/shard_map/ppermute | solution.py:59
  118.8 15.9 %collective-permute-start.23 = (bf16[256,512]{1,0:T(8,128)(2,1)S(1)}, bf16[256,512]{1,0:T(8,128)(2,1)S(1)}, u32[]{:S(2)}, u32[]{:S(2)}) collective-permute-start(bf16[256,512]{1,0:T(8,128)(2,1)S(1)} %collective-permute-done.19.refs_2_), channel_id=1, source_target_pairs={{0,1},{1,0},{2,3},{3,2},{4,5},{5,4},{6,7},{7,6},{8,9},{9,8},{10,11... | collective-permute-start | bytes 786440 | tf_op jit(solution)/shard_map/ppermute | solution.py:59
  130.6 4.1 %collective-permute-start.22 = (bf16[256,512]{1,0:T(8,128)(2,1)S(1)}, bf16[256,512]{1,0:T(8,128)(2,1)S(1)}, u32[]{:S(2)}, u32[]{:S(2)}) collective-permute-start(bf16[256,512]{1,0:T(8,128)(2,1)S(1)} %collective-permute-done.18.refs_1_), channel_id=1, source_target_pairs={{0,1},{1,0},{2,3},{3,2},{4,5},{5,4},{6,7},{7,6},{8,9},{9,8},{10,11... | collective-permute-start | bytes 786440 | tf_op jit(solution)/shard_map/ppermute | solution.py:59
  131.0 3.7 %collective-permute-start.24 = (bf16[256,512]{1,0:T(8,128)(2,1)S(1)}, bf16[256,512]{1,0:T(8,128)(2,1)S(1)}, u32[]{:S(2)}, u32[]{:S(2)}) collective-permute-start(bf16[256,512]{1,0:T(8,128)(2,1)S(1)} %collective-permute-done.20.refs_3_), channel_id=1, source_target_pairs={{0,1},{1,0},{2,3},{3,2},{4,5},{5,4},{6,7},{7,6},{8,9},{9,8},{10,11... | collective-permute-start | bytes 786440 | tf_op jit(solution)/shard_map/ppermute | solution.py:59
  133.3 1.3 collective-permute-start.21

commit v4 on v3

--- a/solution.py
+++ b/solution.py
@@ -427,9 +427,8 @@
     side = values(place, halves, (right_ga, right_gb, left_ga, left_gb))
     known = (place, first, side, halves, (far_ga, far_gb))
 
-    (out_far,) = value_parts((3,), *known)
+    out_far, out_right, out_left, mine, over = value_parts((3, 1, 2, 0), *known)
     from_far = send(out_far, first_ring(2))
-    out_right, out_left, mine, over = value_parts((1, 2, 0), *known)
     from_left = send(out_right, up)
     from_right = send(out_left, down)
     got = (from_right, from_far, from_left)

time: 137 us -> 135 us (0.985)
  starting transfers between devices: 45.7 us -> 39.7 us
  waiting for transfers between devices: 30.8 us -> 35.3 us
    ppermute x25, starting transfers between devices: 45.7 us -> 39.7 us  [send(): return lax.ppermute(array, AXES, perm)]
    ppermute x25, waiting for transfers between devices: 30.8 us -> 35.3 us  [send(): return lax.ppermute(array, AXES, perm)]
    pallas_call x2 -> x1, Pallas kernels: 3 us -> 2.18 us  [value_parts(): pl.pallas_call(functools.partial(last_kernel, devices), in_specs=scalars(...]
  transfers between devices with their start and end apart: 25 -> 25, of which waited for: 11 -> 11; matrix products, arithmetic and copies ran while one was open for 0% -> 0% of each run, Pallas kernels for 8% -> 7%
where the time goes in v4:
time: 135 us
  starting transfers between devices  39.7 us (29%)
  blocking collectives  37.4 us (28%)
  waiting for transfers between devices  35.3 us (26%)
  Pallas kernels  18.9 us (14%)
  other arithmetic  2.1 us (2%)
    ppermute x25, starting transfers between devices, send(): return lax.ppermute(array, AXES, perm)  39.7 us
    ppermute x25, waiting for transfers between devices, send(): return lax.ppermute(array, AXES, perm)  35.3 us
    all_to_all x1, blocking collectives, body(): lax.all_to_all(ring_sum.reshape(8, 16, width), ('zl', 'zh'), 0, 0, tiled=...  21.2 us
    all_to_all x1, blocking collectives, body(): column = lax.all_to_all(copies, ('zl', 'zh'), 0, 0, tiled=True)  16.3 us
    pallas_call x1, Pallas kernels, shared(): pl.pallas_call(share_kernel, in_specs=scalars() + in_vmem(1) + [hbm] * 3,...  3.89 us
    pallas_call x2, Pallas kernels, values(): pl.pallas_call(functools.partial(values_kernel, groups), in_specs=scalars...  3.88 us
    pallas_call x2, Pallas kernels, grad_parts(): pl.pallas_call(functools.partial(far_kernel, starts), in_specs=in_vmem(3)...  3.45 us
    pallas_call x1, Pallas kernels, near_grad(): pl.pallas_call(near_kernel, in_specs=in_vmem(7), out_specs=in_vmem(1)[0],...  3.42 us
  transfers between devices with their start and end apart: 25, of which 11 were waited for; matrix products, arithmetic and copies ran while one was open for 0% of the time, Pallas kernels for 7%

profile of v4, /device:TPU:1, one launch (start us, length us, event | category | flops | bytes accessed | tf_op | source)
XLA Modules:
  0.0 134.5 jit_solution(16362672005793328733)
XLA Ops:
  0.6 0.7 compare_select_fusion
  1.3 0.1 pad_add_fusion.refs_0_.place_ref
  1.4 3.9 %shared.1 = (bf16[1408,256]{1,0:T(8,128)(2,1)S(1)}, bf16[1408,256]{1,0:T(8,128)(2,1)S(1)}, bf16[1664,256]{1,0:T(8,128)(2,1)S(1)}, bf16[1664,256]{1,0:T(8,128)(2,1)S(1)}, bf16[512,256]{1,0:T(8,128)(2,1)S(1)}) custom-call(s32[3]{0:T(128)S(1)} %pad_add_fusion.refs_0_.place_ref, s32[1,256]{1,0:T(1,128)S(1)} %bitcast.14, bf16[512,2304]{1,0:T(8,128)(2,1)} %refs_2_.1, ...), custom_call_target="tpu_custom_call" | custom-call | flops 905969664 | bytes 4718592 | tf_op jit(solution)/shard_map/shared/pallas_call | solution.py:155
  5.3 2.2 %collective-permute-start.2 = (bf16[1408,256]{1,0:T(8,128)(2,1)S(1)}, bf16[1408,256]{1,0:T(8,128)(2,1)S(1)}, u32[]{:S(2)}, u32[]{:S(2)}) collective-permute-start(bf16[1408,256]{1,0:T(8,128)(2,1)S(1)} %get-tuple-element.23.refs_0_.refs_6_), channel_id=1, source_target_pairs={{0,32},{1,9},{2,34},{3,11},{4,36},{5,13},{6,38},{7,15},{8,40},{9,1... | collective-permute-start | bytes 2162696 | tf_op jit(solution)/shard_map/ppermute | solution.py:59
  7.5 1.5 %collective-permute-start.1 = (bf16[1408,256]{1,0:T(8,128)(2,1)S(1)}, bf16[1408,256]{1,0:T(8,128)(2,1)S(1)}, u32[]{:S(2)}, u32[]{:S(2)}) collective-permute-start(bf16[1408,256]{1,0:T(8,128)(2,1)S(1)} %get-tuple-element.24.refs_1_.refs_7_), channel_id=1, source_target_pairs={{0,96},{1,25},{2,98},{3,27},{4,100},{5,29},{6,102},{7,31},{8,104},... | collective-permute-start | bytes 2162696 | tf_op jit(solution)/shard_map/ppermute | solution.py:59
  9.0 1.4 %collective-permute-start = (bf16[1664,256]{1,0:T(8,128)(2,1)S(1)}, bf16[1664,256]{1,0:T(8,128)(2,1)S(1)}, u32[]{:S(2)}, u32[]{:S(2)}) collective-permute-start(bf16[1664,256]{1,0:T(8,128)(2,1)S(1)} %get-tuple-element.25), channel_id=1, source_target_pairs={{0,96},{1,25},{2,98},{3,27},{4,100},{5,29},{6,102},{7,31},{8,104},... | collective-permute-start | bytes 2555912 | tf_op jit(solution)/shard_map/ppermute | solution.py:59
  10.4 0.1 collective-permute-start.3
  10.5 7.4 %collective-permute-done.2.refs_4_ = bf16[1408,256]{1,0:T(8,128)(2,1)S(1)} collective-permute-done((bf16[1408,256]{1,0:T(8,128)(2,1)S(1)}, bf16[1408,256]{1,0:T(8,128)(2,1)S(1)}, u32[]{:S(2)}, u32[]{:S(2)}) %collective-permute-start.2) | collective-permute-done | bytes 720928 | tf_op jit(solution)/shard_map/ppermute | solution.py:59
  17.9 0.0 collective-permute-start.4
  17.9 0.0 collective-permute-done.1.refs_3_
  17.9 2.7 %collective-permute-start.5 = (bf16[1408,256]{1,0:T(8,128)(2,1)S(1)}, bf16[1408,256]{1,0:T(8,128)(2,1)S(1)}, u32[]{:S(2)}, u32[]{:S(2)}) collective-permute-start(bf16[1408,256]{1,0:T(8,128)(2,1)S(1)} %collective-permute-done.1.refs_3_), channel_id=1, source_target_pairs={{0,96},{1,25},{2,98},{3,27},{4,100},{5,29},{6,102},{7,31},{8,104},... | collective-permute-start | bytes 2162696 | tf_op jit(solution)/shard_map/ppermute | solution.py:59
  20.7 6.4 %collective-permute-done.refs_2_ = bf16[1664,256]{1,0:T(8,128)(2,1)S(1)} collective-permute-done((bf16[1664,256]{1,0:T(8,128)(2,1)S(1)}, bf16[1664,256]{1,0:T(8,128)(2,1)S(1)}, u32[]{:S(2)}, u32[]{:S(2)}) %collective-permute-start) | collective-permute-done | bytes 852000 | tf_op jit(solution)/shard_map/ppermute | solution.py:59
  27.1 0.0 collective-permute-done.3.refs_5_
  27.1 3.4 %near_grad.1.near_ref = f32[512,2304]{1,0:T(8,128)S(1)} custom-call(bf16[512,256]{1,0:T(8,128)(2,1)S(1)} %get-tuple-element.22.own_ref, bf16[1408,256]{1,0:T(8,128)(2,1)S(1)} %get-tuple-element.23.refs_0_.refs_6_, bf16[1408,256]{1,0:T(8,128)(2,1)S(1)} %get-tuple-element.24.refs_1_.refs_7_, bf16[1664,256]{1,0:T(8,128)(2,1)S(1)} %collective-permute-done.refs_2_, ...), custom_call_target="tpu_custom_call" | custom-call | flops 1811939328 | bytes 9437184 | tf_op jit(solution)/shard_map/near_grad/pallas_call | solution.py:199
  30.5 4.3 %collective-permute-done.4.a_ref.refs_6_.refs_0_ = bf16[1408,256]{1,0:T(8,128)(2,1)S(1)} collective-permute-done((bf16[1408,256]{1,0:T(8,128)(2,1)S(1)}, bf16[1408,256]{1,0:T(8,128)(2,1)S(1)}, u32[]{:S(2)}, u32[]{:S(2)}) %collective-permute-start.4) | collective-permute-done | bytes 720928 | tf_op jit(solution)/shard_map/ppermute | solution.py:59
  34.8 0.0 collective-permute-done.5.b_ref.refs_7_.refs_1_
  34.8 1.5 %grad_parts.3 = (bf16[64,2304]{1,0:T(8,128)(2,1)S(1)}, bf16[64,2304]{1,0:T(8,128)(2,1)S(1)}) custom-call(f32[512,2304]{1,0:T(8,128)S(1)} %near_grad.1.near_ref, bf16[1408,256]{1,0:T(8,128)(2,1)S(1)} %collective-permute-done.4.a_ref.refs_6_.refs_0_, bf16[1408,256]{1,0:T(8,128)(2,1)S(1)} %collective-permute-done.5.b_ref.refs_7_.refs_1_), custom_call_target="tpu_custom_call" | custom-call | flops 150994944 | bytes 4718592 | tf_op jit(solution)/shard_map/grad_parts/pallas_call | solution.py:233
  36.3 2.6 %collective-permute-start.9 = (bf16[64,2304]{1,0:T(8,128)(2,1)S(1)}, bf16[64,2304]{1,0:T(8,128)(2,1)S(1)}, u32[]{:S(2)}, u32[]{:S(2)}) collective-permute-start(bf16[64,2304]{1,0:T(8,128)(2,1)S(1)} %get-tuple-element.32), channel_id=1, source_target_pairs={{0,24},{1,97},{2,26},{3,99},{4,28},{5,101},{6,30},{7,103},{8,0},{9... | collective-permute-start | bytes 884744 | tf_op jit(solution)/shard_map/ppermute | solution.py:59
  38.9 1.9 %grad_parts.2 = (bf16[64,2304]{1,0:T(8,128)(2,1)S(1)}, bf16[64,2304]{1,0:T(8,128)(2,1)S(1)}, bf16[64,2304]{1,0:T(8,128)(2,1)S(1)}, bf16[64,2304]{1,0:T(8,128)(2,1)S(1)}, f32[128,2304]{1,0:T(8,128)S(1)}) custom-call(f32[512,2304]{1,0:T(8,128)S(1)} %near_grad.1.near_ref, bf16[1408,256]{1,0:T(8,128)(2,1)S(1)} %collective-permute-done.4.a_ref.refs_6_.refs_0_, ...), custom_call_target="tpu_custom_call" | custom-call | flops 377487360 | bytes 4718592 | tf_op jit(solution)/shard_map/grad_parts/pallas_call | solution.py:233
  40.8 0.3 collective-permute-start.11
  41.1 2.6 %collective-permute-start.8 = (bf16[64,2304]{1,0:T(8,128)(2,1)S(1)}, bf16[64,2304]{1,0:T(8,128)(2,1)S(1)}, u32[]{:S(2)}, u32[]{:S(2)}) collective-permute-start(bf16[64,2304]{1,0:T(8,128)(2,1)S(1)} %get-tuple-element.30), channel_id=1, source_target_pairs={{0,24},{1,97},{2,26},{3,99},{4,28},{5,101},{6,30},{7,103},{8,0},{9... | collective-permute-start | bytes 884744 | tf_op jit(solution)/shard_map/ppermute | solution.py:59
  43.7 0.0 collective-permute-done.9
  43.7 0.1 add_convert_fusion.1
  43.7 2.1 %collective-permute-start.10 = (bf16[64,2304]{1,0:T(8,128)(2,1)S(1)}, bf16[64,2304]{1,0:T(8,128)(2,1)S(1)}, u32[]{:S(2)}, u32[]{:S(2)}) collective-permute-start(bf16[64,2304]{1,0:T(8,128)(2,1)S(1)} %add_convert_fusion.1), channel_id=1, source_target_pairs={{0,24},{1,97},{2,26},{3,99},{4,28},{5,101},{6,30},{7,103},{8,0},{9... | collective-permute-start | bytes 884744 | tf_op jit(solution)/shard_map/ppermute | solution.py:59
  45.8 0.1 collective-permute-done.6
  46.0 0.1 add_convert_fusion.3
  46.0 0.1 collective-permute-start.7
  46.1 3.0 %collective-permute-done.11 = bf16[64,2304]{1,0:T(8,128)(2,1)S(1)} collective-permute-done((bf16[64,2304]{1,0:T(8,128)(2,1)S(1)}, bf16[64,2304]{1,0:T(8,128)(2,1)S(1)}, u32[]{:S(2)}, u32[]{:S(2)}) %collective-permute-start.11) | collective-permute-done | bytes 294944 | tf_op jit(solution)/shard_map/ppermute | solution.py:59
  49.1 0.0 collective-permute-done.8
  49.1 1.4 %collective-permute-done.10 = bf16[64,2304]{1,0:T(8,128)(2,1)S(1)} collective-permute-done((bf16[64,2304]{1,0:T(8,128)(2,1)S(1)}, bf16[64,2304]{1,0:T(8,128)(2,1)S(1)}, u32[]{:S(2)}, u32[]{:S(2)}) %collective-permute-start.10) | collective-permute-done | bytes 294944 | tf_op jit(solution)/shard_map/ppermute | solution.py:59
  50.5 2.4 %collective-permute-done.7 = bf16[64,2304]{1,0:T(8,128)(2,1)S(1)} collective-permute-done((bf16[64,2304]{1,0:T(8,128)(2,1)S(1)}, bf16[64,2304]{1,0:T(8,128)(2,1)S(1)}, u32[]{:S(2)}, u32[]{:S(2)}) %collective-permute-start.7) | collective-permute-done | bytes 294944 | tf_op jit(solution)/shard_map/ppermute | solution.py:59
  52.9 0.2 add_convert_fusion.2
  53.1 0.0 copy-start
  53.1 0.0 copy-start.1
  53.1 0.0 copy-start.2
  53.2 0.0 copy-start.3
  53.2 21.2 %all_to_all.10 = bf16[8,16,2304]{2,1,0:T(8,128)(2,1)S(1)} all-to-all(bf16[8,16,2304]{2,1,0:T(8,128)(2,1)S(1)} %bitcast.15), channel_id=1, replica_groups=mesh['zl'=2,'x'=4,'y'=4,'zh'=4,'c'=2] {'zl','zh'}, dimensions={0} | all-to-all | bytes 1179648 | tf_op jit(solution)/shard_map/all_to_all | solution.py:405
  74.3 0.1 convert_reduce_fusion
  74.5 0.9 subtract_convert_fusion
  75.4 16.3 %all_to_all.11 = bf16[8,16,2304]{2,1,0:T(8,128)(2,1)S(1)} all-to-all(bf16[8,16,2304]{2,1,0:T(8,128)(2,1)S(1)} %broadcast_in_dim.11), channel_id=1, replica_groups=mesh['zl'=2,'x'=4,'y'=4,'zh'=4,'c'=2] {'zl','zh'}, dimensions={0} | all-to-all | bytes 1179648 | tf_op jit(solution)/shard_map/all_to_all | solution.py:417
  91.7 0.1 collective-permute-start.14
  91.8 2.7 %collective-permute-start.13 = (bf16[64,2304]{1,0:T(8,128)(2,1)S(1)}, bf16[64,2304]{1,0:T(8,128)(2,1)S(1)}, u32[]{:S(2)}, u32[]{:S(2)}) collective-permute-start(bf16[64,2304]{1,0:T(8,128)(2,1)S(1)} %bitcast.8), channel_id=1, source_target_pairs={{0,24},{1,97},{2,26},{3,99},{4,28},{5,101},{6,30},{7,103},{8,0},{9... | collective-permute-start | bytes 884744 | tf_op jit(solution)/shard_map/ppermute | solution.py:59
  94.5 0.0 collective-permute-start.12
  94.5 1.4 %collective-permute-start.15 = (bf16[64,2304]{1,0:T(8,128)(2,1)S(1)}, bf16[64,2304]{1,0:T(8,128)(2,1)S(1)}, u32[]{:S(2)}, u32[]{:S(2)}) collective-permute-start(bf16[64,2304]{1,0:T(8,128)(2,1)S(1)} %bitcast.9), channel_id=1, source_target_pairs={{0,8},{1,33},{2,10},{3,35},{4,12},{5,37},{6,14},{7,39},{8,16},{9,4... | collective-permute-start | bytes 884744 | tf_op jit(solution)/shard_map/ppermute | solution.py:59
  95.9 2.6 %collective-permute-done.14.refs_10_ = bf16[64,2304]{1,0:T(8,128)(2,1)S(1)} collective-permute-done((bf16[64,2304]{1,0:T(8,128)(2,1)S(1)}, bf16[64,2304]{1,0:T(8,128)(2,1)S(1)}, u32[]{:S(2)}, u32[]{:S(2)}) %collective-permute-start.14) | collective-permute-done | bytes 294944 | tf_op jit(solution)/shard_map/ppermute | solution.py:59
  98.6 0.0 collective-permute-start.16
  98.6 0.0 collective-permute-done.13.refs_9_
  98.6 2.7 %collective-permute-start.17 = (bf16[64,2304]{1,0:T(8,128)(2,1)S(1)}, bf16[64,2304]{1,0:T(8,128)(2,1)S(1)}, u32[]{:S(2)}, u32[]{:S(2)}) collective-permute-start(bf16[64,2304]{1,0:T(8,128)(2,1)S(1)} %collective-permute-done.13.refs_9_), channel_id=1, source_target_pairs={{0,24},{1,97},{2,26},{3,99},{4,28},{5,101},{6,30},{7,103},{8,0},{9... | collective-permute-start | bytes 884744 | tf_op jit(solution)/shard_map/ppermute | solution.py:59
  101.2 1.9 %values.2.own_ref = f32[1024,128]{1,0:T(8,128)S(1)} custom-call(s32[3]{0:T(128)S(1)} %pad_add_fusion.refs_0_.place_ref, bf16[1408,256]{1,0:T(8,128)(2,1)S(1)} %get-tuple-element.23.refs_0_.refs_6_, bf16[1408,256]{1,0:T(8,128)(2,1)S(1)} %get-tuple-element.24.refs_1_.refs_7_, bf16[1664,256]{1,0:T(8,128)(2,1)S(1)} %collective-permute-done.refs_2_, ...), custom_call_target="tpu_custom_call" | custom-call | flops 603979776 | bytes 9437184 | tf_op jit(solution)/shard_map/values/pallas_call | solution.py:264
  103.2 2.0 %values.3.side_ref = f32[1024,256]{1,0:T(8,128)S(1)} custom-call(s32[3]{0:T(128)S(1)} %pad_add_fusion.refs_0_.place_ref, bf16[1408,256]{1,0:T(8,128)(2,1)S(1)} %get-tuple-element.23.refs_0_.refs_6_, bf16[1408,256]{1,0:T(8,128)(2,1)S(1)} %get-tuple-element.24.refs_1_.refs_7_, bf16[1664,256]{1,0:T(8,128)(2,1)S(1)} %collective-permute-done.refs_2_, ...), custom_call_target="tpu_custom_call" | custom-call | flops 1207959552 | bytes 9437184 | tf_op jit(solution)/shard_map/values/pallas_call | solution.py:264
  105.2 0.0 copy-start.4
  105.2 0.2 collective-permute-done.16.refs_8_
  105.3 0.0 collective-permute-done.17.refs_9_
  105.4 2.2 %value_parts.1 = (bf16[256,512]{1,0:T(8,128)(2,1)S(1)}, bf16[256,512]{1,0:T(8,128)(2,1)S(1)}, bf16[256,512]{1,0:T(8,128)(2,1)S(1)}, f32[256,256]{1,0:T(8,128)S(1)}, bf16[256,256]{1,0:T(8,128)(2,1)S(1)}) custom-call(s32[3]{0:T(128)S(1)} %pad_add_fusion.refs_0_.place_ref, f32[1024,128]{1,0:T(8,128)S(1)} %values.2.own_ref, f32[1024,256]{1,0:T(8,128)S(1)} %values.3.side_ref, ...), custom_call_target="tpu_custom_call" | custom-call | flops 603979776 | bytes 2359296 | tf_op jit(solution)/shard_map/value_parts/pallas_call | solution.py:319
  107.5 8.0 %collective-permute-start.18 = (bf16[256,512]{1,0:T(8,128)(2,1)S(1)}, bf16[256,512]{1,0:T(8,128)(2,1)S(1)}, u32[]{:S(2)}, u32[]{:S(2)}) collective-permute-start(bf16[256,512]{1,0:T(8,128)(2,1)S(1)} %get-tuple-element.35), channel_id=1, source_target_pairs={{0,96},{1,25},{2,98},{3,27},{4,100},{5,29},{6,102},{7,31},{8,104},... | collective-permute-start | bytes 786440 | tf_op jit(solution)/shard_map/ppermute | solution.py:59
  115.5 0.7 collective-permute-start.20
  116.2 6.3 %collective-permute-done.18.refs_1_ = bf16[256,512]{1,0:T(8,128)(2,1)S(1)} collective-permute-done((bf16[256,512]{1,0:T(8,128)(2,1)S(1)}, bf16[256,512]{1,0:T(8,128)(2,1)S(1)}, u32[]{:S(2)}, u32[]{:S(2)}) %collective-permute-start.18) | collective-permute-done | bytes 262176 | tf_op jit(solution)/shard_map/ppermute | solution.py:59
  122.4 4.3 %collective-permute-start.22 = (bf16[256,512]{1,0:T(8,128)(2,1)S(1)}, bf16[256,512]{1,0:T(8,128)(2,1)S(1)}, u32[]{:S(2)}, u32[]{:S(2)}) collective-permute-start(bf16[256,512]{1,0:T(8,128)(2,1)S(1)} %collective-permute-done.18.refs_1_), channel_id=1, source_target_pairs={{0,1},{1,0},{2,3},{3,2},{4,5},{5,4},{6,7},{7,6},{8,9},{9,8},{10,11... | collective-permute-start | bytes 786440 | tf_op jit(solution)/shard_map/ppermute | solution.py:59
  126.7 1.7 %collective-permute-start.23 = (bf16[256,512]{1,0:T(8,128)(2,1)S(1)}, bf16[256,512]{1,0:T(8,128)(2,1)S(1)}, u32[]{:S(2)}, u32[]{:S(2)}) collective-permute-start(bf16[256,512]{1,0:T(8,128)(2,1)S(1)} %collective-permute-done.19.refs_2_), channel_id=1, source_target_pairs={{0,1},{1,0},{2,3},{3,2},{4,5},{5,4},{6,7},{7,6},{8,9},{9,8},{10,11... | collective-permute-start | bytes 786440 | tf_op jit(solution)/shard_map/ppermute | solution.py:59
  128.4 2.7 %collective-permute-start.24 = (bf16[256,512]{1,0:T(8,128)(2,1)S(1)}, bf16[256,512]{1,0:T(8,128)(2,1)S(1)}, u32[]{:S(2)}, u32[]{:S(2)}) collective-permute-start(bf16[256,512]{1,0:T(8,128)(2,1)S(1)} %collective-permute-done.20.refs_3_), channel_id=1, source_target_pairs={{0,1},{1,0},{2,3},{3,2},{4,5},{5,4},{6,7},{7,6},{8,9},{9,8},{10,11... | collective-permute-start | bytes 786440 | tf_op jit(solution)/shard_map/ppermute | solution.py:59
  131.1 0.0 collective-permute-start.21
  131.1 0.1 copy.14.flag_ref
  131.3 1.2 collective-permute-done.21.refs_4_
  132.5 2.0 %joined.1 = f32[256,1024]{1,0:T(8,128)} custom-call(s32[3]{0:T(128)S(1)} %pad_add_fusion.refs_0_.place_ref, s32[256,1]{1,0:T(8,128)S(1)} %copy.14.flag_ref, f32[256,256]{1,0:T(8,128)S(1)} %get-tuple-element.34.refs_0_, bf16[256,512]{1,0:T(8,128)(2,1)S(1)} %collective-permute-done.18.refs_1_, bf16[256,512]{1,0:T(8,128)(2,1)S(1)} %collective-permute-done.19.refs_2_, ...), custom_call_target="tpu_custom_call" | custom-call | tf_op jit(solution)/shard_map/joined/pallas_call | solution.py:352
  (17 shorter events, 0.2 us)
Async XLA Ops:
  5.3 12.6 %collective-permute-start.2 = (bf16[1408,256]{1,0:T(8,128)(2,1)S(1)}, bf16[1408,256]{1,0:T(8,128)(2,1)S(1)}, u32[]{:S(2)}, u32[]{:S(2)}) collective-permute-start(bf16[1408,256]{1,0:T(8,128)(2,1)S(1)} %get-tuple-element.23.refs_0_.refs_6_), channel_id=1, source_target_pairs={{0,32},{1,9},{2,34},{3,11},{4,36},{5,13},{6,38},{7,15},{8,40},{9,1... | collective-permute-start | bytes 2162696 | tf_op jit(solution)/shard_map/ppermute | solution.py:59
  7.5 10.4 %collective-permute-start.1 = (bf16[1408,256]{1,0:T(8,128)(2,1)S(1)}, bf16[1408,256]{1,0:T(8,128)(2,1)S(1)}, u32[]{:S(2)}, u32[]{:S(2)}) collective-permute-start(bf16[1408,256]{1,0:T(8,128)(2,1)S(1)} %get-tuple-element.24.refs_1_.refs_7_), channel_id=1, source_target_pairs={{0,96},{1,25},{2,98},{3,27},{4,100},{5,29},{6,102},{7,31},{8,104},... | collective-permute-start | bytes 2162696 | tf_op jit(solution)/shard_map/ppermute | solution.py:59
  9.0 18.0 %collective-permute-start = (bf16[1664,256]{1,0:T(8,128)(2,1)S(1)}, bf16[1664,256]{1,0:T(8,128)(2,1)S(1)}, u32[]{:S(2)}, u32[]{:S(2)}) collective-permute-start(bf16[1664,256]{1,0:T(8,128)(2,1)S(1)} %get-tuple-element.25), channel_id=1, source_target_pairs={{0,96},{1,25},{2,98},{3,27},{4,100},{5,29},{6,102},{7,31},{8,104},... | collective-permute-start | bytes 2555912 | tf_op jit(solution)/shard_map/ppermute | solution.py:59
  10.4 16.7 %collective-permute-start.3 = (bf16[1664,256]{1,0:T(8,128)(2,1)S(1)}, bf16[1664,256]{1,0:T(8,128)(2,1)S(1)}, u32[]{:S(2)}, u32[]{:S(2)}) collective-permute-start(bf16[1664,256]{1,0:T(8,128)(2,1)S(1)} %get-tuple-element.26), channel_id=1, source_target_pairs={{0,32},{1,9},{2,34},{3,11},{4,36},{5,13},{6,38},{7,15},{8,40},{9,1... | collective-permute-start | bytes 2555912 | tf_op jit(solution)/shard_map/ppermute | solution.py:59
  17.9 16.9 %collective-permute-start.4 = (bf16[1408,256]{1,0:T(8,128)(2,1)S(1)}, bf16[1408,256]{1,0:T(8,128)(2,1)S(1)}, u32[]{:S(2)}, u32[]{:S(2)}) collective-permute-start(bf16[1408,256]{1,0:T(8,128)(2,1)S(1)} %collective-permute-done.2.refs_4_), channel_id=1, source_target_pairs={{0,32},{1,9},{2,34},{3,11},{4,36},{5,13},{6,38},{7,15},{8,40},{9,1... | collective-permute-start | bytes 2162696 | tf_op jit(solution)/shard_map/ppermute | solution.py:59
  17.9 16.8 %collective-permute-start.5 = (bf16[1408,256]{1,0:T(8,128)(2,1)S(1)}, bf16[1408,256]{1,0:T(8,128)(2,1)S(1)}, u32[]{:S(2)}, u32[]{:S(2)}) collective-permute-start(bf16[1408,256]{1,0:T(8,128)(2,1)S(1)} %collective-permute-done.1.refs_3_), channel_id=1, source_target_pairs={{0,96},{1,25},{2,98},{3,27},{4,100},{5,29},{6,102},{7,31},{8,104},... | collective-permute-start | bytes 2162696 | tf_op jit(solution)/shard_map/ppermute | solution.py:59
  36.3 7.4 %collective-permute-start.9 = (bf16[64,2304]{1,0:T(8,128)(2,1)S(1)}, bf16[64,2304]{1,0:T(8,128)(2,1)S(1)}, u32[]{:S(2)}, u32[]{:S(2)}) collective-permute-start(bf16[64,2304]{1,0:T(8,128)(2,1)S(1)} %get-tuple-element.32), channel_id=1, source_target_pairs={{0,24},{1,97},{2,26},{3,99},{4,28},{5,101},{6,30},{7,103},{8,0},{9... | collective-permute-start | bytes 884744 | tf_op jit(solution)/shard_map/ppermute | solution.py:59
  38.9 7.1 %collective-permute-start.6 = (bf16[64,2304]{1,0:T(8,128)(2,1)S(1)}, bf16[64,2304]{1,0:T(8,128)(2,1)S(1)}, u32[]{:S(2)}, u32[]{:S(2)}) collective-permute-start(bf16[64,2304]{1,0:T(8,128)(2,1)S(1)} %get-tuple-element.29), channel_id=1, source_target_pairs={{0,8},{1,33},{2,10},{3,35},{4,12},{5,37},{6,14},{7,39},{8,16},{9,4... | collective-permute-start | bytes 884744 | tf_op jit(solution)/shard_map/ppermute | solution.py:59
  40.8 8.3 %collective-permute-start.11 = (bf16[64,2304]{1,0:T(8,128)(2,1)S(1)}, bf16[64,2304]{1,0:T(8,128)(2,1)S(1)}, u32[]{:S(2)}, u32[]{:S(2)}) collective-permute-start(bf16[64,2304]{1,0:T(8,128)(2,1)S(1)} %get-tuple-element.33), channel_id=1, source_target_pairs={{0,8},{1,33},{2,10},{3,35},{4,12},{5,37},{6,14},{7,39},{8,16},{9,4... | collective-permute-start | bytes 884744 | tf_op jit(solution)/shard_map/ppermute | solution.py:59
  41.1 8.0 %collective-permute-start.8 = (bf16[64,2304]{1,0:T(8,128)(2,1)S(1)}, bf16[64,2304]{1,0:T(8,128)(2,1)S(1)}, u32[]{:S(2)}, u32[]{:S(2)}) collective-permute-start(bf16[64,2304]{1,0:T(8,128)(2,1)S(1)} %get-tuple-element.30), channel_id=1, source_target_pairs={{0,24},{1,97},{2,26},{3,99},{4,28},{5,101},{6,30},{7,103},{8,0},{9... | collective-permute-start | bytes 884744 | tf_op jit(solution)/shard_map/ppermute | solution.py:59
  43.7 6.8 %collective-permute-start.10 = (bf16[64,2304]{1,0:T(8,128)(2,1)S(1)}, bf16[64,2304]{1,0:T(8,128)(2,1)S(1)}, u32[]{:S(2)}, u32[]{:S(2)}) collective-permute-start(bf16[64,2304]{1,0:T(8,128)(2,1)S(1)} %add_convert_fusion.1), channel_id=1, source_target_pairs={{0,24},{1,97},{2,26},{3,99},{4,28},{5,101},{6,30},{7,103},{8,0},{9... | collective-permute-start | bytes 884744 | tf_op jit(solution)/shard_map/ppermute | solution.py:59
  46.0 6.9 %collective-permute-start.7 = (bf16[64,2304]{1,0:T(8,128)(2,1)S(1)}, bf16[64,2304]{1,0:T(8,128)(2,1)S(1)}, u32[]{:S(2)}, u32[]{:S(2)}) collective-permute-start(bf16[64,2304]{1,0:T(8,128)(2,1)S(1)} %add_convert_fusion.3), channel_id=1, source_target_pairs={{0,8},{1,33},{2,10},{3,35},{4,12},{5,37},{6,14},{7,39},{8,16},{9,4... | collective-permute-start | bytes 884744 | tf_op jit(solution)/shard_map/ppermute | solution.py:59
  53.1 21.3 %copy-start = (f32[16,2304]{1,0:T(8,128)S(1)}, f32[16,2304]{1,0:T(8,128)}, u32[]{:S(2)}) copy-start(f32[16,2304]{1,0:T(8,128)} %param.17) | copy-start | bytes 442372
  53.1 21.3 %copy-start.1 = (f32[16,2304]{1,0:T(8,128)S(1)}, f32[16,2304]{1,0:T(8,128)}, u32[]{:S(2)}) copy-start(f32[16,2304]{1,0:T(8,128)} %param.14) | copy-start | bytes 442372
  53.1 21.3 %copy-start.2 = (f32[16,2304]{1,0:T(8,128)S(1)}, f32[16,2304]{1,0:T(8,128)}, u32[]{:S(2)}) copy-start(f32[16,2304]{1,0:T(8,128)} %param.15) | copy-start | bytes 442372
  53.2 21.3 %copy-start.3 = (f32[16,2304]{1,0:T(8,128)S(1)}, f32[16,2304]{1,0:T(8,128)}, u32[]{:S(2)}) copy-start(f32[16,2304]{1,0:T(8,128)} %param.16) | copy-start | bytes 442372
  91.7 6.9 %collective-permute-start.14 = (bf16[64,2304]{1,0:T(8,128)(2,1)S(1)}, bf16[64,2304]{1,0:T(8,128)(2,1)S(1)}, u32[]{:S(2)}, u32[]{:S(2)}) collective-permute-start(bf16[64,2304]{1,0:T(8,128)(2,1)S(1)} %bitcast.11), channel_id=1, source_target_pairs={{0,8},{1,33},{2,10},{3,35},{4,12},{5,37},{6,14},{7,39},{8,16},{9,4... | collective-permute-start | bytes 884744 | tf_op jit(solution)/shard_map/ppermute | solution.py:59
  91.8 6.8 %collective-permute-start.13 = (bf16[64,2304]{1,0:T(8,128)(2,1)S(1)}, bf16[64,2304]{1,0:T(8,128)(2,1)S(1)}, u32[]{:S(2)}, u32[]{:S(2)}) collective-permute-start(bf16[64,2304]{1,0:T(8,128)(2,1)S(1)} %bitcast.8), channel_id=1, source_target_pairs={{0,24},{1,97},{2,26},{3,99},{4,28},{5,101},{6,30},{7,103},{8,0},{9... | collective-permute-start | bytes 884744 | tf_op jit(solution)/shard_map/ppermute | solution.py:59
  94.5 8.7 %collective-permute-start.12 = (bf16[64,2304]{1,0:T(8,128)(2,1)S(1)}, bf16[64,2304]{1,0:T(8,128)(2,1)S(1)}, u32[]{:S(2)}, u32[]{:S(2)}) collective-permute-start(bf16[64,2304]{1,0:T(8,128)(2,1)S(1)} %bitcast.12), channel_id=1, source_target_pairs={{0,24},{1,97},{2,26},{3,99},{4,28},{5,101},{6,30},{7,103},{8,0},{9... | collective-permute-start | bytes 884744 | tf_op jit(solution)/shard_map/ppermute | solution.py:59
  94.5 8.7 %collective-permute-start.15 = (bf16[64,2304]{1,0:T(8,128)(2,1)S(1)}, bf16[64,2304]{1,0:T(8,128)(2,1)S(1)}, u32[]{:S(2)}, u32[]{:S(2)}) collective-permute-start(bf16[64,2304]{1,0:T(8,128)(2,1)S(1)} %bitcast.9), channel_id=1, source_target_pairs={{0,8},{1,33},{2,10},{3,35},{4,12},{5,37},{6,14},{7,39},{8,16},{9,4... | collective-permute-start | bytes 884744 | tf_op jit(solution)/shard_map/ppermute | solution.py:59
  98.6 6.8 %collective-permute-start.16 = (bf16[64,2304]{1,0:T(8,128)(2,1)S(1)}, bf16[64,2304]{1,0:T(8,128)(2,1)S(1)}, u32[]{:S(2)}, u32[]{:S(2)}) collective-permute-start(bf16[64,2304]{1,0:T(8,128)(2,1)S(1)} %collective-permute-done.14.refs_10_), channel_id=1, source_target_pairs={{0,8},{1,33},{2,10},{3,35},{4,12},{5,37},{6,14},{7,39},{8,16},{9,4... | collective-permute-start | bytes 884744 | tf_op jit(solution)/shard_map/ppermute | solution.py:59
  98.6 6.8 %collective-permute-start.17 = (bf16[64,2304]{1,0:T(8,128)(2,1)S(1)}, bf16[64,2304]{1,0:T(8,128)(2,1)S(1)}, u32[]{:S(2)}, u32[]{:S(2)}) collective-permute-start(bf16[64,2304]{1,0:T(8,128)(2,1)S(1)} %collective-permute-done.13.refs_9_), channel_id=1, source_target_pairs={{0,24},{1,97},{2,26},{3,99},{4,28},{5,101},{6,30},{7,103},{8,0},{9... | collective-permute-start | bytes 884744 | tf_op jit(solution)/shard_map/ppermute | solution.py:59
  105.2 26.0 %copy-start.4 = (s32[256]{0:T(256)S(1)}, s32[256]{0:T(256)}, u32[]{:S(2)}) copy-start(s32[256]{0:T(256)} %param.12) | copy-start | bytes 3076
  107.5 14.9 %collective-permute-start.18 = (bf16[256,512]{1,0:T(8,128)(2,1)S(1)}, bf16[256,512]{1,0:T(8,128)(2,1)S(1)}, u32[]{:S(2)}, u32[]{:S(2)}) collective-permute-start(bf16[256,512]{1,0:T(8,128)(2,1)S(1)} %get-tuple-element.35), channel_id=1, source_target_pairs={{0,96},{1,25},{2,98},{3,27},{4,100},{5,29},{6,102},{7,31},{8,104},... | collective-permute-start | bytes 786440 | tf_op jit(solution)/shard_map/ppermute | solution.py:59
  115.5 11.2 %collective-permute-start.19 = (bf16[256,512]{1,0:T(8,128)(2,1)S(1)}, bf16[256,512]{1,0:T(8,128)(2,1)S(1)}, u32[]{:S(2)}, u32[]{:S(2)}) collective-permute-start(bf16[256,512]{1,0:T(8,128)(2,1)S(1)} %get-tuple-element.36), channel_id=1, source_target_pairs={{0,64},{1,17},{2,66},{3,19},{4,68},{5,21},{6,70},{7,23},{8,72},{9,... | collective-permute-start | bytes 786440 | tf_op jit(solution)/shard_map/ppermute | solution.py:59
  115.5 12.9 %collective-permute-start.20 = (bf16[256,512]{1,0:T(8,128)(2,1)S(1)}, bf16[256,512]{1,0:T(8,128)(2,1)S(1)}, u32[]{:S(2)}, u32[]{:S(2)}) collective-permute-start(bf16[256,512]{1,0:T(8,128)(2,1)S(1)} %get-tuple-element.37), channel_id=1, source_target_pairs={{0,32},{1,9},{2,34},{3,11},{4,36},{5,13},{6,38},{7,15},{8,40},{9,1... | collective-permute-start | bytes 786440 | tf_op jit(solution)/shard_map/ppermute | solution.py:59
  122.4 10.0 %collective-permute-start.22 = (bf16[256,512]{1,0:T(8,128)(2,1)S(1)}, bf16[256,512]{1,0:T(8,128)(2,1)S(1)}, u32[]{:S(2)}, u32[]{:S(2)}) collective-permute-start(bf16[256,512]{1,0:T(8,128)(2,1)S(1)} %collective-permute-done.18.refs_1_), channel_id=1, source_target_pairs={{0,1},{1,0},{2,3},{3,2},{4,5},{5,4},{6,7},{7,6},{8,9},{9,8},{10,11... | collective-permute-start | bytes 786440 | tf_op jit(solution)/shard_map/ppermute | solution.py:59
  126.7 5.8 %collective-permute-start.23 = (bf16[256,512]{1,0:T(8,128)(2,1)S(1)}, bf16[256,512]{1,0:T(8,128)(2,1)S(1)}, u32[]{:S(2)}, u32[]{:S(2)}) collective-permute-start(bf16[256,512]{1,0:T(8,128)(2,1)S(1)} %collective-permute-done.19.refs_2_), channel_id=1, source_target_pairs={{0,1},{1,0},{2,3},{3,2},{4,5},{5,4},{6,7},{7,6},{8,9},{9,8},{10,11... | collective-permute-start | bytes 786440 | tf_op jit(solution)/shard_map/ppermute | solution.py:59
  128.4 4.1 %collective-permute-start.24 = (bf16[256,512]{1,0:T(8,128)(2,1)S(1)}, bf16[256,512]{1,0:T(8,128)(2,1)S(1)}, u32[]{:S(2)}, u32[]{:S(2)}) collective-permute-start(bf16[256,512]{1,0:T(8,128)(2,1)S(1)} %collective-permute-done.20.refs_3_), channel_id=1, source_target_pairs={{0,1},{1,0},{2,3},{3,2},{4,5},{5,4},{6,7},{7,6},{8,9},{9,8},{10,11... | collective-permute-start | bytes 786440 | tf_op jit(solution)/shard_map/ppermute | solution.py:59
  131.1 1.3 %collective-permute-start.21 = (bf16[256,256]{1,0:T(8,128)(2,1)S(1)}, bf16[256,256]{1,0:T(8,128)(2,1)S(1)}, u32[]{:S(2)}, u32[]{:S(2)}) collective-permute-start(bf16[256,256]{1,0:T(8,128)(2,1)S(1)} %get-tuple-element.38), channel_id=1, source_target_pairs={{0,1},{1,0},{2,3},{3,2},{4,5},{5,4},{6,7},{7,6},{8,9},{9,8},{10,11... | collective-permute-start | bytes 393224 | tf_op jit(solution)/shard_map/ppermute | solution.py:59

commit v5 on v4

--- a/solution.py
+++ b/solution.py
@@ -328,12 +328,13 @@
 
 
 def join_kernel(place_ref, flag_ref, *refs):
-    mine, over, out_ref, held = refs[:4], refs[4:8], refs[8], refs[9]
+    mine, over, out_hbm, held, out_ref, sems = refs[:4], refs[4:8], *refs[8:]
     c, p, q = place_ref[0], place_ref[1], place_ref[2]
     for d in range(4):
-        held[c, (p + d) % 4] = mine[d][:, :256].astype(f32)
-        held[1 - c, (q + d) % 4] = over[d][:, -256:].astype(f32)
+        held[c, (p + d) % 4] = mine[d][:, :256].astype(bf16)
+        held[1 - c, (q + d) % 4] = over[d][:, -256:]
     flag = flag_ref[...].astype(f32)
+    copies = []
     for x in range(4):
         for j in range(2):
             near = held[0, x, :, j * 128 : (j + 1) * 128]
@@ -344,17 +345,26 @@
                 ],
                 axis=1,
             )
-            out_ref[:, x * 256 + j * 128 : x * 256 + (j + 1) * 128] = (near + far) * flag
+            both = near.astype(f32) + far.astype(f32)
+            out_ref[:, x * 256 + j * 128 : x * 256 + (j + 1) * 128] = both * flag
+        cut = (slice(None), pl.ds(x * 256, 256))
+        copies.append(pltpu.make_async_copy(out_ref.at[cut], out_hbm.at[cut], sems.at[x]))
+        copies[-1].start()
+    for copy in copies:
+        copy.wait()
 
 
 def joined(place, flag, mine, over):
-    vmem = pl.BlockSpec(memory_space=pltpu.VMEM)
     return pl.pallas_call(
         join_kernel,
-        in_specs=[pl.BlockSpec(memory_space=pltpu.SMEM)] + [vmem] * 9,
-        out_specs=vmem,
+        in_specs=scalars() + in_vmem(9),
+        out_specs=pl.BlockSpec(memory_space=pl.ANY),
         out_shape=jax.ShapeDtypeStruct((256, 1024), f32),
-        scratch_shapes=[pltpu.VMEM((2, 4, 256, 256), f32)],
+        scratch_shapes=[
+            pltpu.VMEM((2, 4, 256, 256), bf16),
+            pltpu.VMEM((256, 1024), f32),
+            pltpu.SemaphoreType.DMA((4,)),
+        ],
         compiler_params=params(),
         name="joined",
     )(place, flag.reshape(256, 1), *mine, *over)

time: 135 us -> 135 us (level)
  no operation moved by 1% of the time
where the time goes in v5:
time: 135 us; the launch traced here: 134 us
  starting transfers between devices  39.7 us (29%)
  blocking collectives  37.4 us (28%)
  waiting for transfers between devices  35.3 us (26%)
  Pallas kernels  18.6 us (14%)
  other arithmetic  2.1 us (2%)
    ppermute x25, starting transfers between devices, send(): return lax.ppermute(array, AXES, perm)  39.7 us
    ppermute x25, waiting for transfers between devices, send(): return lax.ppermute(array, AXES, perm)  35.3 us
    all_to_all x1, blocking collectives, body(): lax.all_to_all(ring_sum.reshape(8, 16, width), ('zl', 'zh'), 0, 0, tiled=...  21.2 us
    all_to_all x1, blocking collectives, body(): column = lax.all_to_all(copies, ('zl', 'zh'), 0, 0, tiled=True)  16.3 us
    pallas_call x1, Pallas kernels, shared(): pl.pallas_call(share_kernel, in_specs=scalars() + in_vmem(1) + [hbm] * 3,...  3.89 us
    pallas_call x2, Pallas kernels, values(): pl.pallas_call(functools.partial(values_kernel, groups), in_specs=scalars...  3.88 us
    pallas_call x2, Pallas kernels, grad_parts(): pl.pallas_call(functools.partial(far_kernel, starts), in_specs=in_vmem(3)...  3.45 us
    pallas_call x1, Pallas kernels, near_grad(): pl.pallas_call(near_kernel, in_specs=in_vmem(7), out_specs=in_vmem(1)[0],...  3.42 us
  transfers between devices with their start and end apart: 25, of which 11 were waited for; matrix products, arithmetic and copies ran while one was open for 0% of the time, Pallas kernels for 7%

profile of v5, /device:TPU:1, one launch (start us, length us, event | category | flops | bytes accessed | tf_op | source)
XLA Modules:
  0.0 134.4 jit_solution(14476754330602000972)
XLA Ops:
  0.6 0.7 compare_select_fusion
  1.3 0.1 pad_add_fusion.refs_0_.place_ref
  1.4 3.9 %shared.1 = (bf16[1408,256]{1,0:T(8,128)(2,1)S(1)}, bf16[1408,256]{1,0:T(8,128)(2,1)S(1)}, bf16[1664,256]{1,0:T(8,128)(2,1)S(1)}, bf16[1664,256]{1,0:T(8,128)(2,1)S(1)}, bf16[512,256]{1,0:T(8,128)(2,1)S(1)}) custom-call(s32[3]{0:T(128)S(1)} %pad_add_fusion.refs_0_.place_ref, s32[1,256]{1,0:T(1,128)S(1)} %bitcast.14, bf16[512,2304]{1,0:T(8,128)(2,1)} %refs_2_.1, ...), custom_call_target="tpu_custom_call" | custom-call | flops 905969664 | bytes 4718592 | tf_op jit(solution)/shard_map/shared/pallas_call | solution.py:155
  5.3 2.2 %collective-permute-start.2 = (bf16[1408,256]{1,0:T(8,128)(2,1)S(1)}, bf16[1408,256]{1,0:T(8,128)(2,1)S(1)}, u32[]{:S(2)}, u32[]{:S(2)}) collective-permute-start(bf16[1408,256]{1,0:T(8,128)(2,1)S(1)} %get-tuple-element.23.refs_0_.refs_6_), channel_id=1, source_target_pairs={{0,32},{1,9},{2,34},{3,11},{4,36},{5,13},{6,38},{7,15},{8,40},{9,1... | collective-permute-start | bytes 2162696 | tf_op jit(solution)/shard_map/ppermute | solution.py:59
  7.5 1.5 %collective-permute-start.1 = (bf16[1408,256]{1,0:T(8,128)(2,1)S(1)}, bf16[1408,256]{1,0:T(8,128)(2,1)S(1)}, u32[]{:S(2)}, u32[]{:S(2)}) collective-permute-start(bf16[1408,256]{1,0:T(8,128)(2,1)S(1)} %get-tuple-element.24.refs_1_.refs_7_), channel_id=1, source_target_pairs={{0,96},{1,25},{2,98},{3,27},{4,100},{5,29},{6,102},{7,31},{8,104},... | collective-permute-start | bytes 2162696 | tf_op jit(solution)/shard_map/ppermute | solution.py:59
  9.0 1.4 %collective-permute-start = (bf16[1664,256]{1,0:T(8,128)(2,1)S(1)}, bf16[1664,256]{1,0:T(8,128)(2,1)S(1)}, u32[]{:S(2)}, u32[]{:S(2)}) collective-permute-start(bf16[1664,256]{1,0:T(8,128)(2,1)S(1)} %get-tuple-element.25), channel_id=1, source_target_pairs={{0,96},{1,25},{2,98},{3,27},{4,100},{5,29},{6,102},{7,31},{8,104},... | collective-permute-start | bytes 2555912 | tf_op jit(solution)/shard_map/ppermute | solution.py:59
  10.4 0.1 collective-permute-start.3
  10.5 7.4 %collective-permute-done.2.refs_4_ = bf16[1408,256]{1,0:T(8,128)(2,1)S(1)} collective-permute-done((bf16[1408,256]{1,0:T(8,128)(2,1)S(1)}, bf16[1408,256]{1,0:T(8,128)(2,1)S(1)}, u32[]{:S(2)}, u32[]{:S(2)}) %collective-permute-start.2) | collective-permute-done | bytes 720928 | tf_op jit(solution)/shard_map/ppermute | solution.py:59
  17.9 0.0 collective-permute-start.4
  17.9 0.0 collective-permute-done.1.refs_3_
  17.9 2.7 %collective-permute-start.5 = (bf16[1408,256]{1,0:T(8,128)(2,1)S(1)}, bf16[1408,256]{1,0:T(8,128)(2,1)S(1)}, u32[]{:S(2)}, u32[]{:S(2)}) collective-permute-start(bf16[1408,256]{1,0:T(8,128)(2,1)S(1)} %collective-permute-done.1.refs_3_), channel_id=1, source_target_pairs={{0,96},{1,25},{2,98},{3,27},{4,100},{5,29},{6,102},{7,31},{8,104},... | collective-permute-start | bytes 2162696 | tf_op jit(solution)/shard_map/ppermute | solution.py:59
  20.7 6.4 %collective-permute-done.refs_2_ = bf16[1664,256]{1,0:T(8,128)(2,1)S(1)} collective-permute-done((bf16[1664,256]{1,0:T(8,128)(2,1)S(1)}, bf16[1664,256]{1,0:T(8,128)(2,1)S(1)}, u32[]{:S(2)}, u32[]{:S(2)}) %collective-permute-start) | collective-permute-done | bytes 852000 | tf_op jit(solution)/shard_map/ppermute | solution.py:59
  27.1 0.0 collective-permute-done.3.refs_5_
  27.1 3.4 %near_grad.1.near_ref = f32[512,2304]{1,0:T(8,128)S(1)} custom-call(bf16[512,256]{1,0:T(8,128)(2,1)S(1)} %get-tuple-element.22.own_ref, bf16[1408,256]{1,0:T(8,128)(2,1)S(1)} %get-tuple-element.23.refs_0_.refs_6_, bf16[1408,256]{1,0:T(8,128)(2,1)S(1)} %get-tuple-element.24.refs_1_.refs_7_, bf16[1664,256]{1,0:T(8,128)(2,1)S(1)} %collective-permute-done.refs_2_, ...), custom_call_target="tpu_custom_call" | custom-call | flops 1811939328 | bytes 9437184 | tf_op jit(solution)/shard_map/near_grad/pallas_call | solution.py:199
  30.5 4.3 %collective-permute-done.4.a_ref.refs_6_.refs_0_ = bf16[1408,256]{1,0:T(8,128)(2,1)S(1)} collective-permute-done((bf16[1408,256]{1,0:T(8,128)(2,1)S(1)}, bf16[1408,256]{1,0:T(8,128)(2,1)S(1)}, u32[]{:S(2)}, u32[]{:S(2)}) %collective-permute-start.4) | collective-permute-done | bytes 720928 | tf_op jit(solution)/shard_map/ppermute | solution.py:59
  34.8 0.0 collective-permute-done.5.b_ref.refs_7_.refs_1_
  34.8 1.5 %grad_parts.3 = (bf16[64,2304]{1,0:T(8,128)(2,1)S(1)}, bf16[64,2304]{1,0:T(8,128)(2,1)S(1)}) custom-call(f32[512,2304]{1,0:T(8,128)S(1)} %near_grad.1.near_ref, bf16[1408,256]{1,0:T(8,128)(2,1)S(1)} %collective-permute-done.4.a_ref.refs_6_.refs_0_, bf16[1408,256]{1,0:T(8,128)(2,1)S(1)} %collective-permute-done.5.b_ref.refs_7_.refs_1_), custom_call_target="tpu_custom_call" | custom-call | flops 150994944 | bytes 4718592 | tf_op jit(solution)/shard_map/grad_parts/pallas_call | solution.py:233
  36.3 2.6 %collective-permute-start.9 = (bf16[64,2304]{1,0:T(8,128)(2,1)S(1)}, bf16[64,2304]{1,0:T(8,128)(2,1)S(1)}, u32[]{:S(2)}, u32[]{:S(2)}) collective-permute-start(bf16[64,2304]{1,0:T(8,128)(2,1)S(1)} %get-tuple-element.32), channel_id=1, source_target_pairs={{0,24},{1,97},{2,26},{3,99},{4,28},{5,101},{6,30},{7,103},{8,0},{9... | collective-permute-start | bytes 884744 | tf_op jit(solution)/shard_map/ppermute | solution.py:59
  38.9 0.0 collective-permute-start.6
  38.9 1.9 %grad_parts.2 = (bf16[64,2304]{1,0:T(8,128)(2,1)S(1)}, bf16[64,2304]{1,0:T(8,128)(2,1)S(1)}, bf16[64,2304]{1,0:T(8,128)(2,1)S(1)}, bf16[64,2304]{1,0:T(8,128)(2,1)S(1)}, f32[128,2304]{1,0:T(8,128)S(1)}) custom-call(f32[512,2304]{1,0:T(8,128)S(1)} %near_grad.1.near_ref, bf16[1408,256]{1,0:T(8,128)(2,1)S(1)} %collective-permute-done.4.a_ref.refs_6_.refs_0_, ...), custom_call_target="tpu_custom_call" | custom-call | flops 377487360 | bytes 4718592 | tf_op jit(solution)/shard_map/grad_parts/pallas_call | solution.py:233
  40.8 0.3 collective-permute-start.11
  41.1 2.6 %collective-permute-start.8 = (bf16[64,2304]{1,0:T(8,128)(2,1)S(1)}, bf16[64,2304]{1,0:T(8,128)(2,1)S(1)}, u32[]{:S(2)}, u32[]{:S(2)}) collective-permute-start(bf16[64,2304]{1,0:T(8,128)(2,1)S(1)} %get-tuple-element.30), channel_id=1, source_target_pairs={{0,24},{1,97},{2,26},{3,99},{4,28},{5,101},{6,30},{7,103},{8,0},{9... | collective-permute-start | bytes 884744 | tf_op jit(solution)/shard_map/ppermute | solution.py:59
  43.7 0.1 add_convert_fusion.1
  43.7 2.1 %collective-permute-start.10 = (bf16[64,2304]{1,0:T(8,128)(2,1)S(1)}, bf16[64,2304]{1,0:T(8,128)(2,1)S(1)}, u32[]{:S(2)}, u32[]{:S(2)}) collective-permute-start(bf16[64,2304]{1,0:T(8,128)(2,1)S(1)} %add_convert_fusion.1), channel_id=1, source_target_pairs={{0,24},{1,97},{2,26},{3,99},{4,28},{5,101},{6,30},{7,103},{8,0},{9... | collective-permute-start | bytes 884744 | tf_op jit(solution)/shard_map/ppermute | solution.py:59
  45.8 0.1 collective-permute-done.6
  46.0 0.1 add_convert_fusion.3
  46.0 0.1 collective-permute-start.7
  46.1 3.0 %collective-permute-done.11 = bf16[64,2304]{1,0:T(8,128)(2,1)S(1)} collective-permute-done((bf16[64,2304]{1,0:T(8,128)(2,1)S(1)}, bf16[64,2304]{1,0:T(8,128)(2,1)S(1)}, u32[]{:S(2)}, u32[]{:S(2)}) %collective-permute-start.11) | collective-permute-done | bytes 294944 | tf_op jit(solution)/shard_map/ppermute | solution.py:59
  49.1 1.4 %collective-permute-done.10 = bf16[64,2304]{1,0:T(8,128)(2,1)S(1)} collective-permute-done((bf16[64,2304]{1,0:T(8,128)(2,1)S(1)}, bf16[64,2304]{1,0:T(8,128)(2,1)S(1)}, u32[]{:S(2)}, u32[]{:S(2)}) %collective-permute-start.10) | collective-permute-done | bytes 294944 | tf_op jit(solution)/shard_map/ppermute | solution.py:59
  50.5 2.4 %collective-permute-done.7 = bf16[64,2304]{1,0:T(8,128)(2,1)S(1)} collective-permute-done((bf16[64,2304]{1,0:T(8,128)(2,1)S(1)}, bf16[64,2304]{1,0:T(8,128)(2,1)S(1)}, u32[]{:S(2)}, u32[]{:S(2)}) %collective-permute-start.7) | collective-permute-done | bytes 294944 | tf_op jit(solution)/shard_map/ppermute | solution.py:59
  52.9 0.2 add_convert_fusion.2
  53.1 0.0 copy-start
  53.1 0.0 copy-start.1
  53.1 0.0 copy-start.2
  53.2 0.0 copy-start.3
  53.2 21.2 %all_to_all.10 = bf16[8,16,2304]{2,1,0:T(8,128)(2,1)S(1)} all-to-all(bf16[8,16,2304]{2,1,0:T(8,128)(2,1)S(1)} %bitcast.15), channel_id=1, replica_groups=mesh['zl'=2,'x'=4,'y'=4,'zh'=4,'c'=2] {'zl','zh'}, dimensions={0} | all-to-all | bytes 1179648 | tf_op jit(solution)/shard_map/all_to_all | solution.py:415
  74.3 0.1 convert_reduce_fusion
  74.5 0.9 subtract_convert_fusion
  75.4 16.3 %all_to_all.11 = bf16[8,16,2304]{2,1,0:T(8,128)(2,1)S(1)} all-to-all(bf16[8,16,2304]{2,1,0:T(8,128)(2,1)S(1)} %broadcast_in_dim.11), channel_id=1, replica_groups=mesh['zl'=2,'x'=4,'y'=4,'zh'=4,'c'=2] {'zl','zh'}, dimensions={0} | all-to-all | bytes 1179648 | tf_op jit(solution)/shard_map/all_to_all | solution.py:427
  91.7 0.1 collective-permute-start.14
  91.8 2.7 %collective-permute-start.13 = (bf16[64,2304]{1,0:T(8,128)(2,1)S(1)}, bf16[64,2304]{1,0:T(8,128)(2,1)S(1)}, u32[]{:S(2)}, u32[]{:S(2)}) collective-permute-start(bf16[64,2304]{1,0:T(8,128)(2,1)S(1)} %bitcast.8), channel_id=1, source_target_pairs={{0,24},{1,97},{2,26},{3,99},{4,28},{5,101},{6,30},{7,103},{8,0},{9... | collective-permute-start | bytes 884744 | tf_op jit(solution)/shard_map/ppermute | solution.py:59
  94.5 0.0 collective-permute-start.12
  94.5 1.4 %collective-permute-start.15 = (bf16[64,2304]{1,0:T(8,128)(2,1)S(1)}, bf16[64,2304]{1,0:T(8,128)(2,1)S(1)}, u32[]{:S(2)}, u32[]{:S(2)}) collective-permute-start(bf16[64,2304]{1,0:T(8,128)(2,1)S(1)} %bitcast.9), channel_id=1, source_target_pairs={{0,8},{1,33},{2,10},{3,35},{4,12},{5,37},{6,14},{7,39},{8,16},{9,4... | collective-permute-start | bytes 884744 | tf_op jit(solution)/shard_map/ppermute | solution.py:59
  95.9 2.6 %collective-permute-done.14.refs_10_ = bf16[64,2304]{1,0:T(8,128)(2,1)S(1)} collective-permute-done((bf16[64,2304]{1,0:T(8,128)(2,1)S(1)}, bf16[64,2304]{1,0:T(8,128)(2,1)S(1)}, u32[]{:S(2)}, u32[]{:S(2)}) %collective-permute-start.14) | collective-permute-done | bytes 294944 | tf_op jit(solution)/shard_map/ppermute | solution.py:59
  98.6 2.7 %collective-permute-start.17 = (bf16[64,2304]{1,0:T(8,128)(2,1)S(1)}, bf16[64,2304]{1,0:T(8,128)(2,1)S(1)}, u32[]{:S(2)}, u32[]{:S(2)}) collective-permute-start(bf16[64,2304]{1,0:T(8,128)(2,1)S(1)} %collective-permute-done.13.refs_9_), channel_id=1, source_target_pairs={{0,24},{1,97},{2,26},{3,99},{4,28},{5,101},{6,30},{7,103},{8,0},{9... | collective-permute-start | bytes 884744 | tf_op jit(solution)/shard_map/ppermute | solution.py:59
  101.2 1.9 %values.2.own_ref = f32[1024,128]{1,0:T(8,128)S(1)} custom-call(s32[3]{0:T(128)S(1)} %pad_add_fusion.refs_0_.place_ref, bf16[1408,256]{1,0:T(8,128)(2,1)S(1)} %get-tuple-element.23.refs_0_.refs_6_, bf16[1408,256]{1,0:T(8,128)(2,1)S(1)} %get-tuple-element.24.refs_1_.refs_7_, bf16[1664,256]{1,0:T(8,128)(2,1)S(1)} %collective-permute-done.refs_2_, ...), custom_call_target="tpu_custom_call" | custom-call | flops 603979776 | bytes 9437184 | tf_op jit(solution)/shard_map/values/pallas_call | solution.py:264
  103.2 0.0 collective-permute-done.12.refs_8_
  103.2 0.0 collective-permute-done.15.refs_11_
  103.2 2.0 %values.3.side_ref = f32[1024,256]{1,0:T(8,128)S(1)} custom-call(s32[3]{0:T(128)S(1)} %pad_add_fusion.refs_0_.place_ref, bf16[1408,256]{1,0:T(8,128)(2,1)S(1)} %get-tuple-element.23.refs_0_.refs_6_, bf16[1408,256]{1,0:T(8,128)(2,1)S(1)} %get-tuple-element.24.refs_1_.refs_7_, bf16[1664,256]{1,0:T(8,128)(2,1)S(1)} %collective-permute-done.refs_2_, ...), custom_call_target="tpu_custom_call" | custom-call | flops 1207959552 | bytes 9437184 | tf_op jit(solution)/shard_map/values/pallas_call | solution.py:264
  105.2 0.0 copy-start.4
  105.2 0.2 collective-permute-done.16.refs_8_
  105.4 2.2 %value_parts.1 = (bf16[256,512]{1,0:T(8,128)(2,1)S(1)}, bf16[256,512]{1,0:T(8,128)(2,1)S(1)}, bf16[256,512]{1,0:T(8,128)(2,1)S(1)}, f32[256,256]{1,0:T(8,128)S(1)}, bf16[256,256]{1,0:T(8,128)(2,1)S(1)}) custom-call(s32[3]{0:T(128)S(1)} %pad_add_fusion.refs_0_.place_ref, f32[1024,128]{1,0:T(8,128)S(1)} %values.2.own_ref, f32[1024,256]{1,0:T(8,128)S(1)} %values.3.side_ref, ...), custom_call_target="tpu_custom_call" | custom-call | flops 603979776 | bytes 2359296 | tf_op jit(solution)/shard_map/value_parts/pallas_call | solution.py:319
  107.5 8.0 %collective-permute-start.18 = (bf16[256,512]{1,0:T(8,128)(2,1)S(1)}, bf16[256,512]{1,0:T(8,128)(2,1)S(1)}, u32[]{:S(2)}, u32[]{:S(2)}) collective-permute-start(bf16[256,512]{1,0:T(8,128)(2,1)S(1)} %get-tuple-element.35), channel_id=1, source_target_pairs={{0,96},{1,25},{2,98},{3,27},{4,100},{5,29},{6,102},{7,31},{8,104},... | collective-permute-start | bytes 786440 | tf_op jit(solution)/shard_map/ppermute | solution.py:59
  115.5 0.0 collective-permute-start.19
  115.5 0.7 collective-permute-start.20
  116.2 6.3 %collective-permute-done.18.refs_1_ = bf16[256,512]{1,0:T(8,128)(2,1)S(1)} collective-permute-done((bf16[256,512]{1,0:T(8,128)(2,1)S(1)}, bf16[256,512]{1,0:T(8,128)(2,1)S(1)}, u32[]{:S(2)}, u32[]{:S(2)}) %collective-permute-start.18) | collective-permute-done | bytes 262176 | tf_op jit(solution)/shard_map/ppermute | solution.py:59
  122.4 4.3 %collective-permute-start.22 = (bf16[256,512]{1,0:T(8,128)(2,1)S(1)}, bf16[256,512]{1,0:T(8,128)(2,1)S(1)}, u32[]{:S(2)}, u32[]{:S(2)}) collective-permute-start(bf16[256,512]{1,0:T(8,128)(2,1)S(1)} %collective-permute-done.18.refs_1_), channel_id=1, source_target_pairs={{0,1},{1,0},{2,3},{3,2},{4,5},{5,4},{6,7},{7,6},{8,9},{9,8},{10,11... | collective-permute-start | bytes 786440 | tf_op jit(solution)/shard_map/ppermute | solution.py:59
  126.7 1.7 %collective-permute-start.23 = (bf16[256,512]{1,0:T(8,128)(2,1)S(1)}, bf16[256,512]{1,0:T(8,128)(2,1)S(1)}, u32[]{:S(2)}, u32[]{:S(2)}) collective-permute-start(bf16[256,512]{1,0:T(8,128)(2,1)S(1)} %collective-permute-done.19.refs_2_), channel_id=1, source_target_pairs={{0,1},{1,0},{2,3},{3,2},{4,5},{5,4},{6,7},{7,6},{8,9},{9,8},{10,11... | collective-permute-start | bytes 786440 | tf_op jit(solution)/shard_map/ppermute | solution.py:59
  128.4 0.0 collective-permute-done.20.refs_3_
  128.4 2.7 %collective-permute-start.24 = (bf16[256,512]{1,0:T(8,128)(2,1)S(1)}, bf16[256,512]{1,0:T(8,128)(2,1)S(1)}, u32[]{:S(2)}, u32[]{:S(2)}) collective-permute-start(bf16[256,512]{1,0:T(8,128)(2,1)S(1)} %collective-permute-done.20.refs_3_), channel_id=1, source_target_pairs={{0,1},{1,0},{2,3},{3,2},{4,5},{5,4},{6,7},{7,6},{8,9},{9,8},{10,11... | collective-permute-start | bytes 786440 | tf_op jit(solution)/shard_map/ppermute | solution.py:59
  131.1 0.0 collective-permute-start.21
  131.1 0.1 copy.14.flag_ref
  131.3 1.2 collective-permute-done.21.refs_4_
  132.5 1.8 %joined.1 = f32[256,1024]{1,0:T(8,128)} custom-call(s32[3]{0:T(128)S(1)} %pad_add_fusion.refs_0_.place_ref, s32[256,1]{1,0:T(8,128)S(1)} %copy.14.flag_ref, f32[256,256]{1,0:T(8,128)S(1)} %get-tuple-element.34.refs_0_, bf16[256,512]{1,0:T(8,128)(2,1)S(1)} %collective-permute-done.18.refs_1_, bf16[256,512]{1,0:T(8,128)(2,1)S(1)} %collective-permute-done.19.refs_2_, ...), custom_call_target="tpu_custom_call" | custom-call | tf_op jit(solution)/shard_map/joined/pallas_call | solution.py:358
  (17 shorter events, 0.2 us)
Async XLA Ops:
  5.3 12.6 %collective-permute-start.2 = (bf16[1408,256]{1,0:T(8,128)(2,1)S(1)}, bf16[1408,256]{1,0:T(8,128)(2,1)S(1)}, u32[]{:S(2)}, u32[]{:S(2)}) collective-permute-start(bf16[1408,256]{1,0:T(8,128)(2,1)S(1)} %get-tuple-element.23.refs_0_.refs_6_), channel_id=1, source_target_pairs={{0,32},{1,9},{2,34},{3,11},{4,36},{5,13},{6,38},{7,15},{8,40},{9,1... | collective-permute-start | bytes 2162696 | tf_op jit(solution)/shard_map/ppermute | solution.py:59
  7.5 10.4 %collective-permute-start.1 = (bf16[1408,256]{1,0:T(8,128)(2,1)S(1)}, bf16[1408,256]{1,0:T(8,128)(2,1)S(1)}, u32[]{:S(2)}, u32[]{:S(2)}) collective-permute-start(bf16[1408,256]{1,0:T(8,128)(2,1)S(1)} %get-tuple-element.24.refs_1_.refs_7_), channel_id=1, source_target_pairs={{0,96},{1,25},{2,98},{3,27},{4,100},{5,29},{6,102},{7,31},{8,104},... | collective-permute-start | bytes 2162696 | tf_op jit(solution)/shard_map/ppermute | solution.py:59
  9.0 18.0 %collective-permute-start = (bf16[1664,256]{1,0:T(8,128)(2,1)S(1)}, bf16[1664,256]{1,0:T(8,128)(2,1)S(1)}, u32[]{:S(2)}, u32[]{:S(2)}) collective-permute-start(bf16[1664,256]{1,0:T(8,128)(2,1)S(1)} %get-tuple-element.25), channel_id=1, source_target_pairs={{0,96},{1,25},{2,98},{3,27},{4,100},{5,29},{6,102},{7,31},{8,104},... | collective-permute-start | bytes 2555912 | tf_op jit(solution)/shard_map/ppermute | solution.py:59
  10.4 16.7 %collective-permute-start.3 = (bf16[1664,256]{1,0:T(8,128)(2,1)S(1)}, bf16[1664,256]{1,0:T(8,128)(2,1)S(1)}, u32[]{:S(2)}, u32[]{:S(2)}) collective-permute-start(bf16[1664,256]{1,0:T(8,128)(2,1)S(1)} %get-tuple-element.26), channel_id=1, source_target_pairs={{0,32},{1,9},{2,34},{3,11},{4,36},{5,13},{6,38},{7,15},{8,40},{9,1... | collective-permute-start | bytes 2555912 | tf_op jit(solution)/shard_map/ppermute | solution.py:59
  17.9 16.9 %collective-permute-start.4 = (bf16[1408,256]{1,0:T(8,128)(2,1)S(1)}, bf16[1408,256]{1,0:T(8,128)(2,1)S(1)}, u32[]{:S(2)}, u32[]{:S(2)}) collective-permute-start(bf16[1408,256]{1,0:T(8,128)(2,1)S(1)} %collective-permute-done.2.refs_4_), channel_id=1, source_target_pairs={{0,32},{1,9},{2,34},{3,11},{4,36},{5,13},{6,38},{7,15},{8,40},{9,1... | collective-permute-start | bytes 2162696 | tf_op jit(solution)/shard_map/ppermute | solution.py:59
  17.9 16.8 %collective-permute-start.5 = (bf16[1408,256]{1,0:T(8,128)(2,1)S(1)}, bf16[1408,256]{1,0:T(8,128)(2,1)S(1)}, u32[]{:S(2)}, u32[]{:S(2)}) collective-permute-start(bf16[1408,256]{1,0:T(8,128)(2,1)S(1)} %collective-permute-done.1.refs_3_), channel_id=1, source_target_pairs={{0,96},{1,25},{2,98},{3,27},{4,100},{5,29},{6,102},{7,31},{8,104},... | collective-permute-start | bytes 2162696 | tf_op jit(solution)/shard_map/ppermute | solution.py:59
  36.3 7.4 %collective-permute-start.9 = (bf16[64,2304]{1,0:T(8,128)(2,1)S(1)}, bf16[64,2304]{1,0:T(8,128)(2,1)S(1)}, u32[]{:S(2)}, u32[]{:S(2)}) collective-permute-start(bf16[64,2304]{1,0:T(8,128)(2,1)S(1)} %get-tuple-element.32), channel_id=1, source_target_pairs={{0,24},{1,97},{2,26},{3,99},{4,28},{5,101},{6,30},{7,103},{8,0},{9... | collective-permute-start | bytes 884744 | tf_op jit(solution)/shard_map/ppermute | solution.py:59
  38.9 7.1 %collective-permute-start.6 = (bf16[64,2304]{1,0:T(8,128)(2,1)S(1)}, bf16[64,2304]{1,0:T(8,128)(2,1)S(1)}, u32[]{:S(2)}, u32[]{:S(2)}) collective-permute-start(bf16[64,2304]{1,0:T(8,128)(2,1)S(1)} %get-tuple-element.29), channel_id=1, source_target_pairs={{0,8},{1,33},{2,10},{3,35},{4,12},{5,37},{6,14},{7,39},{8,16},{9,4... | collective-permute-start | bytes 884744 | tf_op jit(solution)/shard_map/ppermute | solution.py:59
  40.8 8.3 %collective-permute-start.11 = (bf16[64,2304]{1,0:T(8,128)(2,1)S(1)}, bf16[64,2304]{1,0:T(8,128)(2,1)S(1)}, u32[]{:S(2)}, u32[]{:S(2)}) collective-permute-start(bf16[64,2304]{1,0:T(8,128)(2,1)S(1)} %get-tuple-element.33), channel_id=1, source_target_pairs={{0,8},{1,33},{2,10},{3,35},{4,12},{5,37},{6,14},{7,39},{8,16},{9,4... | collective-permute-start | bytes 884744 | tf_op jit(solution)/shard_map/ppermute | solution.py:59
  41.1 8.0 %collective-permute-start.8 = (bf16[64,2304]{1,0:T(8,128)(2,1)S(1)}, bf16[64,2304]{1,0:T(8,128)(2,1)S(1)}, u32[]{:S(2)}, u32[]{:S(2)}) collective-permute-start(bf16[64,2304]{1,0:T(8,128)(2,1)S(1)} %get-tuple-element.30), channel_id=1, source_target_pairs={{0,24},{1,97},{2,26},{3,99},{4,28},{5,101},{6,30},{7,103},{8,0},{9... | collective-permute-start | bytes 884744 | tf_op jit(solution)/shard_map/ppermute | solution.py:59
  43.7 6.8 %collective-permute-start.10 = (bf16[64,2304]{1,0:T(8,128)(2,1)S(1)}, bf16[64,2304]{1,0:T(8,128)(2,1)S(1)}, u32[]{:S(2)}, u32[]{:S(2)}) collective-permute-start(bf16[64,2304]{1,0:T(8,128)(2,1)S(1)} %add_convert_fusion.1), channel_id=1, source_target_pairs={{0,24},{1,97},{2,26},{3,99},{4,28},{5,101},{6,30},{7,103},{8,0},{9... | collective-permute-start | bytes 884744 | tf_op jit(solution)/shard_map/ppermute | solution.py:59
  46.0 6.9 %collective-permute-start.7 = (bf16[64,2304]{1,0:T(8,128)(2,1)S(1)}, bf16[64,2304]{1,0:T(8,128)(2,1)S(1)}, u32[]{:S(2)}, u32[]{:S(2)}) collective-permute-start(bf16[64,2304]{1,0:T(8,128)(2,1)S(1)} %add_convert_fusion.3), channel_id=1, source_target_pairs={{0,8},{1,33},{2,10},{3,35},{4,12},{5,37},{6,14},{7,39},{8,16},{9,4... | collective-permute-start | bytes 884744 | tf_op jit(solution)/shard_map/ppermute | solution.py:59
  53.1 21.3 %copy-start = (f32[16,2304]{1,0:T(8,128)S(1)}, f32[16,2304]{1,0:T(8,128)}, u32[]{:S(2)}) copy-start(f32[16,2304]{1,0:T(8,128)} %param.17) | copy-start | bytes 442372
  53.1 21.3 %copy-start.1 = (f32[16,2304]{1,0:T(8,128)S(1)}, f32[16,2304]{1,0:T(8,128)}, u32[]{:S(2)}) copy-start(f32[16,2304]{1,0:T(8,128)} %param.14) | copy-start | bytes 442372
  53.1 21.3 %copy-start.2 = (f32[16,2304]{1,0:T(8,128)S(1)}, f32[16,2304]{1,0:T(8,128)}, u32[]{:S(2)}) copy-start(f32[16,2304]{1,0:T(8,128)} %param.15) | copy-start | bytes 442372
  53.2 21.3 %copy-start.3 = (f32[16,2304]{1,0:T(8,128)S(1)}, f32[16,2304]{1,0:T(8,128)}, u32[]{:S(2)}) copy-start(f32[16,2304]{1,0:T(8,128)} %param.16) | copy-start | bytes 442372
  91.7 6.9 %collective-permute-start.14 = (bf16[64,2304]{1,0:T(8,128)(2,1)S(1)}, bf16[64,2304]{1,0:T(8,128)(2,1)S(1)}, u32[]{:S(2)}, u32[]{:S(2)}) collective-permute-start(bf16[64,2304]{1,0:T(8,128)(2,1)S(1)} %bitcast.11), channel_id=1, source_target_pairs={{0,8},{1,33},{2,10},{3,35},{4,12},{5,37},{6,14},{7,39},{8,16},{9,4... | collective-permute-start | bytes 884744 | tf_op jit(solution)/shard_map/ppermute | solution.py:59
  91.8 6.8 %collective-permute-start.13 = (bf16[64,2304]{1,0:T(8,128)(2,1)S(1)}, bf16[64,2304]{1,0:T(8,128)(2,1)S(1)}, u32[]{:S(2)}, u32[]{:S(2)}) collective-permute-start(bf16[64,2304]{1,0:T(8,128)(2,1)S(1)} %bitcast.8), channel_id=1, source_target_pairs={{0,24},{1,97},{2,26},{3,99},{4,28},{5,101},{6,30},{7,103},{8,0},{9... | collective-permute-start | bytes 884744 | tf_op jit(solution)/shard_map/ppermute | solution.py:59
  94.5 8.7 %collective-permute-start.12 = (bf16[64,2304]{1,0:T(8,128)(2,1)S(1)}, bf16[64,2304]{1,0:T(8,128)(2,1)S(1)}, u32[]{:S(2)}, u32[]{:S(2)}) collective-permute-start(bf16[64,2304]{1,0:T(8,128)(2,1)S(1)} %bitcast.12), channel_id=1, source_target_pairs={{0,24},{1,97},{2,26},{3,99},{4,28},{5,101},{6,30},{7,103},{8,0},{9... | collective-permute-start | bytes 884744 | tf_op jit(solution)/shard_map/ppermute | solution.py:59
  94.5 8.7 %collective-permute-start.15 = (bf16[64,2304]{1,0:T(8,128)(2,1)S(1)}, bf16[64,2304]{1,0:T(8,128)(2,1)S(1)}, u32[]{:S(2)}, u32[]{:S(2)}) collective-permute-start(bf16[64,2304]{1,0:T(8,128)(2,1)S(1)} %bitcast.9), channel_id=1, source_target_pairs={{0,8},{1,33},{2,10},{3,35},{4,12},{5,37},{6,14},{7,39},{8,16},{9,4... | collective-permute-start | bytes 884744 | tf_op jit(solution)/shard_map/ppermute | solution.py:59
  98.6 6.8 %collective-permute-start.16 = (bf16[64,2304]{1,0:T(8,128)(2,1)S(1)}, bf16[64,2304]{1,0:T(8,128)(2,1)S(1)}, u32[]{:S(2)}, u32[]{:S(2)}) collective-permute-start(bf16[64,2304]{1,0:T(8,128)(2,1)S(1)} %collective-permute-done.14.refs_10_), channel_id=1, source_target_pairs={{0,8},{1,33},{2,10},{3,35},{4,12},{5,37},{6,14},{7,39},{8,16},{9,4... | collective-permute-start | bytes 884744 | tf_op jit(solution)/shard_map/ppermute | solution.py:59
  98.6 6.8 %collective-permute-start.17 = (bf16[64,2304]{1,0:T(8,128)(2,1)S(1)}, bf16[64,2304]{1,0:T(8,128)(2,1)S(1)}, u32[]{:S(2)}, u32[]{:S(2)}) collective-permute-start(bf16[64,2304]{1,0:T(8,128)(2,1)S(1)} %collective-permute-done.13.refs_9_), channel_id=1, source_target_pairs={{0,24},{1,97},{2,26},{3,99},{4,28},{5,101},{6,30},{7,103},{8,0},{9... | collective-permute-start | bytes 884744 | tf_op jit(solution)/shard_map/ppermute | solution.py:59
  105.2 26.0 %copy-start.4 = (s32[256]{0:T(256)S(1)}, s32[256]{0:T(256)}, u32[]{:S(2)}) copy-start(s32[256]{0:T(256)} %param.12) | copy-start | bytes 3076
  107.5 14.9 %collective-permute-start.18 = (bf16[256,512]{1,0:T(8,128)(2,1)S(1)}, bf16[256,512]{1,0:T(8,128)(2,1)S(1)}, u32[]{:S(2)}, u32[]{:S(2)}) collective-permute-start(bf16[256,512]{1,0:T(8,128)(2,1)S(1)} %get-tuple-element.35), channel_id=1, source_target_pairs={{0,96},{1,25},{2,98},{3,27},{4,100},{5,29},{6,102},{7,31},{8,104},... | collective-permute-start | bytes 786440 | tf_op jit(solution)/shard_map/ppermute | solution.py:59
  115.5 11.2 %collective-permute-start.19 = (bf16[256,512]{1,0:T(8,128)(2,1)S(1)}, bf16[256,512]{1,0:T(8,128)(2,1)S(1)}, u32[]{:S(2)}, u32[]{:S(2)}) collective-permute-start(bf16[256,512]{1,0:T(8,128)(2,1)S(1)} %get-tuple-element.36), channel_id=1, source_target_pairs={{0,64},{1,17},{2,66},{3,19},{4,68},{5,21},{6,70},{7,23},{8,72},{9,... | collective-permute-start | bytes 786440 | tf_op jit(solution)/shard_map/ppermute | solution.py:59
  115.5 12.9 %collective-permute-start.20 = (bf16[256,512]{1,0:T(8,128)(2,1)S(1)}, bf16[256,512]{1,0:T(8,128)(2,1)S(1)}, u32[]{:S(2)}, u32[]{:S(2)}) collective-permute-start(bf16[256,512]{1,0:T(8,128)(2,1)S(1)} %get-tuple-element.37), channel_id=1, source_target_pairs={{0,32},{1,9},{2,34},{3,11},{4,36},{5,13},{6,38},{7,15},{8,40},{9,1... | collective-permute-start | bytes 786440 | tf_op jit(solution)/shard_map/ppermute | solution.py:59
  122.4 10.0 %collective-permute-start.22 = (bf16[256,512]{1,0:T(8,128)(2,1)S(1)}, bf16[256,512]{1,0:T(8,128)(2,1)S(1)}, u32[]{:S(2)}, u32[]{:S(2)}) collective-permute-start(bf16[256,512]{1,0:T(8,128)(2,1)S(1)} %collective-permute-done.18.refs_1_), channel_id=1, source_target_pairs={{0,1},{1,0},{2,3},{3,2},{4,5},{5,4},{6,7},{7,6},{8,9},{9,8},{10,11... | collective-permute-start | bytes 786440 | tf_op jit(solution)/shard_map/ppermute | solution.py:59
  126.7 5.8 %collective-permute-start.23 = (bf16[256,512]{1,0:T(8,128)(2,1)S(1)}, bf16[256,512]{1,0:T(8,128)(2,1)S(1)}, u32[]{:S(2)}, u32[]{:S(2)}) collective-permute-start(bf16[256,512]{1,0:T(8,128)(2,1)S(1)} %collective-permute-done.19.refs_2_), channel_id=1, source_target_pairs={{0,1},{1,0},{2,3},{3,2},{4,5},{5,4},{6,7},{7,6},{8,9},{9,8},{10,11... | collective-permute-start | bytes 786440 | tf_op jit(solution)/shard_map/ppermute | solution.py:59
  128.4 4.1 %collective-permute-start.24 = (bf16[256,512]{1,0:T(8,128)(2,1)S(1)}, bf16[256,512]{1,0:T(8,128)(2,1)S(1)}, u32[]{:S(2)}, u32[]{:S(2)}) collective-permute-start(bf16[256,512]{1,0:T(8,128)(2,1)S(1)} %collective-permute-done.20.refs_3_), channel_id=1, source_target_pairs={{0,1},{1,0},{2,3},{3,2},{4,5},{5,4},{6,7},{7,6},{8,9},{9,8},{10,11... | collective-permute-start | bytes 786440 | tf_op jit(solution)/shard_map/ppermute | solution.py:59
  131.1 1.3 %collective-permute-start.21 = (bf16[256,256]{1,0:T(8,128)(2,1)S(1)}, bf16[256,256]{1,0:T(8,128)(2,1)S(1)}, u32[]{:S(2)}, u32[]{:S(2)}) collective-permute-start(bf16[256,256]{1,0:T(8,128)(2,1)S(1)} %get-tuple-element.38), channel_id=1, source_target_pairs={{0,1},{1,0},{2,3},{3,2},{4,5},{5,4},{6,7},{7,6},{8,9},{9,8},{10,11... | collective-permute-start | bytes 393224 | tf_op jit(solution)/shard_map/ppermute | solution.py:59

commit v6 on v5

--- a/solution.py
+++ b/solution.py
@@ -331,8 +331,8 @@
     mine, over, out_hbm, held, out_ref, sems = refs[:4], refs[4:8], *refs[8:]
     c, p, q = place_ref[0], place_ref[1], place_ref[2]
     for d in range(4):
-        held[c, (p + d) % 4] = mine[d][:, :256].astype(bf16)
-        held[1 - c, (q + d) % 4] = over[d][:, -256:]
+        held[c, (p + d) % 4] = mine[d][:, :256].astype(f32)
+        held[1 - c, (q + d) % 4] = over[d][:, -256:].astype(f32)
     flag = flag_ref[...].astype(f32)
     copies = []
     for x in range(4):
@@ -345,7 +345,7 @@
                 ],
                 axis=1,
             )
-            both = near.astype(f32) + far.astype(f32)
+            both = near + far
             out_ref[:, x * 256 + j * 128 : x * 256 + (j + 1) * 128] = both * flag
         cut = (slice(None), pl.ds(x * 256, 256))
         copies.append(pltpu.make_async_copy(out_ref.at[cut], out_hbm.at[cut], sems.at[x]))
@@ -361,7 +361,7 @@
         out_specs=pl.BlockSpec(memory_space=pl.ANY),
         out_shape=jax.ShapeDtypeStruct((256, 1024), f32),
         scratch_shapes=[
-            pltpu.VMEM((2, 4, 256, 256), bf16),
+            pltpu.VMEM((2, 4, 256, 256), f32),
             pltpu.VMEM((256, 1024), f32),
             pltpu.SemaphoreType.DMA((4,)),
         ],

time: 135 us -> 135 us (level)
  no operation moved by 1% of the time
where the time goes in v6:
time: 135 us; the launch traced here: 134 us
  starting transfers between devices  39.7 us (29%)
  blocking collectives  37.4 us (28%)
  waiting for transfers between devices  35.3 us (26%)
  Pallas kernels  18.7 us (14%)
  other arithmetic  2.1 us (2%)
    ppermute x25, starting transfers between devices, send(): return lax.ppermute(array, AXES, perm)  39.7 us
    ppermute x25, waiting for transfers between devices, send(): return lax.ppermute(array, AXES, perm)  35.3 us
    all_to_all x1, blocking collectives, body(): lax.all_to_all(ring_sum.reshape(8, 16, width), ('zl', 'zh'), 0, 0, tiled=...  21.2 us
    all_to_all x1, blocking collectives, body(): column = lax.all_to_all(copies, ('zl', 'zh'), 0, 0, tiled=True)  16.3 us
    pallas_call x1, Pallas kernels, shared(): pl.pallas_call(share_kernel, in_specs=scalars() + in_vmem(1) + [hbm] * 3,...  3.89 us
    pallas_call x2, Pallas kernels, values(): pl.pallas_call(functools.partial(values_kernel, groups), in_specs=scalars...  3.88 us
    pallas_call x2, Pallas kernels, grad_parts(): pl.pallas_call(functools.partial(far_kernel, starts), in_specs=in_vmem(3)...  3.45 us
    pallas_call x1, Pallas kernels, near_grad(): pl.pallas_call(near_kernel, in_specs=in_vmem(7), out_specs=in_vmem(1)[0],...  3.42 us
  transfers between devices with their start and end apart: 25, of which 11 were waited for; matrix products, arithmetic and copies ran while one was open for 0% of the time, Pallas kernels for 7%

profile of v6, /device:TPU:1, one launch (start us, length us, event | category | flops | bytes accessed | tf_op | source)
XLA Modules:
  0.0 134.5 jit_solution(11461495747796467215)
XLA Ops:
  0.6 0.7 compare_select_fusion
  1.3 0.1 pad_add_fusion.refs_0_.place_ref
  1.4 3.9 %shared.1 = (bf16[1408,256]{1,0:T(8,128)(2,1)S(1)}, bf16[1408,256]{1,0:T(8,128)(2,1)S(1)}, bf16[1664,256]{1,0:T(8,128)(2,1)S(1)}, bf16[1664,256]{1,0:T(8,128)(2,1)S(1)}, bf16[512,256]{1,0:T(8,128)(2,1)S(1)}) custom-call(s32[3]{0:T(128)S(1)} %pad_add_fusion.refs_0_.place_ref, s32[1,256]{1,0:T(1,128)S(1)} %bitcast.14, bf16[512,2304]{1,0:T(8,128)(2,1)} %refs_2_.1, ...), custom_call_target="tpu_custom_call" | custom-call | flops 905969664 | bytes 4718592 | tf_op jit(solution)/shard_map/shared/pallas_call | solution.py:155
  5.3 2.2 %collective-permute-start.2 = (bf16[1408,256]{1,0:T(8,128)(2,1)S(1)}, bf16[1408,256]{1,0:T(8,128)(2,1)S(1)}, u32[]{:S(2)}, u32[]{:S(2)}) collective-permute-start(bf16[1408,256]{1,0:T(8,128)(2,1)S(1)} %get-tuple-element.23.refs_0_.refs_6_), channel_id=1, source_target_pairs={{0,32},{1,9},{2,34},{3,11},{4,36},{5,13},{6,38},{7,15},{8,40},{9,1... | collective-permute-start | bytes 2162696 | tf_op jit(solution)/shard_map/ppermute | solution.py:59
  7.5 1.5 %collective-permute-start.1 = (bf16[1408,256]{1,0:T(8,128)(2,1)S(1)}, bf16[1408,256]{1,0:T(8,128)(2,1)S(1)}, u32[]{:S(2)}, u32[]{:S(2)}) collective-permute-start(bf16[1408,256]{1,0:T(8,128)(2,1)S(1)} %get-tuple-element.24.refs_1_.refs_7_), channel_id=1, source_target_pairs={{0,96},{1,25},{2,98},{3,27},{4,100},{5,29},{6,102},{7,31},{8,104},... | collective-permute-start | bytes 2162696 | tf_op jit(solution)/shard_map/ppermute | solution.py:59
  9.0 1.4 %collective-permute-start = (bf16[1664,256]{1,0:T(8,128)(2,1)S(1)}, bf16[1664,256]{1,0:T(8,128)(2,1)S(1)}, u32[]{:S(2)}, u32[]{:S(2)}) collective-permute-start(bf16[1664,256]{1,0:T(8,128)(2,1)S(1)} %get-tuple-element.25), channel_id=1, source_target_pairs={{0,96},{1,25},{2,98},{3,27},{4,100},{5,29},{6,102},{7,31},{8,104},... | collective-permute-start | bytes 2555912 | tf_op jit(solution)/shard_map/ppermute | solution.py:59
  10.4 0.1 collective-permute-start.3
  10.5 7.4 %collective-permute-done.2.refs_4_ = bf16[1408,256]{1,0:T(8,128)(2,1)S(1)} collective-permute-done((bf16[1408,256]{1,0:T(8,128)(2,1)S(1)}, bf16[1408,256]{1,0:T(8,128)(2,1)S(1)}, u32[]{:S(2)}, u32[]{:S(2)}) %collective-permute-start.2) | collective-permute-done | bytes 720928 | tf_op jit(solution)/shard_map/ppermute | solution.py:59
  17.9 0.0 collective-permute-start.4
  17.9 0.0 collective-permute-done.1.refs_3_
  17.9 2.7 %collective-permute-start.5 = (bf16[1408,256]{1,0:T(8,128)(2,1)S(1)}, bf16[1408,256]{1,0:T(8,128)(2,1)S(1)}, u32[]{:S(2)}, u32[]{:S(2)}) collective-permute-start(bf16[1408,256]{1,0:T(8,128)(2,1)S(1)} %collective-permute-done.1.refs_3_), channel_id=1, source_target_pairs={{0,96},{1,25},{2,98},{3,27},{4,100},{5,29},{6,102},{7,31},{8,104},... | collective-permute-start | bytes 2162696 | tf_op jit(solution)/shard_map/ppermute | solution.py:59
  20.7 6.4 %collective-permute-done.refs_2_ = bf16[1664,256]{1,0:T(8,128)(2,1)S(1)} collective-permute-done((bf16[1664,256]{1,0:T(8,128)(2,1)S(1)}, bf16[1664,256]{1,0:T(8,128)(2,1)S(1)}, u32[]{:S(2)}, u32[]{:S(2)}) %collective-permute-start) | collective-permute-done | bytes 852000 | tf_op jit(solution)/shard_map/ppermute | solution.py:59
  27.1 0.0 collective-permute-done.3.refs_5_
  27.1 3.4 %near_grad.1.near_ref = f32[512,2304]{1,0:T(8,128)S(1)} custom-call(bf16[512,256]{1,0:T(8,128)(2,1)S(1)} %get-tuple-element.22.own_ref, bf16[1408,256]{1,0:T(8,128)(2,1)S(1)} %get-tuple-element.23.refs_0_.refs_6_, bf16[1408,256]{1,0:T(8,128)(2,1)S(1)} %get-tuple-element.24.refs_1_.refs_7_, bf16[1664,256]{1,0:T(8,128)(2,1)S(1)} %collective-permute-done.refs_2_, ...), custom_call_target="tpu_custom_call" | custom-call | flops 1811939328 | bytes 9437184 | tf_op jit(solution)/shard_map/near_grad/pallas_call | solution.py:199
  30.5 4.3 %collective-permute-done.4.a_ref.refs_6_.refs_0_ = bf16[1408,256]{1,0:T(8,128)(2,1)S(1)} collective-permute-done((bf16[1408,256]{1,0:T(8,128)(2,1)S(1)}, bf16[1408,256]{1,0:T(8,128)(2,1)S(1)}, u32[]{:S(2)}, u32[]{:S(2)}) %collective-permute-start.4) | collective-permute-done | bytes 720928 | tf_op jit(solution)/shard_map/ppermute | solution.py:59
  34.8 0.0 collective-permute-done.5.b_ref.refs_7_.refs_1_
  34.8 1.5 %grad_parts.3 = (bf16[64,2304]{1,0:T(8,128)(2,1)S(1)}, bf16[64,2304]{1,0:T(8,128)(2,1)S(1)}) custom-call(f32[512,2304]{1,0:T(8,128)S(1)} %near_grad.1.near_ref, bf16[1408,256]{1,0:T(8,128)(2,1)S(1)} %collective-permute-done.4.a_ref.refs_6_.refs_0_, bf16[1408,256]{1,0:T(8,128)(2,1)S(1)} %collective-permute-done.5.b_ref.refs_7_.refs_1_), custom_call_target="tpu_custom_call" | custom-call | flops 150994944 | bytes 4718592 | tf_op jit(solution)/shard_map/grad_parts/pallas_call | solution.py:233
  36.3 2.6 %collective-permute-start.9 = (bf16[64,2304]{1,0:T(8,128)(2,1)S(1)}, bf16[64,2304]{1,0:T(8,128)(2,1)S(1)}, u32[]{:S(2)}, u32[]{:S(2)}) collective-permute-start(bf16[64,2304]{1,0:T(8,128)(2,1)S(1)} %get-tuple-element.32), channel_id=1, source_target_pairs={{0,24},{1,97},{2,26},{3,99},{4,28},{5,101},{6,30},{7,103},{8,0},{9... | collective-permute-start | bytes 884744 | tf_op jit(solution)/shard_map/ppermute | solution.py:59
  38.9 0.0 collective-permute-start.6
  38.9 1.9 %grad_parts.2 = (bf16[64,2304]{1,0:T(8,128)(2,1)S(1)}, bf16[64,2304]{1,0:T(8,128)(2,1)S(1)}, bf16[64,2304]{1,0:T(8,128)(2,1)S(1)}, bf16[64,2304]{1,0:T(8,128)(2,1)S(1)}, f32[128,2304]{1,0:T(8,128)S(1)}) custom-call(f32[512,2304]{1,0:T(8,128)S(1)} %near_grad.1.near_ref, bf16[1408,256]{1,0:T(8,128)(2,1)S(1)} %collective-permute-done.4.a_ref.refs_6_.refs_0_, ...), custom_call_target="tpu_custom_call" | custom-call | flops 377487360 | bytes 4718592 | tf_op jit(solution)/shard_map/grad_parts/pallas_call | solution.py:233
  40.8 0.3 collective-permute-start.11
  41.1 2.6 %collective-permute-start.8 = (bf16[64,2304]{1,0:T(8,128)(2,1)S(1)}, bf16[64,2304]{1,0:T(8,128)(2,1)S(1)}, u32[]{:S(2)}, u32[]{:S(2)}) collective-permute-start(bf16[64,2304]{1,0:T(8,128)(2,1)S(1)} %get-tuple-element.30), channel_id=1, source_target_pairs={{0,24},{1,97},{2,26},{3,99},{4,28},{5,101},{6,30},{7,103},{8,0},{9... | collective-permute-start | bytes 884744 | tf_op jit(solution)/shard_map/ppermute | solution.py:59
  43.7 0.1 add_convert_fusion.1
  43.7 2.1 %collective-permute-start.10 = (bf16[64,2304]{1,0:T(8,128)(2,1)S(1)}, bf16[64,2304]{1,0:T(8,128)(2,1)S(1)}, u32[]{:S(2)}, u32[]{:S(2)}) collective-permute-start(bf16[64,2304]{1,0:T(8,128)(2,1)S(1)} %add_convert_fusion.1), channel_id=1, source_target_pairs={{0,24},{1,97},{2,26},{3,99},{4,28},{5,101},{6,30},{7,103},{8,0},{9... | collective-permute-start | bytes 884744 | tf_op jit(solution)/shard_map/ppermute | solution.py:59
  45.8 0.1 collective-permute-done.6
  46.0 0.1 add_convert_fusion.3
  46.0 0.1 collective-permute-start.7
  46.1 3.0 %collective-permute-done.11 = bf16[64,2304]{1,0:T(8,128)(2,1)S(1)} collective-permute-done((bf16[64,2304]{1,0:T(8,128)(2,1)S(1)}, bf16[64,2304]{1,0:T(8,128)(2,1)S(1)}, u32[]{:S(2)}, u32[]{:S(2)}) %collective-permute-start.11) | collective-permute-done | bytes 294944 | tf_op jit(solution)/shard_map/ppermute | solution.py:59
  49.1 1.4 %collective-permute-done.10 = bf16[64,2304]{1,0:T(8,128)(2,1)S(1)} collective-permute-done((bf16[64,2304]{1,0:T(8,128)(2,1)S(1)}, bf16[64,2304]{1,0:T(8,128)(2,1)S(1)}, u32[]{:S(2)}, u32[]{:S(2)}) %collective-permute-start.10) | collective-permute-done | bytes 294944 | tf_op jit(solution)/shard_map/ppermute | solution.py:59
  50.5 2.4 %collective-permute-done.7 = bf16[64,2304]{1,0:T(8,128)(2,1)S(1)} collective-permute-done((bf16[64,2304]{1,0:T(8,128)(2,1)S(1)}, bf16[64,2304]{1,0:T(8,128)(2,1)S(1)}, u32[]{:S(2)}, u32[]{:S(2)}) %collective-permute-start.7) | collective-permute-done | bytes 294944 | tf_op jit(solution)/shard_map/ppermute | solution.py:59
  52.9 0.2 add_convert_fusion.2
  53.1 0.0 copy-start
  53.1 0.0 copy-start.1
  53.1 0.0 copy-start.2
  53.2 0.0 copy-start.3
  53.2 21.2 %all_to_all.10 = bf16[8,16,2304]{2,1,0:T(8,128)(2,1)S(1)} all-to-all(bf16[8,16,2304]{2,1,0:T(8,128)(2,1)S(1)} %bitcast.15), channel_id=1, replica_groups=mesh['zl'=2,'x'=4,'y'=4,'zh'=4,'c'=2] {'zl','zh'}, dimensions={0} | all-to-all | bytes 1179648 | tf_op jit(solution)/shard_map/all_to_all | solution.py:415
  74.3 0.1 convert_reduce_fusion
  74.5 0.9 subtract_convert_fusion
  75.4 16.3 %all_to_all.11 = bf16[8,16,2304]{2,1,0:T(8,128)(2,1)S(1)} all-to-all(bf16[8,16,2304]{2,1,0:T(8,128)(2,1)S(1)} %broadcast_in_dim.11), channel_id=1, replica_groups=mesh['zl'=2,'x'=4,'y'=4,'zh'=4,'c'=2] {'zl','zh'}, dimensions={0} | all-to-all | bytes 1179648 | tf_op jit(solution)/shard_map/all_to_all | solution.py:427
  91.7 0.1 collective-permute-start.14
  91.8 2.7 %collective-permute-start.13 = (bf16[64,2304]{1,0:T(8,128)(2,1)S(1)}, bf16[64,2304]{1,0:T(8,128)(2,1)S(1)}, u32[]{:S(2)}, u32[]{:S(2)}) collective-permute-start(bf16[64,2304]{1,0:T(8,128)(2,1)S(1)} %bitcast.8), channel_id=1, source_target_pairs={{0,24},{1,97},{2,26},{3,99},{4,28},{5,101},{6,30},{7,103},{8,0},{9... | collective-permute-start | bytes 884744 | tf_op jit(solution)/shard_map/ppermute | solution.py:59
  94.5 0.0 collective-permute-start.12
  94.5 1.4 %collective-permute-start.15 = (bf16[64,2304]{1,0:T(8,128)(2,1)S(1)}, bf16[64,2304]{1,0:T(8,128)(2,1)S(1)}, u32[]{:S(2)}, u32[]{:S(2)}) collective-permute-start(bf16[64,2304]{1,0:T(8,128)(2,1)S(1)} %bitcast.9), channel_id=1, source_target_pairs={{0,8},{1,33},{2,10},{3,35},{4,12},{5,37},{6,14},{7,39},{8,16},{9,4... | collective-permute-start | bytes 884744 | tf_op jit(solution)/shard_map/ppermute | solution.py:59
  95.9 2.6 %collective-permute-done.14.refs_10_ = bf16[64,2304]{1,0:T(8,128)(2,1)S(1)} collective-permute-done((bf16[64,2304]{1,0:T(8,128)(2,1)S(1)}, bf16[64,2304]{1,0:T(8,128)(2,1)S(1)}, u32[]{:S(2)}, u32[]{:S(2)}) %collective-permute-start.14) | collective-permute-done | bytes 294944 | tf_op jit(solution)/shard_map/ppermute | solution.py:59
  98.6 2.7 %collective-permute-start.17 = (bf16[64,2304]{1,0:T(8,128)(2,1)S(1)}, bf16[64,2304]{1,0:T(8,128)(2,1)S(1)}, u32[]{:S(2)}, u32[]{:S(2)}) collective-permute-start(bf16[64,2304]{1,0:T(8,128)(2,1)S(1)} %collective-permute-done.13.refs_9_), channel_id=1, source_target_pairs={{0,24},{1,97},{2,26},{3,99},{4,28},{5,101},{6,30},{7,103},{8,0},{9... | collective-permute-start | bytes 884744 | tf_op jit(solution)/shard_map/ppermute | solution.py:59
  101.2 1.9 %values.2.own_ref = f32[1024,128]{1,0:T(8,128)S(1)} custom-call(s32[3]{0:T(128)S(1)} %pad_add_fusion.refs_0_.place_ref, bf16[1408,256]{1,0:T(8,128)(2,1)S(1)} %get-tuple-element.23.refs_0_.refs_6_, bf16[1408,256]{1,0:T(8,128)(2,1)S(1)} %get-tuple-element.24.refs_1_.refs_7_, bf16[1664,256]{1,0:T(8,128)(2,1)S(1)} %collective-permute-done.refs_2_, ...), custom_call_target="tpu_custom_call" | custom-call | flops 603979776 | bytes 9437184 | tf_op jit(solution)/shard_map/values/pallas_call | solution.py:264
  103.2 0.0 collective-permute-done.12.refs_8_
  103.2 0.0 collective-permute-done.15.refs_11_
  103.2 2.0 %values.3.side_ref = f32[1024,256]{1,0:T(8,128)S(1)} custom-call(s32[3]{0:T(128)S(1)} %pad_add_fusion.refs_0_.place_ref, bf16[1408,256]{1,0:T(8,128)(2,1)S(1)} %get-tuple-element.23.refs_0_.refs_6_, bf16[1408,256]{1,0:T(8,128)(2,1)S(1)} %get-tuple-element.24.refs_1_.refs_7_, bf16[1664,256]{1,0:T(8,128)(2,1)S(1)} %collective-permute-done.refs_2_, ...), custom_call_target="tpu_custom_call" | custom-call | flops 1207959552 | bytes 9437184 | tf_op jit(solution)/shard_map/values/pallas_call | solution.py:264
  105.2 0.0 copy-start.4
  105.2 0.2 collective-permute-done.16.refs_8_
  105.4 2.2 %value_parts.1 = (bf16[256,512]{1,0:T(8,128)(2,1)S(1)}, bf16[256,512]{1,0:T(8,128)(2,1)S(1)}, bf16[256,512]{1,0:T(8,128)(2,1)S(1)}, f32[256,256]{1,0:T(8,128)S(1)}, bf16[256,256]{1,0:T(8,128)(2,1)S(1)}) custom-call(s32[3]{0:T(128)S(1)} %pad_add_fusion.refs_0_.place_ref, f32[1024,128]{1,0:T(8,128)S(1)} %values.2.own_ref, f32[1024,256]{1,0:T(8,128)S(1)} %values.3.side_ref, ...), custom_call_target="tpu_custom_call" | custom-call | flops 603979776 | bytes 2359296 | tf_op jit(solution)/shard_map/value_parts/pallas_call | solution.py:319
  107.5 8.0 %collective-permute-start.18 = (bf16[256,512]{1,0:T(8,128)(2,1)S(1)}, bf16[256,512]{1,0:T(8,128)(2,1)S(1)}, u32[]{:S(2)}, u32[]{:S(2)}) collective-permute-start(bf16[256,512]{1,0:T(8,128)(2,1)S(1)} %get-tuple-element.35), channel_id=1, source_target_pairs={{0,96},{1,25},{2,98},{3,27},{4,100},{5,29},{6,102},{7,31},{8,104},... | collective-permute-start | bytes 786440 | tf_op jit(solution)/shard_map/ppermute | solution.py:59
  115.5 0.0 collective-permute-start.19
  115.5 0.7 collective-permute-start.20
  116.2 6.3 %collective-permute-done.18.refs_1_ = bf16[256,512]{1,0:T(8,128)(2,1)S(1)} collective-permute-done((bf16[256,512]{1,0:T(8,128)(2,1)S(1)}, bf16[256,512]{1,0:T(8,128)(2,1)S(1)}, u32[]{:S(2)}, u32[]{:S(2)}) %collective-permute-start.18) | collective-permute-done | bytes 262176 | tf_op jit(solution)/shard_map/ppermute | solution.py:59
  122.4 4.3 %collective-permute-start.22 = (bf16[256,512]{1,0:T(8,128)(2,1)S(1)}, bf16[256,512]{1,0:T(8,128)(2,1)S(1)}, u32[]{:S(2)}, u32[]{:S(2)}) collective-permute-start(bf16[256,512]{1,0:T(8,128)(2,1)S(1)} %collective-permute-done.18.refs_1_), channel_id=1, source_target_pairs={{0,1},{1,0},{2,3},{3,2},{4,5},{5,4},{6,7},{7,6},{8,9},{9,8},{10,11... | collective-permute-start | bytes 786440 | tf_op jit(solution)/shard_map/ppermute | solution.py:59
  126.7 1.7 %collective-permute-start.23 = (bf16[256,512]{1,0:T(8,128)(2,1)S(1)}, bf16[256,512]{1,0:T(8,128)(2,1)S(1)}, u32[]{:S(2)}, u32[]{:S(2)}) collective-permute-start(bf16[256,512]{1,0:T(8,128)(2,1)S(1)} %collective-permute-done.19.refs_2_), channel_id=1, source_target_pairs={{0,1},{1,0},{2,3},{3,2},{4,5},{5,4},{6,7},{7,6},{8,9},{9,8},{10,11... | collective-permute-start | bytes 786440 | tf_op jit(solution)/shard_map/ppermute | solution.py:59
  128.4 0.0 collective-permute-done.20.refs_3_
  128.4 2.7 %collective-permute-start.24 = (bf16[256,512]{1,0:T(8,128)(2,1)S(1)}, bf16[256,512]{1,0:T(8,128)(2,1)S(1)}, u32[]{:S(2)}, u32[]{:S(2)}) collective-permute-start(bf16[256,512]{1,0:T(8,128)(2,1)S(1)} %collective-permute-done.20.refs_3_), channel_id=1, source_target_pairs={{0,1},{1,0},{2,3},{3,2},{4,5},{5,4},{6,7},{7,6},{8,9},{9,8},{10,11... | collective-permute-start | bytes 786440 | tf_op jit(solution)/shard_map/ppermute | solution.py:59
  131.1 0.0 collective-permute-start.21
  131.1 0.1 copy.14.flag_ref
  131.3 1.2 collective-permute-done.21.refs_4_
  132.5 1.9 %joined.1 = f32[256,1024]{1,0:T(8,128)} custom-call(s32[3]{0:T(128)S(1)} %pad_add_fusion.refs_0_.place_ref, s32[256,1]{1,0:T(8,128)S(1)} %copy.14.flag_ref, f32[256,256]{1,0:T(8,128)S(1)} %get-tuple-element.34.refs_0_, bf16[256,512]{1,0:T(8,128)(2,1)S(1)} %collective-permute-done.18.refs_1_, bf16[256,512]{1,0:T(8,128)(2,1)S(1)} %collective-permute-done.19.refs_2_, ...), custom_call_target="tpu_custom_call" | custom-call | tf_op jit(solution)/shard_map/joined/pallas_call | solution.py:358
  (17 shorter events, 0.2 us)
Async XLA Ops:
  5.3 12.6 %collective-permute-start.2 = (bf16[1408,256]{1,0:T(8,128)(2,1)S(1)}, bf16[1408,256]{1,0:T(8,128)(2,1)S(1)}, u32[]{:S(2)}, u32[]{:S(2)}) collective-permute-start(bf16[1408,256]{1,0:T(8,128)(2,1)S(1)} %get-tuple-element.23.refs_0_.refs_6_), channel_id=1, source_target_pairs={{0,32},{1,9},{2,34},{3,11},{4,36},{5,13},{6,38},{7,15},{8,40},{9,1... | collective-permute-start | bytes 2162696 | tf_op jit(solution)/shard_map/ppermute | solution.py:59
  7.5 10.4 %collective-permute-start.1 = (bf16[1408,256]{1,0:T(8,128)(2,1)S(1)}, bf16[1408,256]{1,0:T(8,128)(2,1)S(1)}, u32[]{:S(2)}, u32[]{:S(2)}) collective-permute-start(bf16[1408,256]{1,0:T(8,128)(2,1)S(1)} %get-tuple-element.24.refs_1_.refs_7_), channel_id=1, source_target_pairs={{0,96},{1,25},{2,98},{3,27},{4,100},{5,29},{6,102},{7,31},{8,104},... | collective-permute-start | bytes 2162696 | tf_op jit(solution)/shard_map/ppermute | solution.py:59
  9.0 18.0 %collective-permute-start = (bf16[1664,256]{1,0:T(8,128)(2,1)S(1)}, bf16[1664,256]{1,0:T(8,128)(2,1)S(1)}, u32[]{:S(2)}, u32[]{:S(2)}) collective-permute-start(bf16[1664,256]{1,0:T(8,128)(2,1)S(1)} %get-tuple-element.25), channel_id=1, source_target_pairs={{0,96},{1,25},{2,98},{3,27},{4,100},{5,29},{6,102},{7,31},{8,104},... | collective-permute-start | bytes 2555912 | tf_op jit(solution)/shard_map/ppermute | solution.py:59
  10.4 16.7 %collective-permute-start.3 = (bf16[1664,256]{1,0:T(8,128)(2,1)S(1)}, bf16[1664,256]{1,0:T(8,128)(2,1)S(1)}, u32[]{:S(2)}, u32[]{:S(2)}) collective-permute-start(bf16[1664,256]{1,0:T(8,128)(2,1)S(1)} %get-tuple-element.26), channel_id=1, source_target_pairs={{0,32},{1,9},{2,34},{3,11},{4,36},{5,13},{6,38},{7,15},{8,40},{9,1... | collective-permute-start | bytes 2555912 | tf_op jit(solution)/shard_map/ppermute | solution.py:59
  17.9 16.9 %collective-permute-start.4 = (bf16[1408,256]{1,0:T(8,128)(2,1)S(1)}, bf16[1408,256]{1,0:T(8,128)(2,1)S(1)}, u32[]{:S(2)}, u32[]{:S(2)}) collective-permute-start(bf16[1408,256]{1,0:T(8,128)(2,1)S(1)} %collective-permute-done.2.refs_4_), channel_id=1, source_target_pairs={{0,32},{1,9},{2,34},{3,11},{4,36},{5,13},{6,38},{7,15},{8,40},{9,1... | collective-permute-start | bytes 2162696 | tf_op jit(solution)/shard_map/ppermute | solution.py:59
  17.9 16.8 %collective-permute-start.5 = (bf16[1408,256]{1,0:T(8,128)(2,1)S(1)}, bf16[1408,256]{1,0:T(8,128)(2,1)S(1)}, u32[]{:S(2)}, u32[]{:S(2)}) collective-permute-start(bf16[1408,256]{1,0:T(8,128)(2,1)S(1)} %collective-permute-done.1.refs_3_), channel_id=1, source_target_pairs={{0,96},{1,25},{2,98},{3,27},{4,100},{5,29},{6,102},{7,31},{8,104},... | collective-permute-start | bytes 2162696 | tf_op jit(solution)/shard_map/ppermute | solution.py:59
  36.3 7.4 %collective-permute-start.9 = (bf16[64,2304]{1,0:T(8,128)(2,1)S(1)}, bf16[64,2304]{1,0:T(8,128)(2,1)S(1)}, u32[]{:S(2)}, u32[]{:S(2)}) collective-permute-start(bf16[64,2304]{1,0:T(8,128)(2,1)S(1)} %get-tuple-element.32), channel_id=1, source_target_pairs={{0,24},{1,97},{2,26},{3,99},{4,28},{5,101},{6,30},{7,103},{8,0},{9... | collective-permute-start | bytes 884744 | tf_op jit(solution)/shard_map/ppermute | solution.py:59
  38.9 7.1 %collective-permute-start.6 = (bf16[64,2304]{1,0:T(8,128)(2,1)S(1)}, bf16[64,2304]{1,0:T(8,128)(2,1)S(1)}, u32[]{:S(2)}, u32[]{:S(2)}) collective-permute-start(bf16[64,2304]{1,0:T(8,128)(2,1)S(1)} %get-tuple-element.29), channel_id=1, source_target_pairs={{0,8},{1,33},{2,10},{3,35},{4,12},{5,37},{6,14},{7,39},{8,16},{9,4... | collective-permute-start | bytes 884744 | tf_op jit(solution)/shard_map/ppermute | solution.py:59
  40.8 8.3 %collective-permute-start.11 = (bf16[64,2304]{1,0:T(8,128)(2,1)S(1)}, bf16[64,2304]{1,0:T(8,128)(2,1)S(1)}, u32[]{:S(2)}, u32[]{:S(2)}) collective-permute-start(bf16[64,2304]{1,0:T(8,128)(2,1)S(1)} %get-tuple-element.33), channel_id=1, source_target_pairs={{0,8},{1,33},{2,10},{3,35},{4,12},{5,37},{6,14},{7,39},{8,16},{9,4... | collective-permute-start | bytes 884744 | tf_op jit(solution)/shard_map/ppermute | solution.py:59
  41.1 8.0 %collective-permute-start.8 = (bf16[64,2304]{1,0:T(8,128)(2,1)S(1)}, bf16[64,2304]{1,0:T(8,128)(2,1)S(1)}, u32[]{:S(2)}, u32[]{:S(2)}) collective-permute-start(bf16[64,2304]{1,0:T(8,128)(2,1)S(1)} %get-tuple-element.30), channel_id=1, source_target_pairs={{0,24},{1,97},{2,26},{3,99},{4,28},{5,101},{6,30},{7,103},{8,0},{9... | collective-permute-start | bytes 884744 | tf_op jit(solution)/shard_map/ppermute | solution.py:59
  43.7 6.8 %collective-permute-start.10 = (bf16[64,2304]{1,0:T(8,128)(2,1)S(1)}, bf16[64,2304]{1,0:T(8,128)(2,1)S(1)}, u32[]{:S(2)}, u32[]{:S(2)}) collective-permute-start(bf16[64,2304]{1,0:T(8,128)(2,1)S(1)} %add_convert_fusion.1), channel_id=1, source_target_pairs={{0,24},{1,97},{2,26},{3,99},{4,28},{5,101},{6,30},{7,103},{8,0},{9... | collective-permute-start | bytes 884744 | tf_op jit(solution)/shard_map/ppermute | solution.py:59
  46.0 6.9 %collective-permute-start.7 = (bf16[64,2304]{1,0:T(8,128)(2,1)S(1)}, bf16[64,2304]{1,0:T(8,128)(2,1)S(1)}, u32[]{:S(2)}, u32[]{:S(2)}) collective-permute-start(bf16[64,2304]{1,0:T(8,128)(2,1)S(1)} %add_convert_fusion.3), channel_id=1, source_target_pairs={{0,8},{1,33},{2,10},{3,35},{4,12},{5,37},{6,14},{7,39},{8,16},{9,4... | collective-permute-start | bytes 884744 | tf_op jit(solution)/shard_map/ppermute | solution.py:59
  53.1 21.3 %copy-start = (f32[16,2304]{1,0:T(8,128)S(1)}, f32[16,2304]{1,0:T(8,128)}, u32[]{:S(2)}) copy-start(f32[16,2304]{1,0:T(8,128)} %param.17) | copy-start | bytes 442372
  53.1 21.3 %copy-start.1 = (f32[16,2304]{1,0:T(8,128)S(1)}, f32[16,2304]{1,0:T(8,128)}, u32[]{:S(2)}) copy-start(f32[16,2304]{1,0:T(8,128)} %param.14) | copy-start | bytes 442372
  53.1 21.3 %copy-start.2 = (f32[16,2304]{1,0:T(8,128)S(1)}, f32[16,2304]{1,0:T(8,128)}, u32[]{:S(2)}) copy-start(f32[16,2304]{1,0:T(8,128)} %param.15) | copy-start | bytes 442372
  53.2 21.3 %copy-start.3 = (f32[16,2304]{1,0:T(8,128)S(1)}, f32[16,2304]{1,0:T(8,128)}, u32[]{:S(2)}) copy-start(f32[16,2304]{1,0:T(8,128)} %param.16) | copy-start | bytes 442372
  91.7 6.9 %collective-permute-start.14 = (bf16[64,2304]{1,0:T(8,128)(2,1)S(1)}, bf16[64,2304]{1,0:T(8,128)(2,1)S(1)}, u32[]{:S(2)}, u32[]{:S(2)}) collective-permute-start(bf16[64,2304]{1,0:T(8,128)(2,1)S(1)} %bitcast.11), channel_id=1, source_target_pairs={{0,8},{1,33},{2,10},{3,35},{4,12},{5,37},{6,14},{7,39},{8,16},{9,4... | collective-permute-start | bytes 884744 | tf_op jit(solution)/shard_map/ppermute | solution.py:59
  91.8 6.8 %collective-permute-start.13 = (bf16[64,2304]{1,0:T(8,128)(2,1)S(1)}, bf16[64,2304]{1,0:T(8,128)(2,1)S(1)}, u32[]{:S(2)}, u32[]{:S(2)}) collective-permute-start(bf16[64,2304]{1,0:T(8,128)(2,1)S(1)} %bitcast.8), channel_id=1, source_target_pairs={{0,24},{1,97},{2,26},{3,99},{4,28},{5,101},{6,30},{7,103},{8,0},{9... | collective-permute-start | bytes 884744 | tf_op jit(solution)/shard_map/ppermute | solution.py:59
  94.5 8.7 %collective-permute-start.12 = (bf16[64,2304]{1,0:T(8,128)(2,1)S(1)}, bf16[64,2304]{1,0:T(8,128)(2,1)S(1)}, u32[]{:S(2)}, u32[]{:S(2)}) collective-permute-start(bf16[64,2304]{1,0:T(8,128)(2,1)S(1)} %bitcast.12), channel_id=1, source_target_pairs={{0,24},{1,97},{2,26},{3,99},{4,28},{5,101},{6,30},{7,103},{8,0},{9... | collective-permute-start | bytes 884744 | tf_op jit(solution)/shard_map/ppermute | solution.py:59
  94.5 8.7 %collective-permute-start.15 = (bf16[64,2304]{1,0:T(8,128)(2,1)S(1)}, bf16[64,2304]{1,0:T(8,128)(2,1)S(1)}, u32[]{:S(2)}, u32[]{:S(2)}) collective-permute-start(bf16[64,2304]{1,0:T(8,128)(2,1)S(1)} %bitcast.9), channel_id=1, source_target_pairs={{0,8},{1,33},{2,10},{3,35},{4,12},{5,37},{6,14},{7,39},{8,16},{9,4... | collective-permute-start | bytes 884744 | tf_op jit(solution)/shard_map/ppermute | solution.py:59
  98.6 6.8 %collective-permute-start.16 = (bf16[64,2304]{1,0:T(8,128)(2,1)S(1)}, bf16[64,2304]{1,0:T(8,128)(2,1)S(1)}, u32[]{:S(2)}, u32[]{:S(2)}) collective-permute-start(bf16[64,2304]{1,0:T(8,128)(2,1)S(1)} %collective-permute-done.14.refs_10_), channel_id=1, source_target_pairs={{0,8},{1,33},{2,10},{3,35},{4,12},{5,37},{6,14},{7,39},{8,16},{9,4... | collective-permute-start | bytes 884744 | tf_op jit(solution)/shard_map/ppermute | solution.py:59
  98.6 6.8 %collective-permute-start.17 = (bf16[64,2304]{1,0:T(8,128)(2,1)S(1)}, bf16[64,2304]{1,0:T(8,128)(2,1)S(1)}, u32[]{:S(2)}, u32[]{:S(2)}) collective-permute-start(bf16[64,2304]{1,0:T(8,128)(2,1)S(1)} %collective-permute-done.13.refs_9_), channel_id=1, source_target_pairs={{0,24},{1,97},{2,26},{3,99},{4,28},{5,101},{6,30},{7,103},{8,0},{9... | collective-permute-start | bytes 884744 | tf_op jit(solution)/shard_map/ppermute | solution.py:59
  105.2 26.0 %copy-start.4 = (s32[256]{0:T(256)S(1)}, s32[256]{0:T(256)}, u32[]{:S(2)}) copy-start(s32[256]{0:T(256)} %param.12) | copy-start | bytes 3076
  107.5 14.9 %collective-permute-start.18 = (bf16[256,512]{1,0:T(8,128)(2,1)S(1)}, bf16[256,512]{1,0:T(8,128)(2,1)S(1)}, u32[]{:S(2)}, u32[]{:S(2)}) collective-permute-start(bf16[256,512]{1,0:T(8,128)(2,1)S(1)} %get-tuple-element.35), channel_id=1, source_target_pairs={{0,96},{1,25},{2,98},{3,27},{4,100},{5,29},{6,102},{7,31},{8,104},... | collective-permute-start | bytes 786440 | tf_op jit(solution)/shard_map/ppermute | solution.py:59
  115.5 11.2 %collective-permute-start.19 = (bf16[256,512]{1,0:T(8,128)(2,1)S(1)}, bf16[256,512]{1,0:T(8,128)(2,1)S(1)}, u32[]{:S(2)}, u32[]{:S(2)}) collective-permute-start(bf16[256,512]{1,0:T(8,128)(2,1)S(1)} %get-tuple-element.36), channel_id=1, source_target_pairs={{0,64},{1,17},{2,66},{3,19},{4,68},{5,21},{6,70},{7,23},{8,72},{9,... | collective-permute-start | bytes 786440 | tf_op jit(solution)/shard_map/ppermute | solution.py:59
  115.5 12.9 %collective-permute-start.20 = (bf16[256,512]{1,0:T(8,128)(2,1)S(1)}, bf16[256,512]{1,0:T(8,128)(2,1)S(1)}, u32[]{:S(2)}, u32[]{:S(2)}) collective-permute-start(bf16[256,512]{1,0:T(8,128)(2,1)S(1)} %get-tuple-element.37), channel_id=1, source_target_pairs={{0,32},{1,9},{2,34},{3,11},{4,36},{5,13},{6,38},{7,15},{8,40},{9,1... | collective-permute-start | bytes 786440 | tf_op jit(solution)/shard_map/ppermute | solution.py:59
  122.4 10.0 %collective-permute-start.22 = (bf16[256,512]{1,0:T(8,128)(2,1)S(1)}, bf16[256,512]{1,0:T(8,128)(2,1)S(1)}, u32[]{:S(2)}, u32[]{:S(2)}) collective-permute-start(bf16[256,512]{1,0:T(8,128)(2,1)S(1)} %collective-permute-done.18.refs_1_), channel_id=1, source_target_pairs={{0,1},{1,0},{2,3},{3,2},{4,5},{5,4},{6,7},{7,6},{8,9},{9,8},{10,11... | collective-permute-start | bytes 786440 | tf_op jit(solution)/shard_map/ppermute | solution.py:59
  126.7 5.8 %collective-permute-start.23 = (bf16[256,512]{1,0:T(8,128)(2,1)S(1)}, bf16[256,512]{1,0:T(8,128)(2,1)S(1)}, u32[]{:S(2)}, u32[]{:S(2)}) collective-permute-start(bf16[256,512]{1,0:T(8,128)(2,1)S(1)} %collective-permute-done.19.refs_2_), channel_id=1, source_target_pairs={{0,1},{1,0},{2,3},{3,2},{4,5},{5,4},{6,7},{7,6},{8,9},{9,8},{10,11... | collective-permute-start | bytes 786440 | tf_op jit(solution)/shard_map/ppermute | solution.py:59
  128.4 4.1 %collective-permute-start.24 = (bf16[256,512]{1,0:T(8,128)(2,1)S(1)}, bf16[256,512]{1,0:T(8,128)(2,1)S(1)}, u32[]{:S(2)}, u32[]{:S(2)}) collective-permute-start(bf16[256,512]{1,0:T(8,128)(2,1)S(1)} %collective-permute-done.20.refs_3_), channel_id=1, source_target_pairs={{0,1},{1,0},{2,3},{3,2},{4,5},{5,4},{6,7},{7,6},{8,9},{9,8},{10,11... | collective-permute-start | bytes 786440 | tf_op jit(solution)/shard_map/ppermute | solution.py:59
  131.1 1.3 %collective-permute-start.21 = (bf16[256,256]{1,0:T(8,128)(2,1)S(1)}, bf16[256,256]{1,0:T(8,128)(2,1)S(1)}, u32[]{:S(2)}, u32[]{:S(2)}) collective-permute-start(bf16[256,256]{1,0:T(8,128)(2,1)S(1)} %get-tuple-element.38), channel_id=1, source_target_pairs={{0,1},{1,0},{2,3},{3,2},{4,5},{5,4},{6,7},{7,6},{8,9},{9,8},{10,11... | collective-permute-start | bytes 393224 | tf_op jit(solution)/shard_map/ppermute | solution.py:59
